TPU v7x, 128 devices: a whole 4x4x4 slice. The times are simulated.
128 devices in a mesh: dp: 16 (over x_hi, y, core), tensor: 8 (over x_lo, z).
Axes of the slice: x: 4 (x_hi: 2, x_lo: 2; x = x_hi * 2 + x_lo), y: 4, z: 4, core: 2. Of those that a mesh axis runs over, the one named last changes fastest.
Arguments:
- activations: bfloat16 [4096, 6144], P('dp'), may hold values from -22 to 22
- out_grads: bfloat16 [4096, 24576], P('dp', 'tensor'), may hold values from -22 to 22
- weight_grad: bfloat16 [6144, 24576], P('dp', 'tensor'), may hold values from -6 to 6
Outputs:
- preconditioned: bfloat16 [6144, 24576], P('dp', 'tensor')
All inputs are finite; a program needn't handle non-finite values.
Results may differ from a plain program's by a relative error of at most 0.035.
Values may be sent and summed in bfloat16 or wider, within the bound.
No kernel may reach another device: no remote copies, remote signals or barrier semaphores. Data moves between devices by JAX's collectives and lax.ppermute only.
A program may use at most 192 MiB of HBM per device.

v0:
```python
import jax
import jax.numpy as jnp
from jax import lax
from jax.sharding import PartitionSpec as P

D = 6144
BLK = 1536


def broadcast(block, axis, holder):
    block = jnp.where(lax.axis_index(axis) == holder, block, jnp.zeros_like(block))
    return lax.psum(block, axis)


def swapped(array, axis, distance):
    return lax.ppermute(array, axis, [(i, i ^ 1 << distance) for i in range(lax.axis_size(axis))])


def covar_block(data, start):
    piece = lax.dynamic_slice_in_dim(data, start, BLK, 1)
    return lax.dot_general(
        piece, piece, (((0,), (0,)), ((), ())), preferred_element_type=jnp.float32
    )


def damped_pair(covar):
    identity = jnp.eye(BLK, dtype=jnp.float32)
    mean_diag = jnp.trace(covar) / BLK + 1e-06
    damped = (covar + mean_diag * identity).astype(jnp.bfloat16)
    scale = 1.0 / (2.0 * mean_diag)
    first = (2.0 * scale * identity - scale * scale * damped.astype(jnp.float32)).astype(
        jnp.bfloat16
    )
    return (damped, first)


def newton_rows(damped, first, start, count):
    leading = lax.dynamic_slice_in_dim(first, start, count, 0)
    product = jnp.dot(leading, damped, preferred_element_type=jnp.float32).astype(jnp.bfloat16)
    second = jnp.dot(product, first, preferred_element_type=jnp.float32)
    return (2.0 * leading.astype(jnp.float32) - second).astype(jnp.bfloat16)


def on_device(activations, out_grads, weight_grad):
    dp_count = lax.axis_size("dp")
    dp_index = lax.axis_index("dp")
    tp_index = lax.axis_index("tensor")
    grad_rows, grad_cols = weight_grad.shape
    g_blocks = grad_cols // BLK
    tp_width = D // lax.axis_size("tensor")
    token_total = activations.shape[0] * dp_count
    a_block = tp_index * tp_width // BLK
    a_start = tp_index * tp_width % BLK
    g_partial = jnp.stack([covar_block(out_grads, job * BLK) for job in range(g_blocks)]).astype(
        jnp.bfloat16
    )
    a_partial = covar_block(activations, a_block * BLK).astype(jnp.bfloat16)
    g_total, a_total = (
        lax.psum(g_partial, "dp").astype(jnp.float32),
        lax.psum(a_partial, "dp").astype(jnp.float32),
    )
    g_total = g_total / token_total
    a_total = a_total / token_total
    jobs = g_blocks + 1
    row_offset = dp_index * grad_rows % tp_width
    inverses = []
    for job in range(g_blocks):
        owner = (tp_index * jobs + job) % dp_count
        block_cov = g_total[job]

        def solve_whole(block_cov=block_cov):
            damped, first = damped_pair(block_cov)
            return newton_rows(damped, first, 0, BLK)

        def skip_whole():
            return jnp.zeros((BLK, BLK), jnp.bfloat16)

        local_inverse = lax.cond(dp_index == owner, solve_whole, skip_whole)
        inverses.append(broadcast(local_inverse, "dp", owner))
    g_inverse = jnp.stack(inverses)
    a_damped, a_first = damped_pair(a_total)
    picked = newton_rows(a_damped, a_first, a_start + row_offset, grad_rows)
    tp_root = dp_index * grad_rows // tp_width
    own_rows = broadcast(picked, "tensor", tp_root)
    blocked = weight_grad.reshape(grad_rows, g_blocks, BLK)
    right = jnp.einsum("rgk,gkl->rgl", blocked, g_inverse, preferred_element_type=jnp.float32)
    collected = right.astype(jnp.bfloat16).reshape(grad_rows, grad_cols)
    for bit_level in range((BLK // grad_rows).bit_length() - 1):
        partner = swapped(collected, "dp", bit_level)
        high_bit = dp_index // (1 << bit_level) % 2
        collected = jnp.where(
            high_bit == 1,
            jnp.concatenate([partner, collected], 0),
            jnp.concatenate([collected, partner], 0),
        )
    return jnp.dot(own_rows, collected, preferred_element_type=jnp.float32).astype(jnp.bfloat16)


def solution(mesh):
    return jax.shard_map(
        on_device,
        mesh=mesh,
        in_specs=(P("dp", None), P("dp", "tensor"), P("dp", "tensor")),
        out_specs=P("dp", "tensor"),
        check_vma=False,
    )
```

profile of v0, /device:TPU:1, one launch (start us, length us, event | category | flops | bytes accessed | tf_op | source)
XLA Modules:
  0.0 581.2 jit_solution(12969710666932361149)
XLA Ops:
  6.5 0.0 copy-start
  6.5 0.0 all-reduce.7.cloned.1.call-start
  6.5 5.1 fusion.51
  11.6 5.2 fusion.52
  16.8 8.3 %pad_maximum_fusion = bf16[2,1536,1536]{2,1,0:T(8,128)(2,1)} fusion(bf16[1,1536,1536]{2,1,0:T(8,128)(2,1)} %fusion.52, bf16[1,1536,1536]{2,1,0:T(8,128)(2,1)} %fusion.51), kind=kLoop, calls=%fused_computation.45 | loop fusion | flops 4718592 | bytes 18874368 | tf_op jit(solution)/shard_map/stack | solution.py:54
  25.0 0.0 all-reduce.7.cloned.1.call-update
  25.1 0.0 all-reduce.9.cloned.1.call-start
  25.2 3.6 convolution_convert_fusion.4
  28.8 165.2 %all-reduce.7.cloned.1.call-done = bf16[2,1536,1536]{2,1,0:T(8,128)(2,1)} async-done(((bf16[2,1536,1536]{2,1,0:T(8,128)(2,1)}), bf16[2,1536,1536]{2,1,0:T(8,128)(2,1)}) %all-reduce.7.cloned.1.call-update) | async-done | bytes 9437200 | tf_op jit(solution)/shard_map/psum | solution.py:59
  194.0 12.9 %convert_multiply_fusion = f32[2,1536,1536]{2,1,0:T(8,128)} fusion(bf16[2,1536,1536]{2,1,0:T(8,128)(2,1)} %all-reduce.7.cloned.1.call-done), kind=kLoop, calls=%fused_computation.44 | loop fusion | flops 9437184 | bytes 28311552 | tf_op jit(solution)/shard_map/div | solution.py:62
  206.9 39.4 %conditional.3 = (bf16[1536,1536]{0,1:T(8,128)(2,1)}) conditional(s32[]{:T(128)} %convert_element_type.120, () %tuple.18, f32[2,1536,1536]{2,1,0:T(8,128)} %convert_multiply_fusion), branch_computations={%region_8.9_spmd, %region_9.11_spmd} | conditional | flops 14587527168 | bytes 61346900 | solution.py:78
  206.9 4.5 fusion.20
  212.1 27.5 %subtract_convert_fusion.4 = bf16[1536,1536]{1,0:T(8,128)(2,1)} fusion(f32[2,1536,1536]{2,1,0:T(8,128)} %param.3, f32[]{:T(128)S(6)} %add.56, f32[]{:T(128)S(6)} %mul.107, f32[]{:T(128)S(6)} %mul.104), kind=kOutput, calls=%fused_computation.26 | convolution fusion | flops 14580449280 | bytes 42472448 | tf_op jit(solution)/shard_map/cond/branch_1_fun/dot_general | solution.py:40
  239.6 6.7 %copy.10 = bf16[1536,1536]{0,1:T(8,128)(2,1)} copy(bf16[1536,1536]{1,0:T(8,128)(2,1)} %subtract_convert_fusion.4) | data formatting | bytes 9437184 | tf_op jit(solution)/shard_map/cond | solution.py:78
  246.3 2.6 conditional.2
  246.3 2.6 broadcast.70.clone
  248.9 6.6 %select_bitcast_fusion = (bf16[1,1536,1536]{1,2,0:T(8,128)(2,1)}, bf16[1,1536,1536]{1,2,0:T(8,128)(2,1)}) fusion(bf16[1536,1536]{0,1:T(8,128)(2,1)} %get-tuple-element.18, pred[]{:T(512)S(6)} %eq.78, bf16[1536,1536]{0,1:T(8,128)(2,1)} %get-tuple-element.17, pred[]{:T(512)S(6)} %eq.77), kind=kLoop, calls=%fused_computation.69 | loop fusion | flops 4718592 | bytes 18874370 | tf_op jit(solution)/shard_map/stack | solution.py:80
  255.5 0.0 all-reduce.9.cloned.1.call-update
  255.5 0.0 all-reduce.5.cloned.1.call-start
  255.5 181.3 %all-reduce.9.cloned.1.call-done = (bf16[1536,1536]{1,0:T(8,128)(2,1)}, bf16[1,1536,1536]{1,2,0:T(8,128)(2,1)}, bf16[1,1536,1536]{1,2,0:T(8,128)(2,1)}) async-done(((bf16[1536,1536]{1,0:T(8,128)(2,1)}, bf16[1,1536,1536]{1,2,0:T(8,128)(2,1)}, bf16[1,1536,1536]{1,2,0:T(8,128)(2,1)}), (bf16[1536,1536]{1,0:T(8,128)(2,1)}, bf16[1,1536,1536]{1,2,0:T(8,128)(2,1)}, ...) | async-done | bytes 14155792 | tf_op jit(solution)/shard_map/psum | solution.py:60
  436.9 8.3 %fusion.54 = bf16[2,1536,384]{2,1,0:T(8,128)(2,1)S(1)} fusion(bf16[1,1536,1536]{1,2,0:T(8,128)(2,1)} %get-tuple-element.20, bf16[1,1536,1536]{1,2,0:T(8,128)(2,1)} %get-tuple-element.21, bf16[48,2,8,1536]{3,2,1,0:T(8,128)(2,1)} %bitcast.65), kind=kOutput, calls=%fused_computation.72 | convolution fusion | flops 3629776896 | bytes 14155776 | tf_op jit(solution)/shard_map/rgk,gkl->rgl/dot_general | solution.py:86
  445.2 3.8 collective-permute-start
  449.0 4.3 collective-permute-done
  453.3 6.3 %maximum_select_fusion.2 = bf16[768,3072]{0,1:T(8,128)(2,1)} fusion(bf16[384,3072]{0,1:T(8,128)(2,1)S(1)} %bitcast.64, bf16[384,3072]{0,1:T(8,128)(2,1)} %collective-permute-done, pred[]{:T(512)S(6)} %eq.76), kind=kLoop, calls=%fused_computation.68 | loop fusion | flops 21233664 | bytes 9437185 | tf_op jit(solution)/shard_map/jit(_where)/select_n | solution.py:91
  459.6 0.0 collective-permute-start.1
  459.6 3.1 select_reduce_fusion
  463.4 6.0 %subtract_convert_fusion.8 = bf16[1536,1536]{1,0:T(8,128)(2,1)} fusion(f32[]{:T(128)S(6)} %mul.141, f32[]{:T(128)S(6)} %mul.138, f32[]{:T(128)S(6)} %add.72, bf16[1536,1536]{1,0:T(8,128)(2,1)} %get-tuple-element.19), kind=kLoop, calls=%fused_computation.57 | loop fusion | flops 25952256 | bytes 9437196 | tf_op jit(solution)/shard_map/convert_element_type | solution.py:31
  469.4 9.3 %fusion.58 = bf16[384,1536]{1,0:T(8,128)(2,1)} fusion(bf16[1536,1536]{1,0:T(8,128)(2,1)} %subtract_convert_fusion.8, bf16[1536,1536]{1,0:T(8,128)(2,1)} %get-tuple-element.19, f32[]{:T(128)S(6)} %add.72, s32[]{:T(128)S(6)} %select_n.100, pred[]{:T(512)S(6)} %eq.73), kind=kOutput, calls=%fused_computation.76 | convolution fusion | flops 3641573376 | bytes 12978176 | tf_op jit(solution)/shard_map/dot_general | solution.py:40
  478.8 0.0 all-reduce.5.cloned.1.call-update
  478.8 73.4 %all-reduce.5.cloned.1.call-done = bf16[384,1536]{1,0:T(8,128)(2,1)} async-done(((bf16[384,1536]{1,0:T(8,128)(2,1)}), bf16[384,1536]{1,0:T(8,128)(2,1)}) %all-reduce.5.cloned.1.call-update) | async-done | bytes 1179664 | tf_op jit(solution)/shard_map/psum | solution.py:12
  552.2 10.7 %collective-permute-done.1 = bf16[768,3072]{0,1:T(8,128)(2,1)} collective-permute-done((bf16[768,3072]{0,1:T(8,128)(2,1)}, bf16[768,3072]{0,1:T(8,128)(2,1)}, u32[]{:S(2)}, u32[]{:S(2)}) %collective-permute-start.1) | collective-permute-done | bytes 4718624 | tf_op jit(solution)/shard_map/ppermute | solution.py:16
  562.9 11.7 %fusion.53 = bf16[384,3072]{1,0:T(8,128)(2,1)} fusion(bf16[384,1536]{1,0:T(8,128)(2,1)} %all-reduce.5.cloned.1.call-done, bf16[768,3072]{0,1:T(8,128)(2,1)} %maximum_select_fusion.2, bf16[768,3072]{0,1:T(8,128)(2,1)} %collective-permute-done.1, pred[]{:T(512)S(6)} %eq.75), kind=kOutput, calls=%fused_computation.71 | convolution fusion | flops 3667525632 | bytes 12976129 | tf_op jit(solution)/shard_map/dot_general | solution.py:96
  (3 shorter events, 0.0 us)
Async XLA Ops:
  6.5 18.6 %copy-start = (bf16[256,6144]{1,0:T(8,128)(2,1)S(1)}, bf16[256,6144]{1,0:T(8,128)(2,1)}, u32[]{:S(2)}) copy-start(bf16[256,6144]{1,0:T(8,128)(2,1)} %param.7) | copy-start | bytes 9437188
  6.5 187.5 %all-reduce.7.cloned.1.call-start = ((), (), s32[]{:S(2)}) async-start(), calls=%async_computation.1 | async-start | bytes 18874368 | tf_op jit(solution)/shard_map/psum | solution.py:59
  25.1 411.8 %all-reduce.9.cloned.1.call-start = ((), (), s32[]{:S(2)}) async-start(), calls=%async_computation.2 | async-start | bytes 28311552 | tf_op jit(solution)/shard_map/psum | solution.py:60
  255.5 296.8 %all-reduce.5.cloned.1.call-start = ((), (), s32[]{:S(2)}) async-start(), calls=%async_computation | async-start | bytes 2359296 | tf_op jit(solution)/shard_map/psum | solution.py:12
  445.2 8.1 %collective-permute-start = (bf16[384,3072]{0,1:T(8,128)(2,1)S(1)}, bf16[384,3072]{0,1:T(8,128)(2,1)}, u32[]{:S(2)}, u32[]{:S(2)}) collective-permute-start(bf16[384,3072]{0,1:T(8,128)(2,1)S(1)} %bitcast.63), channel_id=1, source_target_pairs={{0,8},{8,0},{16,24},{24,16},{32,40},{40,32},{48,56},{56,48},{64,72... | collective-permute-start | bytes 7077896 | tf_op jit(solution)/shard_map/ppermute | solution.py:16
  459.6 103.3 %collective-permute-start.1 = (bf16[768,3072]{0,1:T(8,128)(2,1)}, bf16[768,3072]{0,1:T(8,128)(2,1)}, u32[]{:S(2)}, u32[]{:S(2)}) collective-permute-start(bf16[768,3072]{0,1:T(8,128)(2,1)} %maximum_select_fusion.2), channel_id=1, source_target_pairs={{0,16},{8,24},{16,0},{24,8},{32,48},{40,56},{48,32},{56,40},{64,80... | collective-permute-start | bytes 14155784 | tf_op jit(solution)/shard_map/ppermute | solution.py:16
  562.9 11.7 %copy-start.1 = (bf16[256,6144]{1,0:T(8,128)(2,1)S(1)}, bf16[256,6144]{1,0:T(8,128)(2,1)}, u32[]{:S(2)}) copy-start(bf16[256,6144]{1,0:T(8,128)(2,1)} %param.7) | copy-start | bytes 9437188
Sparse Core Ops, SparseCore 0:
  25.2 168.7 all-reduce.6
  255.6 181.2 all-reduce.8
  478.9 73.3 all-reduce.4
where the time goes:
time: 582 us; the launch traced here: 581 us
  waiting for transfers between devices  435 us (75%)
  matrix products  70.7 us (12%)
  other arithmetic  47.7 us (8%)
  between operations  13.9 us (2%)
  local copies, waits for them, and re-layouts  9.25 us (2%)
    psum x1, waiting for transfers between devices, on_device(): lax.psum(a_partial, 'dp').astype(jnp.float32)  181 us
    psum x1, waiting for transfers between devices, on_device(): lax.psum(g_partial, 'dp').astype(jnp.float32)  165 us
    psum x1, waiting for transfers between devices, broadcast(): return lax.psum(block, axis)  73.4 us
    dot_general x2, matrix products, newton_rows(): second = jnp.dot(product, first, preferred_element_type=jnp.float32)  36.8 us
    ppermute x2, waiting for transfers between devices, swapped(): lax.ppermute(array, axis, [(i, i ^ 1 << distance) for i in range(lax.axis...  15 us
    dot_general x3, matrix products, covar_block(): lax.dot_general(piece, piece, (((0,), (0,)), ((), ())), preferred_element...  13.8 us
    div x1, other arithmetic, on_device(): g_total = g_total / token_total  12.9 us
    dot_general x1, matrix products, on_device(): jnp.dot(own_rows, collected, preferred_element_type=jnp.float32)  11.7 us
  transfers between devices with their start and end apart: 5, of which 5 were waited for; matrix products, arithmetic and copies ran while one was open for 4% of the time, Pallas kernels for 0%

commit v1 on v0

v1 whole, which is shorter than its diff:
```python
import jax
import jax.numpy as jnp
from jax import lax
from jax.experimental import pallas as pl
from jax.experimental.pallas import tpu as pltpu
from jax.sharding import PartitionSpec as P

BLK = 1536
TOKENS = 4096
TILE = 128
SIDE = BLK // TILE
UPPER = [(i, j) for i in range(SIDE) for j in range(i, SIDE)]
SLOTS = 80
PIECE = 5
AXES = ("dp", "tensor")
VMEM = 56 * 1024 * 1024


def moves(target):
    pairs = []
    for dp in range(16):
        for tp in range(8):
            x_hi, y, core = dp // 8, dp // 2 % 4, dp % 2
            x_lo, z = tp // 4, tp % 4
            x_hi, y, core, x_lo, z = target(x_hi, y, core, x_lo, z)
            there = (x_hi * 8 + y * 2 + core) * 8 + x_lo * 4 + z % 4
            pairs.append((dp * 8 + tp, there))
    return pairs


CORE = moves(lambda h, y, c, l, z: (h, y, c ^ 1, l, z))
Y_NEAR = moves(lambda h, y, c, l, z: (h, y ^ 1, c, l, z))
Y_NEAR_CORE = moves(lambda h, y, c, l, z: (h, y ^ 1, c ^ 1, l, z))
Y_FAR = moves(lambda h, y, c, l, z: (h, y ^ 3, c, l, z))
X_HALF = moves(lambda h, y, c, l, z: (h ^ 1, y, c, l, z))
X_NEAR = moves(lambda h, y, c, l, z: (h, y, c, l ^ 1, z))
Z_UP = moves(lambda h, y, c, l, z: (h, y, c, l, z + 1))
Z_DOWN = moves(lambda h, y, c, l, z: (h, y, c, l, z + 3))
Z_HALF = moves(lambda h, y, c, l, z: (h, y, c, l, z + 2))


def send(array, pairs):
    return lax.ppermute(array, AXES, pairs)


def add(first, second):
    return (first.astype(jnp.float32) + second.astype(jnp.float32)).astype(jnp.bfloat16)


def place():
    dp, tp = lax.axis_index("dp"), lax.axis_index("tensor")
    return dp // 8, dp // 2 % 4, dp % 2, tp // 4, tp % 4


def slot_first(piece, code):
    rel = piece ^ code
    return rel ^ (rel >> 1 & 1)


def slot_second(piece, code):
    rel = piece ^ code
    low, mid, high = rel & 1, rel >> 1 & 1, rel >> 2
    return mid << 2 | (low ^ mid) << 1 | high


def slot_of(tile, code):
    piece, at = tile // PIECE, tile % PIECE
    if piece < 8:
        return slot_first(piece, code) * PIECE + at
    return (slot_second(piece - 8, code) + 8) * PIECE + at


def cov_g(own, got, first_send, second_send, first_keep, second_keep, tokens, packed, sems):
    x_hi, y, core, _, _ = place()
    half = own.shape[0]
    loads = [
        pltpu.make_async_copy(
            own.at[:, pl.ds(pl.multiple_of(core * BLK, BLK), BLK)], tokens.at[pl.ds(0, half)], sems.at[0]
        ),
        pltpu.make_async_copy(got, tokens.at[pl.ds(half, half)], sems.at[1]),
    ]
    for load in loads:
        load.start()
    for load in loads:
        load.wait()
    code = x_hi * 4 + y
    for row in range(SIDE // 2):
        start = row * 2 * TILE
        product = lax.dot_general(
            tokens[:, start : start + 2 * TILE],
            tokens[:, start:],
            (((0,), (0,)), ((), ())),
            preferred_element_type=jnp.float32,
        ).astype(jnp.bfloat16)
        for tile, (i, j) in enumerate(UPPER):
            if i // 2 == row:
                top, left = (i - 2 * row) * TILE, (j - 2 * row) * TILE
                packed[slot_of(tile, code)] = product[top : top + TILE, left : left + TILE]
    for tile in range(len(UPPER), SLOTS):
        packed[slot_of(tile, code)] = jnp.zeros((TILE, TILE), jnp.bfloat16)
    count = 4 * PIECE
    stores = [
        pltpu.make_async_copy(packed.at[pl.ds(at * count, count)], out, sems.at[2 + at])
        for at, out in ((1, first_send), (3, second_send), (0, first_keep), (2, second_keep))
    ]
    for store in stores:
        store.start()
    for store in stores:
        store.wait()


def cov_a(rows, cols, tokens, sent, kept):
    x_hi, y, core, x_lo, z = place()
    tp = x_lo * 4 + z
    own = x_hi * 2 + y // 2
    for out, side in ((sent, 1 - core), (kept, core)):
        for at in range(PIECE):
            tile = (tp * 2 + side) * PIECE + at
            i, j = rows[tile], cols[tile]
            for rel in range(4):
                start = (own ^ rel) * SIDE
                lhs = tokens[:, pl.ds(pl.multiple_of((start + i) * TILE, TILE), TILE)]
                rhs = tokens[:, pl.ds(pl.multiple_of((start + j) * TILE, TILE), TILE)]
                out[rel * PIECE + at] = lax.dot_general(
                    lhs, rhs, (((0,), (0,)), ((), ())), preferred_element_type=jnp.float32
                ).astype(jnp.bfloat16)


def spread(packed, slots, full):
    row = lax.broadcasted_iota(jnp.int32, (TILE, TILE), 0)
    col = lax.broadcasted_iota(jnp.int32, (TILE, TILE), 1)
    diagonal = jnp.zeros((TILE, TILE), jnp.float32)
    for tile, (i, j) in enumerate(UPPER):
        value = packed[slots(tile)]
        full[i * TILE : (i + 1) * TILE, j * TILE : (j + 1) * TILE] = value
        if i == j:
            diagonal = diagonal + value.astype(jnp.float32)
        else:
            full[j * TILE : (j + 1) * TILE, i * TILE : (i + 1) * TILE] = value.T
    return jnp.sum(jnp.where(row == col, diagonal, 0.0))


def scales(trace):
    mean = trace / (TOKENS * BLK) + 1e-06
    return 1.0 / (TOKENS * mean), 1.0 / (2.0 * mean)


STEP = 256


def newton_chain(full, ratio, scale, start_of, second, third, finish):
    @pl.loop(0, BLK // STEP)
    def _(at):
        cols = pl.ds(pl.multiple_of(at * STEP, STEP), STEP)
        second[:, cols] = start_of(cols).astype(jnp.bfloat16)

    @pl.loop(0, BLK // STEP)
    def _(at):
        cols = pl.ds(pl.multiple_of(at * STEP, STEP), STEP)
        turned = jnp.dot(second[...], full[:, cols], preferred_element_type=jnp.float32)
        third[:, cols] = (second[:, cols].astype(jnp.float32) + ratio * turned).astype(jnp.bfloat16)

    @pl.loop(0, BLK // STEP)
    def _(at):
        cols = pl.ds(pl.multiple_of(at * STEP, STEP), STEP)
        turned = jnp.dot(third[...], full[:, cols], preferred_element_type=jnp.float32)
        value = 2.0 * second[:, cols].astype(jnp.float32) - 0.75 * third[:, cols].astype(jnp.float32)
        finish(cols, (scale * (value + 0.25 * ratio * turned)).astype(jnp.bfloat16))


def left_kernel(*refs):
    parts, (w_own, w_core, w_near, w_cross, out) = refs[:8], refs[8:13]
    packed, full, second, third, inverse, weights, sems = refs[13:]
    x_hi, y, core, x_lo, z = place()
    low = y % 2
    count = 2 * PIECE
    copies = [
        pltpu.make_async_copy(part, packed.at[pl.ds(at * count, count)], sems.at[at])
        for at, part in enumerate(parts)
    ]
    rows = w_core.shape[0]
    own = w_own.at[:, pl.ds(pl.multiple_of(core * BLK, BLK), BLK)]
    for at, (source, side, lane) in enumerate(
        ((own, low, core), (w_core, low, 1 - core), (w_near, 1 - low, core), (w_cross, 1 - low, 1 - core))
    ):
        there = pl.multiple_of((side * 2 + lane) * rows, rows)
        copies.append(pltpu.make_async_copy(source, weights.at[pl.ds(there, rows)], sems.at[8 + at]))
    for copy in copies:
        copy.start()
    for copy in copies[:8]:
        copy.wait()

    def slots(tile):
        piece, at = tile // PIECE, tile % PIECE
        side, z_at, x_at = piece % 2, piece // 2 % 4, piece // 8
        return (((side ^ core) * 4 + (z_at - z + 4) % 4) * 2 + (x_at ^ x_lo)) * PIECE + at

    ratio, scale = scales(spread(packed, slots, full))
    first_row = pl.multiple_of(low * 2 * rows, 2 * rows)
    mine = pl.ds(first_row, 2 * rows)

    def start_of(cols):
        row = lax.broadcasted_iota(jnp.int32, (2 * rows, STEP), 0) + first_row
        col = lax.broadcasted_iota(jnp.int32, (2 * rows, STEP), 1) + cols.start
        return jnp.where(row == col, 1.5, 0.0) - 0.5 * ratio * full[mine, cols].astype(jnp.float32)

    def finish(cols, value):
        inverse[:, cols] = value

    newton_chain(full, ratio, scale, start_of, second, third, finish)
    for copy in copies[8:]:
        copy.wait()

    @pl.loop(0, BLK // STEP)
    def _(at):
        cols = pl.ds(pl.multiple_of(at * STEP, STEP), STEP)
        out[:, cols] = jnp.dot(
            inverse[...], weights[:, cols], preferred_element_type=jnp.float32
        ).astype(jnp.bfloat16)


def right_kernel(first_own, first_got, second_own, second_got, left, out, packed, full, second, third, sems):
    x_hi, y, _, _, _ = place()
    code = x_hi * 4 + y
    count = 4 * PIECE
    copies = [
        pltpu.make_async_copy(part, packed.at[pl.ds(at * count, count)], sems.at[at])
        for at, part in enumerate((first_own, first_got, second_own, second_got))
    ]
    for copy in copies:
        copy.start()
    for copy in copies:
        copy.wait()
    ratio, scale = scales(spread(packed, lambda tile: slot_of(tile, code), full))

    def start_of(cols):
        turned = jnp.dot(left[...], full[:, cols], preferred_element_type=jnp.float32)
        return 1.5 * left[:, cols].astype(jnp.float32) - 0.5 * ratio * turned

    def finish(cols, value):
        out[:, cols] = value

    newton_chain(full, ratio, scale, start_of, second, third, finish)


def whole(memory):
    return pl.BlockSpec(memory_space=memory)


def tiles(count):
    return jax.ShapeDtypeStruct((count, TILE, TILE), jnp.bfloat16)


def matrix(rows, cols):
    return pltpu.VMEM((rows, cols), jnp.bfloat16)


def on_device(activations, out_grads, weight_grad):
    rows = weight_grad.shape[0]
    core = lax.axis_index("dp") % 2
    other = (1 - core) * BLK
    params = pltpu.CompilerParams(vmem_limit_bytes=VMEM)

    w_other = lax.dynamic_slice_in_dim(weight_grad, other, BLK, 1)
    w_mine = lax.dynamic_slice_in_dim(weight_grad, core * BLK, BLK, 1)
    g_other = lax.dynamic_slice_in_dim(out_grads, other, BLK, 1)
    g_got = send(g_other, CORE)
    w_near = send(w_mine, Y_NEAR)
    w_cross = send(w_other, Y_NEAR_CORE)
    w_core = send(w_other, CORE)

    pairs = UPPER + [(0, 0)] * (SLOTS - len(UPPER))
    a_sent, a_kept = pl.pallas_call(
        cov_a,
        out_shape=[tiles(4 * PIECE)] * 2,
        in_specs=[whole(pltpu.SMEM)] * 2 + [whole(pltpu.VMEM)],
        out_specs=[whole(pltpu.VMEM)] * 2,
        compiler_params=params,
        cost_estimate=pl.CostEstimate(flops=40 * 2 * 256 * TILE * TILE, bytes_accessed=5 << 20, transcendentals=0),
        name="cov_a",
    )(
        jnp.array([i for i, _ in pairs], jnp.int32),
        jnp.array([j for _, j in pairs], jnp.int32),
        activations,
    )
    first_send, second_send, first_keep, second_keep = pl.pallas_call(
        cov_g,
        out_shape=[tiles(4 * PIECE)] * 4,
        in_specs=[whole(pl.ANY)] * 2,
        out_specs=[whole(pl.ANY)] * 4,
        scratch_shapes=[
            matrix(2 * out_grads.shape[0], BLK),
            pltpu.VMEM((SLOTS, TILE, TILE), jnp.bfloat16),
            pltpu.SemaphoreType.DMA((6,)),
        ],
        compiler_params=params,
        cost_estimate=pl.CostEstimate(flops=21 * 2 * 512 * 256 * 256, bytes_accessed=4 << 20, transcendentals=0),
        name="cov_g",
    )(out_grads, g_got)

    n = PIECE
    first_got = send(first_send, X_HALF)
    second_got = send(second_send, Y_FAR)
    a_sum = add(a_kept, send(a_sent, CORE))
    a_x = send(a_sum[2 * n :], X_HALF)

    first_next = send(add(first_keep[2 * n :], first_got[2 * n :]), Y_FAR)
    second_next = send(add(second_keep[2 * n :], second_got[2 * n :]), Y_NEAR)
    first_sum = add(first_keep[: 2 * n], first_got[: 2 * n])
    second_sum = add(second_keep[: 2 * n], second_got[: 2 * n])
    a_half = add(a_sum[: 2 * n], a_x)
    a_y = send(a_half[n:], Y_FAR)

    first_last = send(add(first_sum[n:], first_next[n:]), Y_NEAR)
    second_last = send(add(second_sum[n:], second_next[n:]), X_HALF)
    first_own = add(add(first_sum[:n], first_next[:n]), first_last)
    second_own = add(add(second_sum[:n], second_next[:n]), second_last)
    a_quarter = add(a_half[:n], a_y)
    a_own = add(a_quarter, send(a_quarter, Y_NEAR))

    first_own = jnp.concatenate([first_own, send(first_own, Y_NEAR)])
    second_own = jnp.concatenate([second_own, send(second_own, X_HALF)])
    a_own = jnp.concatenate([a_own, send(a_own, X_NEAR)])
    first_own = jnp.concatenate([first_own, send(first_own, Y_FAR)])
    second_own = jnp.concatenate([second_own, send(second_own, Y_NEAR)])
    a_parts = [a_own, send(a_own, Z_DOWN), send(a_own, Z_HALF), send(a_own, Z_UP)]
    first_got = send(first_own, X_HALF)
    second_got = send(second_own, Y_FAR)
    a_parts = a_parts + [send(part, CORE) for part in a_parts]

    left = pl.pallas_call(
        left_kernel,
        out_shape=jax.ShapeDtypeStruct((2 * rows, BLK), jnp.bfloat16),
        in_specs=[whole(pl.ANY)] * 12,
        out_specs=whole(pltpu.VMEM),
        scratch_shapes=[
            pltpu.VMEM((SLOTS, TILE, TILE), jnp.bfloat16),
            matrix(BLK, BLK),
            matrix(2 * rows, BLK),
            matrix(2 * rows, BLK),
            matrix(2 * rows, BLK),
            matrix(BLK, BLK),
            pltpu.SemaphoreType.DMA((12,)),
        ],
        compiler_params=params,
        cost_estimate=pl.CostEstimate(flops=6 * 2 * rows * BLK * BLK, bytes_accessed=10 << 20, transcendentals=0),
        name="left",
    )(*a_parts, weight_grad, w_core, w_near, w_cross)
    block = pl.pallas_call(
        right_kernel,
        out_shape=jax.ShapeDtypeStruct((2 * rows, BLK), jnp.bfloat16),
        in_specs=[whole(pl.ANY)] * 4 + [whole(pltpu.VMEM)],
        out_specs=whole(pltpu.VMEM),
        scratch_shapes=[
            pltpu.VMEM((SLOTS, TILE, TILE), jnp.bfloat16),
            matrix(BLK, BLK),
            matrix(2 * rows, BLK),
            matrix(2 * rows, BLK),
            pltpu.SemaphoreType.DMA((4,)),
        ],
        compiler_params=params,
        cost_estimate=pl.CostEstimate(flops=6 * 2 * rows * BLK * BLK, bytes_accessed=8 << 20, transcendentals=0),
        name="right",
    )(first_own, first_got, second_own, second_got, left)
    mine = lax.dynamic_slice_in_dim(block, core * rows, rows, 0)
    theirs = send(lax.dynamic_slice_in_dim(block, (1 - core) * rows, rows, 0), CORE)
    return jnp.where(core == 0, jnp.concatenate([mine, theirs], 1), jnp.concatenate([theirs, mine], 1))


def solution(mesh):
    return jax.shard_map(
        on_device,
        mesh=mesh,
        in_specs=(P("dp", None), P("dp", "tensor"), P("dp", "tensor")),
        out_specs=P("dp", "tensor"),
        check_vma=False,
    )
```

time: 582 us -> 190 us (0.33)
  waiting for transfers between devices: 435 us -> 87 us
  matrix products: 70.7 us -> 0 us
  Pallas kernels: 0 us -> 48.3 us
  other arithmetic: 47.7 us -> 3.97 us
  starting transfers between devices: 3.85 us -> 45.6 us
  between operations: 13.9 us -> 0.36 us
    psum x3 -> x0, waiting for transfers between devices: 420 us -> none  [the longest x1 181 us: on_device(): lax.psum(a_partial, 'dp').astype(jnp.float32)]
    ppermute x2 -> x29, waiting for transfers between devices: 15 us -> 87 us  [send(): return lax.ppermute(array, AXES, pairs)]
    dot_general x7 -> x0, matrix products: 70.7 us -> none  [the longest x2 36.8 us: newton_rows(): second = jnp.dot(product, first, preferred_element_type=jnp.float32)]
    pallas_call x0 -> x4, Pallas kernels: none -> 48.3 us  [the longest x1 19.7 us: on_device(): pl.pallas_call(right_kernel, out_shape=jax.ShapeDtypeStruct((2 * rows, BL...]
    ppermute x2 -> x29, starting transfers between devices: 3.76 us -> 45.6 us  [send(): return lax.ppermute(array, AXES, pairs)]
    another operation x2 -> x0, other arithmetic: 14.9 us -> none  [the longest x1 8.25 us: on_device(): jnp.stack([covar_block(out_grads, job * BLK) for job in range(g_blocks)])]
    div x1 -> x0, other arithmetic: 12.9 us -> none  [on_device(): g_total = g_total / token_total]
    reduce_sum x2 -> x0, other arithmetic: 7.64 us -> none  [damped_pair(): mean_diag = jnp.trace(covar) / BLK + 1e-06]
  transfers between devices with their start and end apart: 5 -> 29, of which waited for: 5 -> 12; matrix products, arithmetic and copies ran while one was open for 4% -> 1% of each run, Pallas kernels for 0% -> 13%
where the time goes in v1:
time: 190 us
  waiting for transfers between devices  87 us (46%)
  Pallas kernels  48.3 us (25%)
  starting transfers between devices  45.6 us (24%)
  local copies, waits for them, and re-layouts  4.66 us (2%)
  other arithmetic  3.97 us (2%)
    ppermute x29, waiting for transfers between devices, send(): return lax.ppermute(array, AXES, pairs)  87 us
    ppermute x29, starting transfers between devices, send(): return lax.ppermute(array, AXES, pairs)  45.6 us
    pallas_call x1, Pallas kernels, on_device(): pl.pallas_call(right_kernel, out_shape=jax.ShapeDtypeStruct((2 * rows, BL...  19.7 us
    pallas_call x1, Pallas kernels, on_device(): pl.pallas_call(left_kernel, out_shape=jax.ShapeDtypeStruct((2 * rows, BLK...  19.1 us
    pallas_call x1, Pallas kernels, on_device(): pl.pallas_call(cov_a, out_shape=[tiles(4 * PIECE)] * 2, in_specs=[whole(p...  4.73 us
    pallas_call x1, Pallas kernels, on_device(): pl.pallas_call(cov_g, out_shape=[tiles(4 * PIECE)] * 4, in_specs=[whole(p...  4.66 us
  transfers between devices with their start and end apart: 29, of which 12 were waited for; matrix products, arithmetic and copies ran while one was open for 1% of the time, Pallas kernels for 13%

profile of v1, /device:TPU:1, one launch (start us, length us, event | category | flops | bytes accessed | tf_op | source)
XLA Modules:
  0.0 189.8 jit_solution(8818091971769574108)
XLA Ops:
  0.0 4.7 %cov_a.1 = (bf16[20,128,128]{2,1,0:T(8,128)(2,1)}, bf16[20,128,128]{2,1,0:T(8,128)(2,1)}) custom-call(s32[80]{0:T(128)} %constant.33.clone.rows, s32[80]{0:T(128)} %constant.34.clone.cols, bf16[256,6144]{1,0:T(8,128)(2,1)} %tokens.1), custom_call_target="tpu_custom_call" | custom-call | flops 335544320 | bytes 5242880 | tf_op jit(solution)/shard_map/cov_a/pallas_call | solution.py:273
  4.7 1.4 collective-permute-start.13
  6.3 1.8 collective-permute-done.13
  8.1 1.3 add_convert_fusion
  9.4 2.9 %collective-permute-start.14 = (bf16[10,128,128]{2,1,0:T(8,128)(2,1)S(1)}, bf16[10,128,128]{2,1,0:T(8,128)(2,1)S(1)}, u32[]{:S(2)}, u32[]{:S(2)}) collective-permute-start(bf16[10,128,128]{2,1,0:T(8,128)(2,1)S(1)} %slice.93), channel_id=1, source_target_pairs={{0,64},{1,65},{2,66},{3,67},{4,68},{5,69},{6,70},{7,71},{8,72},{9,... | collective-permute-start | bytes 983048 | tf_op jit(solution)/shard_map/ppermute | solution.py:43
  12.3 7.6 %collective-permute-done.14 = bf16[10,128,128]{2,1,0:T(8,128)(2,1)S(1)} collective-permute-done((bf16[10,128,128]{2,1,0:T(8,128)(2,1)S(1)}, bf16[10,128,128]{2,1,0:T(8,128)(2,1)S(1)}, u32[]{:S(2)}, u32[]{:S(2)}) %collective-permute-start.14) | collective-permute-done | bytes 327712 | tf_op jit(solution)/shard_map/ppermute | solution.py:43
  20.0 2.9 %collective-permute-start.15 = (bf16[5,128,128]{2,1,0:T(8,128)(2,1)S(1)}, bf16[5,128,128]{2,1,0:T(8,128)(2,1)S(1)}, u32[]{:S(2)}, u32[]{:S(2)}) collective-permute-start(bf16[5,128,128]{2,1,0:T(8,128)(2,1)S(1)} %slice.95), channel_id=1, source_target_pairs={{0,48},{1,49},{2,50},{3,51},{4,52},{5,53},{6,54},{7,55},{8,56},{9,... | collective-permute-start | bytes 491528 | tf_op jit(solution)/shard_map/ppermute | solution.py:43
  23.8 4.7 %cov_g.1 = (bf16[20,128,128]{2,1,0:T(8,128)(2,1)}, bf16[20,128,128]{2,1,0:T(8,128)(2,1)}, bf16[20,128,128]{2,1,0:T(8,128)(2,1)}, bf16[20,128,128]{2,1,0:T(8,128)(2,1)}) custom-call(bf16[256,3072]{1,0:T(8,128)(2,1)} %own.1, bf16[256,1536]{1,0:T(8,128)(2,1)} %copy-done.9), custom_call_target="tpu_custom_call" | custom-call | flops 1409286144 | bytes 4194304 | tf_op jit(solution)/shard_map/cov_g/pallas_call | solution.py:286
  28.6 2.8 %collective-permute-start.1 = (bf16[20,128,128]{2,1,0:T(8,128)(2,1)}, bf16[20,128,128]{2,1,0:T(8,128)(2,1)S(1)}, u32[]{:S(2)}, u32[]{:S(2)}) collective-permute-start(bf16[20,128,128]{2,1,0:T(8,128)(2,1)} %get-tuple-element.12), channel_id=1, source_target_pairs={{0,64},{1,65},{2,66},{3,67},{4,68},{5,69},{6,70},{7,71},{8,72},{9,... | collective-permute-start | bytes 1966088 | tf_op jit(solution)/shard_map/ppermute | solution.py:43
  31.7 2.3 %collective-permute-start.25 = (bf16[384,1536]{1,0:T(8,128)(2,1)S(1)}, bf16[384,1536]{1,0:T(8,128)(2,1)S(1)}, u32[]{:S(2)}, u32[]{:S(2)}) collective-permute-start(bf16[384,1536]{1,0:T(8,128)(2,1)S(1)} %get-tuple-element.20), channel_id=1, source_target_pairs={{0,8},{1,9},{2,10},{3,11},{4,12},{5,13},{6,14},{7,15},{8,0},{9,1},... | collective-permute-start | bytes 3538952 | tf_op jit(solution)/shard_map/ppermute | solution.py:43
  34.0 1.4 collective-permute-start.27
  36.0 8.7 %collective-permute-done.7 = bf16[20,128,128]{2,1,0:T(8,128)(2,1)S(1)} collective-permute-done((bf16[20,128,128]{2,1,0:T(8,128)(2,1)}, bf16[20,128,128]{2,1,0:T(8,128)(2,1)S(1)}, u32[]{:S(2)}, u32[]{:S(2)}) %collective-permute-start.7) | collective-permute-done | bytes 655392 | tf_op jit(solution)/shard_map/ppermute | solution.py:43
  46.4 2.8 %collective-permute-done.17 = bf16[5,128,128]{2,1,0:T(8,128)(2,1)S(1)} collective-permute-done((bf16[5,128,128]{2,1,0:T(8,128)(2,1)S(1)}, bf16[5,128,128]{2,1,0:T(8,128)(2,1)S(1)}, u32[]{:S(2)}, u32[]{:S(2)}) %collective-permute-start.17) | collective-permute-done | bytes 163872 | tf_op jit(solution)/shard_map/ppermute | solution.py:43
  49.3 2.0 %collective-permute-start.2 = (bf16[10,128,128]{2,1,0:T(8,128)(2,1)S(1)}, bf16[10,128,128]{2,1,0:T(8,128)(2,1)S(1)}, u32[]{:S(2)}, u32[]{:S(2)}) collective-permute-start(bf16[10,128,128]{2,1,0:T(8,128)(2,1)S(1)} %get-tuple-element.24), channel_id=1, source_target_pairs={{0,48},{1,49},{2,50},{3,51},{4,52},{5,53},{6,54},{7,55},{8,56},{9,... | collective-permute-start | bytes 983048 | tf_op jit(solution)/shard_map/ppermute | solution.py:43
  51.3 43.0 %collective-permute-done.8 = bf16[10,128,128]{2,1,0:T(8,128)(2,1)S(1)} collective-permute-done((bf16[10,128,128]{2,1,0:T(8,128)(2,1)S(1)}, bf16[10,128,128]{2,1,0:T(8,128)(2,1)S(1)}, u32[]{:S(2)}, u32[]{:S(2)}) %collective-permute-start.8) | collective-permute-done | bytes 327712 | tf_op jit(solution)/shard_map/ppermute | solution.py:43
  94.3 3.8 %collective-permute-start.18 = (bf16[10,128,128]{2,1,0:T(8,128)(2,1)S(1)}, bf16[10,128,128]{2,1,0:T(8,128)(2,1)S(1)}, u32[]{:S(2)}, u32[]{:S(2)}) collective-permute-start(bf16[10,128,128]{2,1,0:T(8,128)(2,1)S(1)} %pad_maximum_fusion.4.refs_0_), channel_id=1, source_target_pairs={{0,3},{1,0},{2,1},{3,2},{4,7},{5,4},{6,5},{7,6},{8,11},{9,8},{10,9... | collective-permute-start | bytes 983048 | tf_op jit(solution)/shard_map/ppermute | solution.py:43
  98.5 5.4 %collective-permute-done.9 = bf16[5,128,128]{2,1,0:T(8,128)(2,1)S(1)} collective-permute-done((bf16[5,128,128]{2,1,0:T(8,128)(2,1)S(1)}, bf16[5,128,128]{2,1,0:T(8,128)(2,1)S(1)}, u32[]{:S(2)}, u32[]{:S(2)}) %collective-permute-start.9) | collective-permute-done | bytes 163872 | tf_op jit(solution)/shard_map/ppermute | solution.py:43
  103.9 1.9 %collective-permute-start.3 = (bf16[5,128,128]{2,1,0:T(8,128)(2,1)S(1)}, bf16[5,128,128]{2,1,0:T(8,128)(2,1)S(1)}, u32[]{:S(2)}, u32[]{:S(2)}) collective-permute-start(bf16[5,128,128]{2,1,0:T(8,128)(2,1)S(1)} %add_convert_fusion.12), channel_id=1, source_target_pairs={{0,16},{1,17},{2,18},{3,19},{4,20},{5,21},{6,22},{7,23},{8,24},{9,... | collective-permute-start | bytes 491528 | tf_op jit(solution)/shard_map/ppermute | solution.py:43
  105.9 2.6 %collective-permute-done.3 = bf16[5,128,128]{2,1,0:T(8,128)(2,1)S(1)} collective-permute-done((bf16[5,128,128]{2,1,0:T(8,128)(2,1)S(1)}, bf16[5,128,128]{2,1,0:T(8,128)(2,1)S(1)}, u32[]{:S(2)}, u32[]{:S(2)}) %collective-permute-start.3) | collective-permute-done | bytes 163872 | tf_op jit(solution)/shard_map/ppermute | solution.py:43
  108.8 5.4 %collective-permute-done.10 = bf16[5,128,128]{2,1,0:T(8,128)(2,1)S(1)} collective-permute-done((bf16[5,128,128]{2,1,0:T(8,128)(2,1)S(1)}, bf16[5,128,128]{2,1,0:T(8,128)(2,1)S(1)}, u32[]{:S(2)}, u32[]{:S(2)}) %collective-permute-start.10) | collective-permute-done | bytes 163872 | tf_op jit(solution)/shard_map/ppermute | solution.py:43
  114.2 1.5 collective-permute-start.4
  115.7 3.0 %collective-permute-done.4 = bf16[5,128,128]{2,1,0:T(8,128)(2,1)S(1)} collective-permute-done((bf16[5,128,128]{2,1,0:T(8,128)(2,1)S(1)}, bf16[5,128,128]{2,1,0:T(8,128)(2,1)S(1)}, u32[]{:S(2)}, u32[]{:S(2)}) %collective-permute-start.4) | collective-permute-done | bytes 163872 | tf_op jit(solution)/shard_map/ppermute | solution.py:43
  121.0 1.6 collective-permute-start.5
  122.6 3.6 %collective-permute-done.19.refs_2_ = bf16[10,128,128]{2,1,0:T(8,128)(2,1)S(1)} collective-permute-done((bf16[10,128,128]{2,1,0:T(8,128)(2,1)S(1)}, bf16[10,128,128]{2,1,0:T(8,128)(2,1)S(1)}, u32[]{:S(2)}, u32[]{:S(2)}) %collective-permute-start.19) | collective-permute-done | bytes 327712 | tf_op jit(solution)/shard_map/ppermute | solution.py:43
  126.2 9.0 %collective-permute-start.21 = (bf16[10,128,128]{2,1,0:T(8,128)(2,1)S(1)}, bf16[10,128,128]{2,1,0:T(8,128)(2,1)}, u32[]{:S(2)}, u32[]{:S(2)}) collective-permute-start(bf16[10,128,128]{2,1,0:T(8,128)(2,1)S(1)} %pad_maximum_fusion.4.refs_0_), channel_id=1, source_target_pairs={{0,8},{1,9},{2,10},{3,11},{4,12},{5,13},{6,14},{7,15},{8,0},{9,1},... | collective-permute-start | bytes 983048 | tf_op jit(solution)/shard_map/ppermute | solution.py:43
  135.2 3.3 %collective-permute-start.22 = (bf16[10,128,128]{2,1,0:T(8,128)(2,1)S(1)}, bf16[10,128,128]{2,1,0:T(8,128)(2,1)}, u32[]{:S(2)}, u32[]{:S(2)}) collective-permute-start(bf16[10,128,128]{2,1,0:T(8,128)(2,1)S(1)} %collective-permute-done.18.refs_1_), channel_id=1, source_target_pairs={{0,8},{1,9},{2,10},{3,11},{4,12},{5,13},{6,14},{7,15},{8,0},{9,1},... | collective-permute-start | bytes 983048 | tf_op jit(solution)/shard_map/ppermute | solution.py:43
  139.5 2.8 %collective-permute-start.12 = (bf16[20,128,128]{2,1,0:T(8,128)(2,1)S(1)}, bf16[20,128,128]{2,1,0:T(8,128)(2,1)S(1)}, u32[]{:S(2)}, u32[]{:S(2)}) collective-permute-start(bf16[20,128,128]{2,1,0:T(8,128)(2,1)S(1)} %pad_maximum_fusion.1.second_own), channel_id=1, source_target_pairs={{0,48},{1,49},{2,50},{3,51},{4,52},{5,53},{6,54},{7,55},{8,56},{9,... | collective-permute-start | bytes 1966088 | tf_op jit(solution)/shard_map/ppermute | solution.py:43
  142.6 19.1 %left.1 = bf16[768,1536]{1,0:T(8,128)(2,1)} custom-call(bf16[10,128,128]{2,1,0:T(8,128)(2,1)} %copy-done.6, bf16[10,128,128]{2,1,0:T(8,128)(2,1)} %copy-done.12, bf16[10,128,128]{2,1,0:T(8,128)(2,1)} %copy-done.13, bf16[10,128,128]{2,1,0:T(8,128)(2,1)} %collective-permute-done.20.refs_3_, bf16[10,128,128]{2,1,0:T(8,128)(2,1)} %collective-permute-done.21.refs_4_, ...), custom_call_target="tpu_custom_call" | custom-call | flops 10871635968 | bytes 10485760 | tf_op jit(solution)/shard_map/left/pallas_call | solution.py:331
  163.4 19.7 %right.1 = bf16[768,1536]{1,0:T(8,128)(2,1)} custom-call(bf16[20,128,128]{2,1,0:T(8,128)(2,1)} %copy-done.2, bf16[20,128,128]{2,1,0:T(8,128)(2,1)} %copy-done.11, bf16[20,128,128]{2,1,0:T(8,128)(2,1)} %copy-done.1, bf16[20,128,128]{2,1,0:T(8,128)(2,1)} %copy-done.10, bf16[768,1536]{1,0:T(8,128)(2,1)} %left.1), custom_call_target="tpu_custom_call" | custom-call | flops 10871635968 | bytes 8388608 | tf_op jit(solution)/shard_map/right/pallas_call | solution.py:349
  183.2 1.8 constant_dynamic-slice_fusion.1
  185.7 2.5 %collective-permute-done.28 = bf16[384,1536]{1,0:T(8,128)(2,1)S(1)} collective-permute-done((bf16[384,1536]{1,0:T(8,128)(2,1)S(1)}, bf16[384,1536]{1,0:T(8,128)(2,1)S(1)}, u32[]{:S(2)}, u32[]{:S(2)}) %collective-permute-start.28) | collective-permute-done | bytes 1179680 | tf_op jit(solution)/shard_map/ppermute | solution.py:43
  188.1 1.7 maximum_select_fusion
  (79 shorter events, 10.5 us)
Async XLA Ops:
  4.7 3.4 %collective-permute-start.13 = (bf16[20,128,128]{2,1,0:T(8,128)(2,1)}, bf16[20,128,128]{2,1,0:T(8,128)(2,1)S(1)}, u32[]{:S(2)}, u32[]{:S(2)}) collective-permute-start(bf16[20,128,128]{2,1,0:T(8,128)(2,1)} %get-tuple-element.16), channel_id=1, source_target_pairs={{0,8},{1,9},{2,10},{3,11},{4,12},{5,13},{6,14},{7,15},{8,0},{9,1},... | collective-permute-start | bytes 1966088 | tf_op jit(solution)/shard_map/ppermute | solution.py:43
  6.2 16.7 %collective-permute-start = (bf16[256,1536]{1,0:T(8,128)(2,1)S(1)}, bf16[256,1536]{1,0:T(8,128)(2,1)S(1)}, u32[]{:S(2)}, u32[]{:S(2)}) collective-permute-start(bf16[256,1536]{1,0:T(8,128)(2,1)S(1)} %constant_dynamic-slice_fusion.4), channel_id=1, source_target_pairs={{0,8},{1,9},{2,10},{3,11},{4,12},{5,13},{6,14},{7,15},{8,0},{9,1},... | collective-permute-start | bytes 2359304 | tf_op jit(solution)/shard_map/ppermute | solution.py:43
  9.4 10.5 %collective-permute-start.14 = (bf16[10,128,128]{2,1,0:T(8,128)(2,1)S(1)}, bf16[10,128,128]{2,1,0:T(8,128)(2,1)S(1)}, u32[]{:S(2)}, u32[]{:S(2)}) collective-permute-start(bf16[10,128,128]{2,1,0:T(8,128)(2,1)S(1)} %slice.93), channel_id=1, source_target_pairs={{0,64},{1,65},{2,66},{3,67},{4,68},{5,69},{6,70},{7,71},{8,72},{9,... | collective-permute-start | bytes 983048 | tf_op jit(solution)/shard_map/ppermute | solution.py:43
  20.0 11.4 %collective-permute-start.15 = (bf16[5,128,128]{2,1,0:T(8,128)(2,1)S(1)}, bf16[5,128,128]{2,1,0:T(8,128)(2,1)S(1)}, u32[]{:S(2)}, u32[]{:S(2)}) collective-permute-start(bf16[5,128,128]{2,1,0:T(8,128)(2,1)S(1)} %slice.95), channel_id=1, source_target_pairs={{0,48},{1,49},{2,50},{3,51},{4,52},{5,53},{6,54},{7,55},{8,56},{9,... | collective-permute-start | bytes 491528 | tf_op jit(solution)/shard_map/ppermute | solution.py:43
  28.5 16.2 %collective-permute-start.7 = (bf16[20,128,128]{2,1,0:T(8,128)(2,1)}, bf16[20,128,128]{2,1,0:T(8,128)(2,1)S(1)}, u32[]{:S(2)}, u32[]{:S(2)}) collective-permute-start(bf16[20,128,128]{2,1,0:T(8,128)(2,1)} %get-tuple-element.14), channel_id=1, source_target_pairs={{0,48},{1,49},{2,50},{3,51},{4,52},{5,53},{6,54},{7,55},{8,56},{9,... | collective-permute-start | bytes 1966088 | tf_op jit(solution)/shard_map/ppermute | solution.py:43
  28.6 17.5 %collective-permute-start.1 = (bf16[20,128,128]{2,1,0:T(8,128)(2,1)}, bf16[20,128,128]{2,1,0:T(8,128)(2,1)S(1)}, u32[]{:S(2)}, u32[]{:S(2)}) collective-permute-start(bf16[20,128,128]{2,1,0:T(8,128)(2,1)} %get-tuple-element.12), channel_id=1, source_target_pairs={{0,64},{1,65},{2,66},{3,67},{4,68},{5,69},{6,70},{7,71},{8,72},{9,... | collective-permute-start | bytes 1966088 | tf_op jit(solution)/shard_map/ppermute | solution.py:43
  31.4 4.5 %collective-permute-start.16 = (bf16[5,128,128]{2,1,0:T(8,128)(2,1)S(1)}, bf16[5,128,128]{2,1,0:T(8,128)(2,1)S(1)}, u32[]{:S(2)}, u32[]{:S(2)}) collective-permute-start(bf16[5,128,128]{2,1,0:T(8,128)(2,1)S(1)} %add_convert_fusion.7), channel_id=1, source_target_pairs={{0,16},{1,17},{2,18},{3,19},{4,20},{5,21},{6,22},{7,23},{8,24},{9,... | collective-permute-start | bytes 491528 | tf_op jit(solution)/shard_map/ppermute | solution.py:43
  31.7 87.0 %collective-permute-start.25 = (bf16[384,1536]{1,0:T(8,128)(2,1)S(1)}, bf16[384,1536]{1,0:T(8,128)(2,1)S(1)}, u32[]{:S(2)}, u32[]{:S(2)}) collective-permute-start(bf16[384,1536]{1,0:T(8,128)(2,1)S(1)} %get-tuple-element.20), channel_id=1, source_target_pairs={{0,8},{1,9},{2,10},{3,11},{4,12},{5,13},{6,14},{7,15},{8,0},{9,1},... | collective-permute-start | bytes 3538952 | tf_op jit(solution)/shard_map/ppermute | solution.py:43
  34.0 105.5 %collective-permute-start.27 = (bf16[384,1536]{1,0:T(8,128)(2,1)S(1)}, bf16[384,1536]{1,0:T(8,128)(2,1)}, u32[]{:S(2)}, u32[]{:S(2)}) collective-permute-start(bf16[384,1536]{1,0:T(8,128)(2,1)S(1)} %get-tuple-element.20), channel_id=1, source_target_pairs={{0,24},{1,25},{2,26},{3,27},{4,28},{5,29},{6,30},{7,31},{8,16},{9,... | collective-permute-start | bytes 3538952 | tf_op jit(solution)/shard_map/ppermute | solution.py:43
  36.0 83.8 %collective-permute-start.26 = (bf16[384,1536]{1,0:T(8,128)(2,1)S(1)}, bf16[384,1536]{1,0:T(8,128)(2,1)S(1)}, u32[]{:S(2)}, u32[]{:S(2)}) collective-permute-start(bf16[384,1536]{1,0:T(8,128)(2,1)S(1)} %get-tuple-element.19), channel_id=1, source_target_pairs={{0,16},{1,17},{2,18},{3,19},{4,20},{5,21},{6,22},{7,23},{8,24},{9,... | collective-permute-start | bytes 3538952 | tf_op jit(solution)/shard_map/ppermute | solution.py:43
  44.7 4.6 %collective-permute-start.17 = (bf16[5,128,128]{2,1,0:T(8,128)(2,1)S(1)}, bf16[5,128,128]{2,1,0:T(8,128)(2,1)S(1)}, u32[]{:S(2)}, u32[]{:S(2)}) collective-permute-start(bf16[5,128,128]{2,1,0:T(8,128)(2,1)S(1)} %add_convert_fusion.6), channel_id=1, source_target_pairs={{0,4},{1,5},{2,6},{3,7},{4,0},{5,1},{6,2},{7,3},{8,12},{9,13},{10,... | collective-permute-start | bytes 491528 | tf_op jit(solution)/shard_map/ppermute | solution.py:43
  46.1 48.2 %collective-permute-start.8 = (bf16[10,128,128]{2,1,0:T(8,128)(2,1)S(1)}, bf16[10,128,128]{2,1,0:T(8,128)(2,1)S(1)}, u32[]{:S(2)}, u32[]{:S(2)}) collective-permute-start(bf16[10,128,128]{2,1,0:T(8,128)(2,1)S(1)} %get-tuple-element.22), channel_id=1, source_target_pairs={{0,16},{1,17},{2,18},{3,19},{4,20},{5,21},{6,22},{7,23},{8,24},{9,... | collective-permute-start | bytes 983048 | tf_op jit(solution)/shard_map/ppermute | solution.py:43
  49.3 48.9 %collective-permute-start.2 = (bf16[10,128,128]{2,1,0:T(8,128)(2,1)S(1)}, bf16[10,128,128]{2,1,0:T(8,128)(2,1)S(1)}, u32[]{:S(2)}, u32[]{:S(2)}) collective-permute-start(bf16[10,128,128]{2,1,0:T(8,128)(2,1)S(1)} %get-tuple-element.24), channel_id=1, source_target_pairs={{0,48},{1,49},{2,50},{3,51},{4,52},{5,53},{6,54},{7,55},{8,56},{9,... | collective-permute-start | bytes 983048 | tf_op jit(solution)/shard_map/ppermute | solution.py:43
  51.3 88.1 %copy-start.6 = (bf16[10,128,128]{2,1,0:T(8,128)(2,1)}, bf16[10,128,128]{2,1,0:T(8,128)(2,1)S(1)}, u32[]{:S(2)}) copy-start(bf16[10,128,128]{2,1,0:T(8,128)(2,1)S(1)} %pad_maximum_fusion.4.refs_0_) | copy-start | bytes 983044
  94.3 26.7 %collective-permute-start.18 = (bf16[10,128,128]{2,1,0:T(8,128)(2,1)S(1)}, bf16[10,128,128]{2,1,0:T(8,128)(2,1)S(1)}, u32[]{:S(2)}, u32[]{:S(2)}) collective-permute-start(bf16[10,128,128]{2,1,0:T(8,128)(2,1)S(1)} %pad_maximum_fusion.4.refs_0_), channel_id=1, source_target_pairs={{0,3},{1,0},{2,1},{3,2},{4,7},{5,4},{6,5},{7,6},{8,11},{9,8},{10,9... | collective-permute-start | bytes 983048 | tf_op jit(solution)/shard_map/ppermute | solution.py:43
  98.1 5.8 %collective-permute-start.9 = (bf16[5,128,128]{2,1,0:T(8,128)(2,1)S(1)}, bf16[5,128,128]{2,1,0:T(8,128)(2,1)S(1)}, u32[]{:S(2)}, u32[]{:S(2)}) collective-permute-start(bf16[5,128,128]{2,1,0:T(8,128)(2,1)S(1)} %add_convert_fusion.9), channel_id=1, source_target_pairs={{0,64},{1,65},{2,66},{3,67},{4,68},{5,69},{6,70},{7,71},{8,72},{9,... | collective-permute-start | bytes 491528 | tf_op jit(solution)/shard_map/ppermute | solution.py:43
  103.9 4.7 %collective-permute-start.3 = (bf16[5,128,128]{2,1,0:T(8,128)(2,1)S(1)}, bf16[5,128,128]{2,1,0:T(8,128)(2,1)S(1)}, u32[]{:S(2)}, u32[]{:S(2)}) collective-permute-start(bf16[5,128,128]{2,1,0:T(8,128)(2,1)S(1)} %add_convert_fusion.12), channel_id=1, source_target_pairs={{0,16},{1,17},{2,18},{3,19},{4,20},{5,21},{6,22},{7,23},{8,24},{9,... | collective-permute-start | bytes 491528 | tf_op jit(solution)/shard_map/ppermute | solution.py:43
  108.5 5.7 %collective-permute-start.10 = (bf16[5,128,128]{2,1,0:T(8,128)(2,1)S(1)}, bf16[5,128,128]{2,1,0:T(8,128)(2,1)S(1)}, u32[]{:S(2)}, u32[]{:S(2)}) collective-permute-start(bf16[5,128,128]{2,1,0:T(8,128)(2,1)S(1)} %add_convert_fusion.8), channel_id=1, source_target_pairs={{0,64},{1,65},{2,66},{3,67},{4,68},{5,69},{6,70},{7,71},{8,72},{9,... | collective-permute-start | bytes 491528 | tf_op jit(solution)/shard_map/ppermute | solution.py:43
  114.2 4.5 %collective-permute-start.4 = (bf16[5,128,128]{2,1,0:T(8,128)(2,1)S(1)}, bf16[5,128,128]{2,1,0:T(8,128)(2,1)S(1)}, u32[]{:S(2)}, u32[]{:S(2)}) collective-permute-start(bf16[5,128,128]{2,1,0:T(8,128)(2,1)S(1)} %add_convert_fusion.11), channel_id=1, source_target_pairs={{0,16},{1,17},{2,18},{3,19},{4,20},{5,21},{6,22},{7,23},{8,24},{9,... | collective-permute-start | bytes 491528 | tf_op jit(solution)/shard_map/ppermute | solution.py:43
  118.7 7.5 %collective-permute-start.19 = (bf16[10,128,128]{2,1,0:T(8,128)(2,1)S(1)}, bf16[10,128,128]{2,1,0:T(8,128)(2,1)S(1)}, u32[]{:S(2)}, u32[]{:S(2)}) collective-permute-start(bf16[10,128,128]{2,1,0:T(8,128)(2,1)S(1)} %pad_maximum_fusion.4.refs_0_), channel_id=1, source_target_pairs={{0,2},{1,3},{2,0},{3,1},{4,6},{5,7},{6,4},{7,5},{8,10},{9,11},{10,... | collective-permute-start | bytes 983048 | tf_op jit(solution)/shard_map/ppermute | solution.py:43
  118.8 16.5 %collective-permute-start.20 = (bf16[10,128,128]{2,1,0:T(8,128)(2,1)S(1)}, bf16[10,128,128]{2,1,0:T(8,128)(2,1)}, u32[]{:S(2)}, u32[]{:S(2)}) collective-permute-start(bf16[10,128,128]{2,1,0:T(8,128)(2,1)S(1)} %pad_maximum_fusion.4.refs_0_), channel_id=1, source_target_pairs={{0,1},{1,2},{2,3},{3,0},{4,5},{5,6},{6,7},{7,4},{8,9},{9,10},{10,1... | collective-permute-start | bytes 983048 | tf_op jit(solution)/shard_map/ppermute | solution.py:43
  119.8 18.8 %collective-permute-start.11 = (bf16[10,128,128]{2,1,0:T(8,128)(2,1)S(1)}, bf16[10,128,128]{2,1,0:T(8,128)(2,1)S(1)}, u32[]{:S(2)}, u32[]{:S(2)}) collective-permute-start(bf16[10,128,128]{2,1,0:T(8,128)(2,1)S(1)} %pad_maximum_fusion.3), channel_id=1, source_target_pairs={{0,16},{1,17},{2,18},{3,19},{4,20},{5,21},{6,22},{7,23},{8,24},{9,... | collective-permute-start | bytes 983048 | tf_op jit(solution)/shard_map/ppermute | solution.py:43
  121.0 17.6 %collective-permute-start.5 = (bf16[10,128,128]{2,1,0:T(8,128)(2,1)S(1)}, bf16[10,128,128]{2,1,0:T(8,128)(2,1)S(1)}, u32[]{:S(2)}, u32[]{:S(2)}) collective-permute-start(bf16[10,128,128]{2,1,0:T(8,128)(2,1)S(1)} %pad_maximum_fusion.2), channel_id=1, source_target_pairs={{0,48},{1,49},{2,50},{3,51},{4,52},{5,53},{6,54},{7,55},{8,56},{9,... | collective-permute-start | bytes 983048 | tf_op jit(solution)/shard_map/ppermute | solution.py:43
  126.2 16.1 %collective-permute-start.21 = (bf16[10,128,128]{2,1,0:T(8,128)(2,1)S(1)}, bf16[10,128,128]{2,1,0:T(8,128)(2,1)}, u32[]{:S(2)}, u32[]{:S(2)}) collective-permute-start(bf16[10,128,128]{2,1,0:T(8,128)(2,1)S(1)} %pad_maximum_fusion.4.refs_0_), channel_id=1, source_target_pairs={{0,8},{1,9},{2,10},{3,11},{4,12},{5,13},{6,14},{7,15},{8,0},{9,1},... | collective-permute-start | bytes 983048 | tf_op jit(solution)/shard_map/ppermute | solution.py:43
  135.2 7.3 %collective-permute-start.22 = (bf16[10,128,128]{2,1,0:T(8,128)(2,1)S(1)}, bf16[10,128,128]{2,1,0:T(8,128)(2,1)}, u32[]{:S(2)}, u32[]{:S(2)}) collective-permute-start(bf16[10,128,128]{2,1,0:T(8,128)(2,1)S(1)} %collective-permute-done.18.refs_1_), channel_id=1, source_target_pairs={{0,8},{1,9},{2,10},{3,11},{4,12},{5,13},{6,14},{7,15},{8,0},{9,1},... | collective-permute-start | bytes 983048 | tf_op jit(solution)/shard_map/ppermute | solution.py:43
  138.6 4.0 %collective-permute-start.23 = (bf16[10,128,128]{2,1,0:T(8,128)(2,1)S(1)}, bf16[10,128,128]{2,1,0:T(8,128)(2,1)}, u32[]{:S(2)}, u32[]{:S(2)}) collective-permute-start(bf16[10,128,128]{2,1,0:T(8,128)(2,1)S(1)} %collective-permute-done.19.refs_2_), channel_id=1, source_target_pairs={{0,8},{1,9},{2,10},{3,11},{4,12},{5,13},{6,14},{7,15},{8,0},{9,1},... | collective-permute-start | bytes 983048 | tf_op jit(solution)/shard_map/ppermute | solution.py:43
  138.6 3.9 %collective-permute-start.24 = (bf16[10,128,128]{2,1,0:T(8,128)(2,1)}, bf16[10,128,128]{2,1,0:T(8,128)(2,1)}, u32[]{:S(2)}, u32[]{:S(2)}) collective-permute-start(bf16[10,128,128]{2,1,0:T(8,128)(2,1)} %collective-permute-done.20.refs_3_), channel_id=1, source_target_pairs={{0,8},{1,9},{2,10},{3,11},{4,12},{5,13},{6,14},{7,15},{8,0},{9,1},... | collective-permute-start | bytes 983048 | tf_op jit(solution)/shard_map/ppermute | solution.py:43
  139.4 22.3 %copy-start.1 = (bf16[20,128,128]{2,1,0:T(8,128)(2,1)}, bf16[20,128,128]{2,1,0:T(8,128)(2,1)S(1)}, u32[]{:S(2)}) copy-start(bf16[20,128,128]{2,1,0:T(8,128)(2,1)S(1)} %pad_maximum_fusion.1.second_own) | copy-start | bytes 1966084
  139.5 22.2 %copy-start.2 = (bf16[20,128,128]{2,1,0:T(8,128)(2,1)}, bf16[20,128,128]{2,1,0:T(8,128)(2,1)S(1)}, u32[]{:S(2)}) copy-start(bf16[20,128,128]{2,1,0:T(8,128)(2,1)S(1)} %pad_maximum_fusion.first_own) | copy-start | bytes 1966084
  139.5 22.2 %collective-permute-start.12 = (bf16[20,128,128]{2,1,0:T(8,128)(2,1)S(1)}, bf16[20,128,128]{2,1,0:T(8,128)(2,1)S(1)}, u32[]{:S(2)}, u32[]{:S(2)}) collective-permute-start(bf16[20,128,128]{2,1,0:T(8,128)(2,1)S(1)} %pad_maximum_fusion.1.second_own), channel_id=1, source_target_pairs={{0,48},{1,49},{2,50},{3,51},{4,52},{5,53},{6,54},{7,55},{8,56},{9,... | collective-permute-start | bytes 1966088 | tf_op jit(solution)/shard_map/ppermute | solution.py:43
  142.3 19.4 %collective-permute-start.6 = (bf16[20,128,128]{2,1,0:T(8,128)(2,1)S(1)}, bf16[20,128,128]{2,1,0:T(8,128)(2,1)S(1)}, u32[]{:S(2)}, u32[]{:S(2)}) collective-permute-start(bf16[20,128,128]{2,1,0:T(8,128)(2,1)S(1)} %pad_maximum_fusion.first_own), channel_id=1, source_target_pairs={{0,64},{1,65},{2,66},{3,67},{4,68},{5,69},{6,70},{7,71},{8,72},{9,... | collective-permute-start | bytes 1966088 | tf_op jit(solution)/shard_map/ppermute | solution.py:43
  185.0 3.2 %collective-permute-start.28 = (bf16[384,1536]{1,0:T(8,128)(2,1)S(1)}, bf16[384,1536]{1,0:T(8,128)(2,1)S(1)}, u32[]{:S(2)}, u32[]{:S(2)}) collective-permute-start(bf16[384,1536]{1,0:T(8,128)(2,1)S(1)} %get-tuple-element.18), channel_id=1, source_target_pairs={{0,8},{1,9},{2,10},{3,11},{4,12},{5,13},{6,14},{7,15},{8,0},{9,1},... | collective-permute-start | bytes 3538952 | tf_op jit(solution)/shard_map/ppermute | solution.py:43
  (11 other events, 122.9 us)

commit v2 on v0

v2 whole, which is shorter than its diff:
```python
import jax
import jax.numpy as jnp
from jax import lax
from jax.experimental import pallas as pl
from jax.experimental.pallas import tpu as pltpu
from jax.sharding import PartitionSpec as P

BLK = 1536
TOKENS = 4096
TILE = 128
SIDE = BLK // TILE
UPPER = [(i, j) for i in range(SIDE) for j in range(i, SIDE)]
SLOTS = 80
PIECE = 10
WIDTH = 5
A_PIECE = 5
STEP = 256
CHUNKS = ((0, 0, 384), (1, 0, 64), (1, 64, 64), (1, 128, 256))
AXES = ("dp", "tensor")
MIB = 1024 * 1024


def moves(target):
    pairs = []
    for dp in range(16):
        for tp in range(8):
            x_hi, y, core = dp // 8, dp // 2 % 4, dp % 2
            x_lo, z = tp // 4, tp % 4
            x_hi, y, core, x_lo, z = target(x_hi, y, core, x_lo, z)
            there = (x_hi * 8 + y * 2 + core) * 8 + x_lo * 4 + z % 4
            pairs.append((dp * 8 + tp, there))
    return pairs


CORE = moves(lambda h, y, c, l, z: (h, y, c ^ 1, l, z))
Y_NEAR = moves(lambda h, y, c, l, z: (h, y ^ 1, c, l, z))
Y_NEAR_CORE = moves(lambda h, y, c, l, z: (h, y ^ 1, c ^ 1, l, z))
Y_FAR = moves(lambda h, y, c, l, z: (h, y ^ 3, c, l, z))
X_HALF = moves(lambda h, y, c, l, z: (h ^ 1, y, c, l, z))
X_Y_FAR = moves(lambda h, y, c, l, z: (h ^ 1, y ^ 3, c, l, z))
X_NEAR = moves(lambda h, y, c, l, z: (h, y, c, l ^ 1, z))
Z_UP = moves(lambda h, y, c, l, z: (h, y, c, l, z + 1))
Z_DOWN = moves(lambda h, y, c, l, z: (h, y, c, l, z + 3))
Z_HALF = moves(lambda h, y, c, l, z: (h, y, c, l, z + 2))


def send(array, pairs, name):
    with jax.named_scope(name):
        return lax.ppermute(array, AXES, pairs)


def together(*values):
    return lax.optimization_barrier(values)


def add(*terms):
    return sum(term.astype(jnp.float32) for term in terms).astype(jnp.bfloat16)


def swapped(array):
    half = array.shape[0] // 2
    return jnp.concatenate([array[half:], array[:half]])


def place():
    dp, tp = lax.axis_index("dp"), lax.axis_index("tensor")
    return dp // 8, dp // 2 % 4, dp % 2, tp // 4, tp % 4


def slot_first(piece, code):
    rel = piece ^ code
    return rel ^ (rel >> 1 & 1)


def slot_second(piece, code):
    rel = piece ^ code
    low, mid, high = rel & 1, rel >> 1 & 1, rel >> 2
    return mid << 2 | (low ^ mid) << 1 | high


def slot_of(tile, code, width):
    piece, at = tile // PIECE, tile % PIECE
    if at < width:
        return 0, slot_first(piece, code), at
    return 1, slot_second(piece, code), at - width


def cov_g(own, got, first_send, second_send, first_keep, second_keep, tokens):
    x_hi, y, core, _, _ = place()
    half = own.shape[0]
    tokens[:half] = own[:, pl.ds(pl.multiple_of(core * BLK, BLK), BLK)]
    tokens[half:] = got[...]
    code = x_hi * 4 + y
    sends, keeps = (first_send, second_send), (first_keep, second_keep)

    def store(tile, value):
        part, piece, at = slot_of(tile, code, WIDTH)
        count = (WIDTH, PIECE - WIDTH)[part]

        @pl.when(piece >= 4)
        def _():
            sends[part][(piece - 4) * count + at] = value

        @pl.when(piece < 4)
        def _():
            keeps[part][piece * count + at] = value

    for row in range(SIDE // 2):
        start = row * 2 * TILE
        product = lax.dot_general(
            tokens[:, start : start + 2 * TILE],
            tokens[:, start:],
            (((0,), (0,)), ((), ())),
            preferred_element_type=jnp.float32,
        ).astype(jnp.bfloat16)
        for tile, (i, j) in enumerate(UPPER):
            if i // 2 == row:
                top, left = (i - 2 * row) * TILE, (j - 2 * row) * TILE
                store(tile, product[top : top + TILE, left : left + TILE])
    for tile in range(len(UPPER), SLOTS):
        store(tile, jnp.zeros((TILE, TILE), jnp.bfloat16))


def corner(tile):
    starts = [i * SIDE - i * (i - 1) // 2 for i in range(SIDE)]
    i = sum((tile >= start).astype(jnp.int32) for start in starts[1:])
    return i, jnp.minimum(tile - (i * SIDE - i * (i - 1) // 2) + i, SIDE - 1)


def cov_a(whole_tokens, whole_weights, sent, kept, *refs):
    chunks, (tokens, sems) = refs[:-2], refs[-2:]
    x_hi, y, core, x_lo, z = place()
    tp = x_lo * 4 + z
    own = x_hi * 2 + y // 2
    loads = [
        pltpu.make_async_copy(
            whole_tokens.at[:, pl.ds(pl.multiple_of((own ^ rel) * BLK, BLK), BLK)], tokens.at[rel], sems.at[rel]
        )
        for rel in range(4)
    ]
    cuts = [
        pltpu.make_async_copy(
            whole_weights.at[pl.ds(start, count), pl.ds(pl.multiple_of((core ^ lane) * BLK, BLK), BLK)],
            chunk,
            sems.at[4 + at],
        )
        for at, ((lane, start, count), chunk) in enumerate(zip(CHUNKS[1:], chunks))
    ]
    for copy in loads + cuts:
        copy.start()
    for rel, load in enumerate(loads):
        load.wait()
        for out, side in ((sent, 1 - core), (kept, core)):
            for at in range(A_PIECE):
                i, j = corner((tp * 2 + side) * A_PIECE + at)
                left, right = (
                    tokens[rel, :, pl.ds(pl.multiple_of(place_of * TILE, TILE), TILE)] for place_of in (i, j)
                )
                out[rel * A_PIECE + at] = lax.dot_general(
                    left, right, (((0,), (0,)), ((), ())), preferred_element_type=jnp.float32
                ).astype(jnp.bfloat16)
    for copy in cuts:
        copy.wait()


def put(full, i, j, value):
    full[i * TILE : (i + 1) * TILE, j * TILE : (j + 1) * TILE] = value
    if i != j:
        full[j * TILE : (j + 1) * TILE, i * TILE : (i + 1) * TILE] = value.T


def diagonal_sum(full):
    row = lax.broadcasted_iota(jnp.int32, (TILE, TILE), 0)
    col = lax.broadcasted_iota(jnp.int32, (TILE, TILE), 1)
    total = jnp.zeros((TILE, TILE), jnp.float32)
    for at in range(0, BLK, TILE):
        total = total + full[at : at + TILE, at : at + TILE].astype(jnp.float32)
    return jnp.sum(jnp.where(row == col, total, 0.0))


def scales(trace):
    mean = trace / (TOKENS * BLK) + 1e-06
    return 1.0 / (TOKENS * mean), 1.0 / (2.0 * mean)


def steps():
    return [slice(at, at + STEP) for at in range(0, BLK, STEP)]


def dot(left, right):
    return jnp.dot(left, right, preferred_element_type=jnp.float32)


def newton_chain(full, ratio, scale, start_of, second, third, finish):
    for cols in steps():
        second[:, cols] = start_of(cols).astype(jnp.bfloat16)
    for cols in steps():
        turned = dot(second[...], full[:, cols])
        third[:, cols] = (second[:, cols].astype(jnp.float32) + ratio * turned).astype(jnp.bfloat16)
    for cols in steps():
        turned = dot(third[...], full[:, cols])
        value = 2.0 * second[:, cols].astype(jnp.float32) - 0.75 * third[:, cols].astype(jnp.float32)
        finish(cols, (scale * (value + 0.25 * ratio * turned)).astype(jnp.bfloat16))


def inverse_kernel(*refs):
    parts, out, packed, full, second, third = refs[:10], *refs[10:]
    _, y, core, x_lo, z = place()
    rows = out.shape[0]
    start = 0
    for part in parts:
        packed[start : start + part.shape[0]] = part[...]
        start += part.shape[0]
    for tile, (i, j) in enumerate(UPPER):
        piece, at = tile // A_PIECE, tile % A_PIECE
        side, z_at, x_at = piece % 2, piece // 2 % 4, piece // 8
        slot = (((side ^ core) * 4 + (z_at - z + 4) % 4) * 2 + (x_at ^ x_lo)) * A_PIECE + at
        put(full, i, j, packed[slot])
    ratio, scale = scales(diagonal_sum(full))
    first_row = pl.multiple_of(y % 2 * rows, rows)

    def start_of(cols):
        row = lax.broadcasted_iota(jnp.int32, (rows, STEP), 0) + first_row
        col = lax.broadcasted_iota(jnp.int32, (rows, STEP), 1) + cols.start
        return jnp.where(row == col, 1.5, 0.0) - 0.5 * ratio * full[pl.ds(first_row, rows), cols].astype(jnp.float32)

    def finish(cols, value):
        out[:, cols] = value

    newton_chain(full, ratio, scale, start_of, second, third, finish)


LATE = BLK // 4 - CHUNKS[-1][2]


def last_start(low, core):
    return pl.multiple_of(((1 - low) * 2 + 1 - core) * (BLK // 4), TILE)


def left_kernel(inverse, w_own, w_core, *refs):
    chunks, (out, weights) = refs[:-2], refs[-2:]
    _, y, core, _, _ = place()
    low = y % 2
    rows = w_core.shape[0]
    pieces = [(w_own.at[:, pl.ds(pl.multiple_of(core * BLK, BLK), BLK)], (low * 2 + core) * rows), (w_core, (low * 2 + 1 - core) * rows)]
    for chunk, (other, start, _) in zip(chunks, CHUNKS):
        lane = 1 - core if other else core
        pieces.append((chunk, ((1 - low) * 2 + lane) * rows + start))
    weights[pl.ds(last_start(low, core) + LATE, CHUNKS[-1][2])] = jnp.zeros((CHUNKS[-1][2], BLK), jnp.bfloat16)
    for piece, there in pieces:
        weights[pl.ds(pl.multiple_of(there, 64), piece.shape[0])] = piece[...]
    for cols in steps():
        out[:, cols] = dot(inverse[...], weights[:, cols])


def right_kernel(
    first_own, first_got, second_own, second_got, part_left, inverse, chunk, theirs, mine, full, left, second, third, late
):
    x_hi, y, core, _, _ = place()
    code = x_hi * 4 + y
    rows = mine.shape[0]
    owns, gots = (first_own, second_own), (first_got, second_got)
    for tile, (i, j) in enumerate(UPPER):
        part, piece, at = slot_of(tile, code, WIDTH)
        index = (piece & 3) * (WIDTH, PIECE - WIDTH)[part] + at
        put(full, i, j, jnp.where(piece >= 4, gots[part][index], owns[part][index]))
    ratio, scale = scales(diagonal_sum(full))

    late[:LATE] = jnp.zeros((LATE, BLK), jnp.bfloat16)
    late[LATE:] = chunk[...]
    last = pl.ds(last_start(y % 2, core), BLK // 4)
    for cols in steps():
        left[:, cols] = (part_left[:, cols] + dot(inverse[:, last], late[:, cols])).astype(jnp.bfloat16)

    def start_of(cols):
        turned = dot(left[...], full[:, cols])
        return 1.5 * left[:, cols].astype(jnp.float32) - 0.5 * ratio * turned

    def finish(cols, value):
        theirs[:, cols] = jnp.where(core == 0, value[rows:], value[:rows])
        mine[:, cols] = jnp.where(core == 0, value[:rows], value[rows:])

    newton_chain(full, ratio, scale, start_of, second, third, finish)


def whole(memory):
    return pl.BlockSpec(memory_space=memory)


def tiles(count):
    return jax.ShapeDtypeStruct((count, TILE, TILE), jnp.bfloat16)


def matrix(rows, cols):
    return pltpu.VMEM((rows, cols), jnp.bfloat16)


def shaped(rows, cols):
    return jax.ShapeDtypeStruct((rows, cols), jnp.bfloat16)


def kernel(body, name, operands, in_specs, out_shape, out_specs, scratch, flops, moved, vmem):
    return pl.pallas_call(
        body,
        out_shape=out_shape,
        in_specs=[whole(space) for space in in_specs],
        out_specs=jax.tree.map(whole, out_specs),
        scratch_shapes=scratch,
        compiler_params=pltpu.CompilerParams(vmem_limit_bytes=vmem * MIB),
        cost_estimate=pl.CostEstimate(flops=flops, bytes_accessed=moved, transcendentals=0),
        name=name,
    )(*operands)


def on_device(activations, out_grads, weight_grad):
    rows = weight_grad.shape[0]
    core = lax.axis_index("dp") % 2
    other = (1 - core) * BLK
    n, m, a = WIDTH, PIECE - WIDTH, A_PIECE

    g_other = lax.dynamic_slice_in_dim(out_grads, other, BLK, 1)
    w_0 = lax.dynamic_slice_in_dim(weight_grad, core * BLK, BLK, 1)
    g_other, w_0, activations = together(g_other, w_0, activations)
    g_got = send(g_other, CORE, "g_tokens")
    w_0 = send(w_0, Y_NEAR, "w_0")
    a_sent, a_kept, w_1, w_2, w_3 = kernel(
        cov_a,
        "cov_a",
        (activations, weight_grad),
        [pltpu.HBM, pltpu.HBM],
        [tiles(4 * a)] * 2 + [shaped(count, BLK) for _, _, count in CHUNKS[1:]],
        [pltpu.VMEM] * 2 + [pl.ANY] * (len(CHUNKS) - 1),
        [pltpu.VMEM((4, activations.shape[0], BLK), jnp.bfloat16), pltpu.SemaphoreType.DMA((3 + len(CHUNKS),))],
        40 * 2 * 256 * TILE * TILE,
        5 << 20,
        16,
    )
    a_swapped = send(a_sent, CORE, "a_core")

    a_swapped, g_got = together(a_swapped, g_got)
    a_sum = add(a_kept, a_swapped)
    a_parts = [a_sum[at * a : (at + 1) * a] for at in range(4)]
    a_both = send(a_parts[3], X_Y_FAR, "a_sum_both")
    a_x = send(a_parts[2], X_HALF, "a_sum_x")
    a_y = send(a_parts[1], Y_FAR, "a_sum_y")
    a_parts = [a_parts[0], a_y, a_x, a_both]
    first_send, second_send, first_keep, second_keep = kernel(
        cov_g,
        "cov_g",
        (out_grads, g_got),
        [pltpu.VMEM] * 2,
        [tiles(4 * n), tiles(4 * m), tiles(4 * n), tiles(4 * m)],
        [pltpu.VMEM] * 4,
        [matrix(2 * out_grads.shape[0], BLK)],
        21 * 2 * 512 * 256 * 256,
        4 << 20,
        16,
    )

    first_send, second_send, w_1, *a_parts = together(first_send, second_send, w_1, *a_parts)
    a_quarter = add(*a_parts)
    first_got = send(first_send, X_HALF, "sum_1_x")
    second_got = send(second_send, Y_FAR, "sum_1_y")
    a_near = send(a_quarter, Y_NEAR, "a_near")
    w_1 = send(w_1, Y_NEAR_CORE, "w_1")

    first_got, second_got, a_near, w_0, w_1 = together(first_got, second_got, a_near, w_0, w_1)
    first_next = send(add(first_keep[2 * n :], first_got[2 * n :]), Y_FAR, "sum_2_y")
    second_next = send(add(second_keep[2 * m :], second_got[2 * m :]), Y_NEAR, "sum_2_near")
    a_own = add(a_quarter, a_near)
    a_pair = send(a_own, X_NEAR, "a_pair")
    first_sum = add(first_keep[: 2 * n], first_got[: 2 * n])
    second_sum = add(second_keep[: 2 * m], second_got[: 2 * m])

    first_next, second_next, a_pair = together(first_next, second_next, a_pair)
    first_sum = add(first_sum, first_next)
    second_sum = add(second_sum, second_next)
    second_last = send(second_sum, X_HALF, "sum_3_x")
    first_last = send(first_sum, Y_NEAR, "sum_3_near")
    a_own = jnp.concatenate([a_own, a_pair])
    a_below, a_above = send(a_own, Z_UP, "a_up"), send(a_own, Z_DOWN, "a_down")

    first_last, second_last, w_2 = together(first_last, second_last, w_2)
    first_own = add(first_sum, swapped(first_last))
    second_own = add(second_sum, swapped(second_last))
    first_got = send(first_own, Y_FAR, "back_4_y")
    second_got = send(second_own, Y_NEAR, "back_4_near")
    a_far = [send(a_below[:a], Z_UP, "a_up_2"), send(a_above[a:], Z_DOWN, "a_down_2")]
    a_parts = (a_own, a_above, *a_far, a_below)
    a_swapped = [send(part, CORE, "a_core_back") for part in a_parts]
    w_core = send(lax.dynamic_slice_in_dim(weight_grad, other, BLK, 1), CORE, "w_core")
    w_2 = send(w_2, Y_NEAR_CORE, "w_2")

    first_got, second_got, w_core, w_2, w_3, a_own = together(first_got, second_got, w_core, w_2, w_3, a_own)
    first_own = jnp.concatenate([first_own, first_got])
    second_own = jnp.concatenate([second_own, second_got])
    first_got = send(first_own, X_HALF, "back_5_x")
    second_got = send(second_own, Y_FAR, "back_5_y")
    w_3 = send(w_3, Y_NEAR_CORE, "w_3")
    a_parts = (a_own, *a_parts[1:], *a_swapped)

    inverse = kernel(
        inverse_kernel,
        "inverse",
        a_parts,
        [pltpu.VMEM] * 10,
        shaped(2 * rows, BLK),
        pltpu.VMEM,
        [pltpu.VMEM((SLOTS, TILE, TILE), jnp.bfloat16), matrix(BLK, BLK), matrix(2 * rows, BLK), matrix(2 * rows, BLK)],
        4 * 2 * rows * BLK * BLK,
        5 << 20,
        24,
    )
    left = kernel(
        left_kernel,
        "left",
        (inverse, weight_grad, w_core, w_0, w_1, w_2),
        [pltpu.VMEM] * 6,
        jax.ShapeDtypeStruct((2 * rows, BLK), jnp.float32),
        pltpu.VMEM,
        [matrix(BLK, BLK)],
        2 * 2 * rows * BLK * BLK,
        9 << 20,
        20,
    )
    theirs, mine = kernel(
        right_kernel,
        "right",
        (first_own, first_got, second_own, second_got, left, inverse, w_3),
        [pltpu.VMEM] * 7,
        [shaped(rows, BLK)] * 2,
        [pltpu.VMEM] * 2,
        [matrix(BLK, BLK)] + [matrix(2 * rows, BLK)] * 3 + [matrix(rows, BLK)],
        6 * 2 * rows * BLK * BLK,
        8 << 20,
        24,
    )
    theirs = send(theirs, CORE, "out_core")
    return jnp.where(core == 0, jnp.concatenate([mine, theirs], 1), jnp.concatenate([theirs, mine], 1))


def solution(mesh):
    return jax.shard_map(
        on_device,
        mesh=mesh,
        in_specs=(P("dp", None), P("dp", "tensor"), P("dp", "tensor")),
        out_specs=P("dp", "tensor"),
        check_vma=False,
    )
```

time: 582 us -> 121 us (0.21)
  waiting for transfers between devices: 435 us -> 35.8 us
  matrix products: 70.7 us -> 0 us
  other arithmetic: 47.7 us -> 2.77 us
  starting transfers between devices: 3.85 us -> 45.7 us
  Pallas kernels: 0 us -> 32.6 us
  between operations: 13.9 us -> 0.23 us
  local copies, waits for them, and re-layouts: 9.25 us -> 3.41 us
    psum x3 -> x0, waiting for transfers between devices: 420 us -> none  [the longest x1 181 us: on_device(): lax.psum(a_partial, 'dp').astype(jnp.float32)]
    dot_general x7 -> x0, matrix products: 70.7 us -> none  [the longest x2 36.8 us: newton_rows(): second = jnp.dot(product, first, preferred_element_type=jnp.float32)]
    ppermute x2 -> x32, starting transfers between devices: 3.76 us -> 45.7 us  [send(): return lax.ppermute(array, AXES, pairs)]
    pallas_call x0 -> x5, Pallas kernels: none -> 32.6 us  [kernel(): pl.pallas_call(body, out_shape=out_shape, in_specs=[whole(space) for spac...]
    ppermute x2 -> x32, waiting for transfers between devices: 15 us -> 35.8 us  [send(): return lax.ppermute(array, AXES, pairs)]
    another operation x2 -> x0, other arithmetic: 14.9 us -> none  [the longest x1 8.25 us: on_device(): jnp.stack([covar_block(out_grads, job * BLK) for job in range(g_blocks)])]
    div x1 -> x0, other arithmetic: 12.9 us -> none  [on_device(): g_total = g_total / token_total]
    reduce_sum x2 -> x0, other arithmetic: 7.64 us -> none  [damped_pair(): mean_diag = jnp.trace(covar) / BLK + 1e-06]
  transfers between devices with their start and end apart: 5 -> 32, of which waited for: 5 -> 16; matrix products, arithmetic and copies ran while one was open for 4% -> 1% of each run, Pallas kernels for 0% -> 16%
where the time goes in v2:
time: 121 us; the launch traced here: 120 us
  starting transfers between devices  45.7 us (38%)
  waiting for transfers between devices  35.8 us (30%)
  Pallas kernels  32.6 us (27%)
  local copies, waits for them, and re-layouts  3.41 us (3%)
  other arithmetic  2.77 us (2%)
    ppermute x32, starting transfers between devices, send(): return lax.ppermute(array, AXES, pairs)  45.7 us
    ppermute x32, waiting for transfers between devices, send(): return lax.ppermute(array, AXES, pairs)  35.8 us
    pallas_call x5, Pallas kernels, kernel(): pl.pallas_call(body, out_shape=out_shape, in_specs=[whole(space) for spac...  32.6 us
  transfers between devices with their start and end apart: 32, of which 16 were waited for; matrix products, arithmetic and copies ran while one was open for 1% of the time, Pallas kernels for 16%

profile of v2, /device:TPU:1, one launch (start us, length us, event | category | flops | bytes accessed | tf_op | source)
XLA Modules:
  0.0 120.5 jit_solution(1677403452199939312)
XLA Ops:
  1.4 1.9 %constant_dynamic-slice_fusion = (bf16[384,1536]{1,0:T(8,128)(2,1)S(1)}, bf16[384,1536]{1,0:T(8,128)(2,1)S(1)}) fusion(bf16[384,3072]{1,0:T(8,128)(2,1)} %w_own.1, s32[]{:T(128)S(6)} %select_n.24, s32[]{:T(128)S(6)} %select_n.25), kind=kLoop, calls=%fused_computation.15 | loop fusion | bytes 4718600 | tf_op jit(solution)/shard_map/dynamic_slice | solution.py:391
  3.3 1.5 %collective-permute-start.1 = (bf16[256,1536]{1,0:T(8,128)(2,1)S(1)}, bf16[256,1536]{1,0:T(8,128)(2,1)S(1)}, u32[]{:S(2)}, u32[]{:S(2)}) collective-permute-start(bf16[256,1536]{1,0:T(8,128)(2,1)S(1)} %constant_dynamic-slice_fusion.2), channel_id=1, source_target_pairs={{0,8},{1,9},{2,10},{3,11},{4,12},{5,13},{6,14},{7,15},{8,0},{9,1},... | collective-permute-start | bytes 2359304 | tf_op jit(solution)/shard_map/g_tokens/ppermute | solution.py:49
  4.8 2.1 %cov_a.1 = (bf16[20,128,128]{2,1,0:T(8,128)(2,1)S(1)}, bf16[20,128,128]{2,1,0:T(8,128)(2,1)S(1)}, bf16[64,1536]{1,0:T(8,128)(2,1)S(1)}, bf16[64,1536]{1,0:T(8,128)(2,1)S(1)}, bf16[256,1536]{1,0:T(8,128)(2,1)S(1)}) custom-call(bf16[256,6144]{1,0:T(8,128)(2,1)S(1)} %copy-done.1, bf16[384,3072]{1,0:T(8,128)(2,1)S(1)} %copy-done), custom_call_target="tpu_custom_call" | custom-call | flops 335544320 | bytes 5242880 | tf_op jit(solution)/shard_map/cov_a/pallas_call | solution.py:303
  7.5 1.4 %collective-permute-start.8 = (bf16[384,1536]{1,0:T(8,128)(2,1)S(1)}, bf16[384,1536]{1,0:T(8,128)(2,1)S(1)}, u32[]{:S(2)}, u32[]{:S(2)}) collective-permute-start(bf16[384,1536]{1,0:T(8,128)(2,1)S(1)} %get-tuple-element.61), channel_id=1, source_target_pairs={{0,16},{1,17},{2,18},{3,19},{4,20},{5,21},{6,22},{7,23},{8,24},{9,... | collective-permute-start | bytes 3538952 | tf_op jit(solution)/shard_map/w_0/ppermute | solution.py:49
  9.5 2.9 %collective-permute-start.2 = (bf16[5,128,128]{2,1,0:T(8,128)(2,1)S(1)}, bf16[5,128,128]{2,1,0:T(8,128)(2,1)S(1)}, u32[]{:S(2)}, u32[]{:S(2)}) collective-permute-start(bf16[5,128,128]{2,1,0:T(8,128)(2,1)S(1)} %get-tuple-element.89), channel_id=1, source_target_pairs={{0,48},{1,49},{2,50},{3,51},{4,52},{5,53},{6,54},{7,55},{8,56},{9,... | collective-permute-start | bytes 491528 | tf_op jit(solution)/shard_map/a_sum_y/ppermute | solution.py:49
  12.3 2.7 %collective-permute-start.3 = (bf16[5,128,128]{2,1,0:T(8,128)(2,1)S(1)}, bf16[5,128,128]{2,1,0:T(8,128)(2,1)S(1)}, u32[]{:S(2)}, u32[]{:S(2)}) collective-permute-start(bf16[5,128,128]{2,1,0:T(8,128)(2,1)S(1)} %get-tuple-element.88), channel_id=1, source_target_pairs={{0,64},{1,65},{2,66},{3,67},{4,68},{5,69},{6,70},{7,71},{8,72},{9,... | collective-permute-start | bytes 491528 | tf_op jit(solution)/shard_map/a_sum_x/ppermute | solution.py:49
  15.1 3.5 %cov_g.1 = (bf16[20,128,128]{2,1,0:T(8,128)(2,1)S(1)}, bf16[20,128,128]{2,1,0:T(8,128)(2,1)S(1)}, bf16[20,128,128]{2,1,0:T(8,128)(2,1)S(1)}, bf16[20,128,128]{2,1,0:T(8,128)(2,1)S(1)}) custom-call(bf16[256,3072]{1,0:T(8,128)(2,1)S(1)} %copy-done.2, bf16[256,1536]{1,0:T(8,128)(2,1)S(1)} %collective-permute-done.1.got), custom_call_target="tpu_custom_call" | custom-call | flops 1409286144 | bytes 4194304 | tf_op jit(solution)/shard_map/cov_g/pallas_call | solution.py:303
  18.9 4.5 %collective-permute-done.4 = bf16[5,128,128]{2,1,0:T(8,128)(2,1)S(1)} collective-permute-done((bf16[5,128,128]{2,1,0:T(8,128)(2,1)S(1)}, bf16[5,128,128]{2,1,0:T(8,128)(2,1)S(1)}, u32[]{:S(2)}, u32[]{:S(2)}) %collective-permute-start.4) | collective-permute-done | bytes 163872 | tf_op jit(solution)/shard_map/a_sum_both/ppermute | solution.py:49
  23.5 1.7 %collective-permute-start.5 = (bf16[20,128,128]{2,1,0:T(8,128)(2,1)S(1)}, bf16[20,128,128]{2,1,0:T(8,128)(2,1)S(1)}, u32[]{:S(2)}, u32[]{:S(2)}) collective-permute-start(bf16[20,128,128]{2,1,0:T(8,128)(2,1)S(1)} %get-tuple-element.55), channel_id=1, source_target_pairs={{0,64},{1,65},{2,66},{3,67},{4,68},{5,69},{6,70},{7,71},{8,72},{9,... | collective-permute-start | bytes 1966088 | tf_op jit(solution)/shard_map/sum_1_x/ppermute | solution.py:49
  25.2 2.4 %collective-permute-start.6 = (bf16[20,128,128]{2,1,0:T(8,128)(2,1)S(1)}, bf16[20,128,128]{2,1,0:T(8,128)(2,1)S(1)}, u32[]{:S(2)}, u32[]{:S(2)}) collective-permute-start(bf16[20,128,128]{2,1,0:T(8,128)(2,1)S(1)} %get-tuple-element.56), channel_id=1, source_target_pairs={{0,48},{1,49},{2,50},{3,51},{4,52},{5,53},{6,54},{7,55},{8,56},{9,... | collective-permute-start | bytes 1966088 | tf_op jit(solution)/shard_map/sum_1_y/ppermute | solution.py:49
  28.3 2.9 %collective-permute-start.7 = (bf16[5,128,128]{2,1,0:T(8,128)(2,1)S(1)}, bf16[5,128,128]{2,1,0:T(8,128)(2,1)S(1)}, u32[]{:S(2)}, u32[]{:S(2)}) collective-permute-start(bf16[5,128,128]{2,1,0:T(8,128)(2,1)S(1)} %add_convert_fusion.10), channel_id=1, source_target_pairs={{0,16},{1,17},{2,18},{3,19},{4,20},{5,21},{6,22},{7,23},{8,24},{9,... | collective-permute-start | bytes 491528 | tf_op jit(solution)/shard_map/a_near/ppermute | solution.py:49
  31.2 11.5 %collective-permute-done.7 = bf16[5,128,128]{2,1,0:T(8,128)(2,1)S(1)} collective-permute-done((bf16[5,128,128]{2,1,0:T(8,128)(2,1)S(1)}, bf16[5,128,128]{2,1,0:T(8,128)(2,1)S(1)}, u32[]{:S(2)}, u32[]{:S(2)}) %collective-permute-start.7) | collective-permute-done | bytes 163872 | tf_op jit(solution)/shard_map/a_near/ppermute | solution.py:49
  42.9 1.5 %collective-permute-start.11 = (bf16[10,128,128]{2,1,0:T(8,128)(2,1)S(1)}, bf16[10,128,128]{2,1,0:T(8,128)(2,1)S(1)}, u32[]{:S(2)}, u32[]{:S(2)}) collective-permute-start(bf16[10,128,128]{2,1,0:T(8,128)(2,1)S(1)} %add_convert_fusion.6), channel_id=1, source_target_pairs={{0,16},{1,17},{2,18},{3,19},{4,20},{5,21},{6,22},{7,23},{8,24},{9,... | collective-permute-start | bytes 983048 | tf_op jit(solution)/shard_map/sum_2_near/ppermute | solution.py:49
  44.4 2.0 %collective-permute-start.10 = (bf16[10,128,128]{2,1,0:T(8,128)(2,1)S(1)}, bf16[10,128,128]{2,1,0:T(8,128)(2,1)S(1)}, u32[]{:S(2)}, u32[]{:S(2)}) collective-permute-start(bf16[10,128,128]{2,1,0:T(8,128)(2,1)S(1)} %add_convert_fusion.7), channel_id=1, source_target_pairs={{0,48},{1,49},{2,50},{3,51},{4,52},{5,53},{6,54},{7,55},{8,56},{9,... | collective-permute-start | bytes 983048 | tf_op jit(solution)/shard_map/sum_2_y/ppermute | solution.py:49
  47.7 1.7 %collective-permute-start.17 = (bf16[384,1536]{1,0:T(8,128)(2,1)S(1)}, bf16[384,1536]{1,0:T(8,128)(2,1)S(1)}, u32[]{:S(2)}, u32[]{:S(2)}) collective-permute-start(bf16[384,1536]{1,0:T(8,128)(2,1)S(1)} %get-tuple-element.85), channel_id=1, source_target_pairs={{0,8},{1,9},{2,10},{3,11},{4,12},{5,13},{6,14},{7,15},{8,0},{9,1},... | collective-permute-start | bytes 3538952 | tf_op jit(solution)/shard_map/w_core/ppermute | solution.py:49
  49.5 1.5 %collective-permute-done.12 = bf16[5,128,128]{2,1,0:T(8,128)(2,1)S(1)} collective-permute-done((bf16[5,128,128]{2,1,0:T(8,128)(2,1)S(1)}, bf16[5,128,128]{2,1,0:T(8,128)(2,1)S(1)}, u32[]{:S(2)}, u32[]{:S(2)}) %collective-permute-start.12) | collective-permute-done | bytes 163872 | tf_op jit(solution)/shard_map/a_pair/ppermute | solution.py:49
  51.3 2.5 %collective-permute-done.10 = bf16[10,128,128]{2,1,0:T(8,128)(2,1)S(1)} collective-permute-done((bf16[10,128,128]{2,1,0:T(8,128)(2,1)S(1)}, bf16[10,128,128]{2,1,0:T(8,128)(2,1)S(1)}, u32[]{:S(2)}, u32[]{:S(2)}) %collective-permute-start.10) | collective-permute-done | bytes 327712 | tf_op jit(solution)/shard_map/sum_2_y/ppermute | solution.py:49
  53.9 2.8 %collective-permute-start.14 = (bf16[10,128,128]{2,1,0:T(8,128)(2,1)S(1)}, bf16[10,128,128]{2,1,0:T(8,128)(2,1)S(1)}, u32[]{:S(2)}, u32[]{:S(2)}) collective-permute-start(bf16[10,128,128]{2,1,0:T(8,128)(2,1)S(1)} %add_convert_fusion.3), channel_id=1, source_target_pairs={{0,64},{1,65},{2,66},{3,67},{4,68},{5,69},{6,70},{7,71},{8,72},{9,... | collective-permute-start | bytes 983048 | tf_op jit(solution)/shard_map/sum_3_x/ppermute | solution.py:49
  57.0 1.7 %collective-permute-start.22 = (bf16[10,128,128]{2,1,0:T(8,128)(2,1)S(1)}, bf16[10,128,128]{2,1,0:T(8,128)(2,1)S(1)}, u32[]{:S(2)}, u32[]{:S(2)}) collective-permute-start(bf16[10,128,128]{2,1,0:T(8,128)(2,1)S(1)} %pad_maximum_fusion.2.refs_0_), channel_id=1, source_target_pairs={{0,1},{1,2},{2,3},{3,0},{4,5},{5,6},{6,7},{7,4},{8,9},{9,10},{10,1... | collective-permute-start | bytes 983048 | tf_op jit(solution)/shard_map/a_up/ppermute | solution.py:49
  58.7 2.2 %collective-permute-start.21 = (bf16[10,128,128]{2,1,0:T(8,128)(2,1)S(1)}, bf16[10,128,128]{2,1,0:T(8,128)(2,1)S(1)}, u32[]{:S(2)}, u32[]{:S(2)}) collective-permute-start(bf16[10,128,128]{2,1,0:T(8,128)(2,1)S(1)} %pad_maximum_fusion.2.refs_0_), channel_id=1, source_target_pairs={{0,3},{1,0},{2,1},{3,2},{4,7},{5,4},{6,5},{7,6},{8,11},{9,8},{10,9... | collective-permute-start | bytes 983048 | tf_op jit(solution)/shard_map/a_down/ppermute | solution.py:49
  60.9 1.7 %collective-permute-done.14 = bf16[10,128,128]{2,1,0:T(8,128)(2,1)S(1)} collective-permute-done((bf16[10,128,128]{2,1,0:T(8,128)(2,1)S(1)}, bf16[10,128,128]{2,1,0:T(8,128)(2,1)S(1)}, u32[]{:S(2)}, u32[]{:S(2)}) %collective-permute-start.14) | collective-permute-done | bytes 327712 | tf_op jit(solution)/shard_map/sum_3_x/ppermute | solution.py:49
  64.4 1.9 %collective-permute-start.15 = (bf16[10,128,128]{2,1,0:T(8,128)(2,1)S(1)}, bf16[10,128,128]{2,1,0:T(8,128)(2,1)S(1)}, u32[]{:S(2)}, u32[]{:S(2)}) collective-permute-start(bf16[10,128,128]{2,1,0:T(8,128)(2,1)S(1)} %add_convert_fusion.2), channel_id=1, source_target_pairs={{0,48},{1,49},{2,50},{3,51},{4,52},{5,53},{6,54},{7,55},{8,56},{9,... | collective-permute-start | bytes 983048 | tf_op jit(solution)/shard_map/back_4_y/ppermute | solution.py:49
  66.5 4.3 %collective-permute-start.18 = (bf16[64,1536]{1,0:T(8,128)(2,1)S(1)}, bf16[64,1536]{1,0:T(8,128)(2,1)S(1)}, u32[]{:S(2)}, u32[]{:S(2)}) collective-permute-start(bf16[64,1536]{1,0:T(8,128)(2,1)S(1)} %get-tuple-element.72), channel_id=1, source_target_pairs={{0,24},{1,25},{2,26},{3,27},{4,28},{5,29},{6,30},{7,31},{8,16},{9,... | collective-permute-start | bytes 589832 | tf_op jit(solution)/shard_map/w_2/ppermute | solution.py:49
  70.8 1.6 %collective-permute-start.23 = (bf16[5,128,128]{2,1,0:T(8,128)(2,1)S(1)}, bf16[5,128,128]{2,1,0:T(8,128)(2,1)S(1)}, u32[]{:S(2)}, u32[]{:S(2)}) collective-permute-start(bf16[5,128,128]{2,1,0:T(8,128)(2,1)S(1)} %slice.76), channel_id=1, source_target_pairs={{0,1},{1,2},{2,3},{3,0},{4,5},{5,6},{6,7},{7,4},{8,9},{9,10},{10,1... | collective-permute-start | bytes 491528 | tf_op jit(solution)/shard_map/a_up_2/ppermute | solution.py:49
  72.4 2.2 %collective-permute-start.24 = (bf16[5,128,128]{2,1,0:T(8,128)(2,1)S(1)}, bf16[5,128,128]{2,1,0:T(8,128)(2,1)S(1)}, u32[]{:S(2)}, u32[]{:S(2)}) collective-permute-start(bf16[5,128,128]{2,1,0:T(8,128)(2,1)S(1)} %slice.77), channel_id=1, source_target_pairs={{0,3},{1,0},{2,1},{3,2},{4,7},{5,4},{6,5},{7,6},{8,11},{9,8},{10,9... | collective-permute-start | bytes 491528 | tf_op jit(solution)/shard_map/a_down_2/ppermute | solution.py:49
  74.7 3.8 %collective-permute-done.23.refs_2_ = bf16[5,128,128]{2,1,0:T(8,128)(2,1)S(1)} collective-permute-done((bf16[5,128,128]{2,1,0:T(8,128)(2,1)S(1)}, bf16[5,128,128]{2,1,0:T(8,128)(2,1)S(1)}, u32[]{:S(2)}, u32[]{:S(2)}) %collective-permute-start.23) | collective-permute-done | bytes 163872 | tf_op jit(solution)/shard_map/a_up_2/ppermute | solution.py:49
  83.5 9.2 %inverse.1 = bf16[768,1536]{1,0:T(8,128)(2,1)S(1)} custom-call(bf16[10,128,128]{2,1,0:T(8,128)(2,1)S(1)} %pad_maximum_fusion.2.refs_0_, bf16[10,128,128]{2,1,0:T(8,128)(2,1)S(1)} %collective-permute-done.21.refs_1_, bf16[5,128,128]{2,1,0:T(8,128)(2,1)S(1)} %collective-permute-done.23.refs_2_, bf16[5,128,128]{2,1,0:T(8,128)(2,1)S(1)} %collective-permute-done.24.refs_3_, ...), custom_call_target="tpu_custom_call" | custom-call | flops 7247757312 | bytes 5242880 | tf_op jit(solution)/shard_map/inverse/pallas_call | solution.py:303
  92.7 4.2 %left.1.part_left = f32[768,1536]{1,0:T(8,128)S(1)} custom-call(bf16[768,1536]{1,0:T(8,128)(2,1)S(1)} %inverse.1, bf16[384,3072]{1,0:T(8,128)(2,1)S(1)} %copy-done, bf16[384,1536]{1,0:T(8,128)(2,1)S(1)} %collective-permute-done.17.w_core, bf16[384,1536]{1,0:T(8,128)(2,1)S(1)} %collective-permute-done.8.refs_0_, ...), custom_call_target="tpu_custom_call" | custom-call | flops 3623878656 | bytes 9437184 | tf_op jit(solution)/shard_map/left/pallas_call | solution.py:303
  98.2 3.8 %collective-permute-done.30.chunk = bf16[256,1536]{1,0:T(8,128)(2,1)S(1)} collective-permute-done((bf16[256,1536]{1,0:T(8,128)(2,1)S(1)}, bf16[256,1536]{1,0:T(8,128)(2,1)S(1)}, u32[]{:S(2)}, u32[]{:S(2)}) %collective-permute-start.30) | collective-permute-done | bytes 786464 | tf_op jit(solution)/shard_map/w_3/ppermute | solution.py:49
  102.0 13.6 %right.1 = (bf16[384,1536]{1,0:T(8,128)(2,1)S(1)}, bf16[384,1536]{1,0:T(8,128)(2,1)S(1)}) custom-call(bf16[20,128,128]{2,1,0:T(8,128)(2,1)S(1)} %pad_maximum_fusion.first_own, bf16[20,128,128]{2,1,0:T(8,128)(2,1)S(1)} %collective-permute-done.19.first_got, bf16[20,128,128]{2,1,0:T(8,128)(2,1)S(1)} %pad_maximum_fusion.1.second_own, ...), custom_call_target="tpu_custom_call" | custom-call | flops 10871635968 | bytes 8388608 | tf_op jit(solution)/shard_map/right/pallas_call | solution.py:303
  116.3 2.5 %collective-permute-done.31 = bf16[384,1536]{1,0:T(8,128)(2,1)S(1)} collective-permute-done((bf16[384,1536]{1,0:T(8,128)(2,1)S(1)}, bf16[384,1536]{1,0:T(8,128)(2,1)S(1)}, u32[]{:S(2)}, u32[]{:S(2)}) %collective-permute-start.31) | collective-permute-done | bytes 1179680 | tf_op jit(solution)/shard_map/out_core/ppermute | solution.py:49
  118.8 1.7 %maximum_select_fusion = bf16[384,3072]{1,0:T(8,128)(2,1)} fusion(bf16[384,1536]{1,0:T(8,128)(2,1)S(1)} %collective-permute-done.31, bf16[384,1536]{1,0:T(8,128)(2,1)S(1)} %get-tuple-element.83, pred[]{:T(512)S(6)} %eq.5), kind=kLoop, calls=%fused_computation | loop fusion | flops 10616832 | bytes 4718593 | tf_op jit(solution)/shard_map/jit(_where)/select_n | solution.py:439
  (62 shorter events, 14.7 us)
Async XLA Ops:
  3.3 5.9 %collective-permute-start.1 = (bf16[256,1536]{1,0:T(8,128)(2,1)S(1)}, bf16[256,1536]{1,0:T(8,128)(2,1)S(1)}, u32[]{:S(2)}, u32[]{:S(2)}) collective-permute-start(bf16[256,1536]{1,0:T(8,128)(2,1)S(1)} %constant_dynamic-slice_fusion.2), channel_id=1, source_target_pairs={{0,8},{1,9},{2,10},{3,11},{4,12},{5,13},{6,14},{7,15},{8,0},{9,1},... | collective-permute-start | bytes 2359304 | tf_op jit(solution)/shard_map/g_tokens/ppermute | solution.py:49
  6.9 2.3 %collective-permute-start = (bf16[20,128,128]{2,1,0:T(8,128)(2,1)S(1)}, bf16[20,128,128]{2,1,0:T(8,128)(2,1)S(1)}, u32[]{:S(2)}, u32[]{:S(2)}) collective-permute-start(bf16[20,128,128]{2,1,0:T(8,128)(2,1)S(1)} %get-tuple-element.46), channel_id=1, source_target_pairs={{0,8},{1,9},{2,10},{3,11},{4,12},{5,13},{6,14},{7,15},{8,0},{9,1},... | collective-permute-start | bytes 1966088 | tf_op jit(solution)/shard_map/a_core/ppermute | solution.py:49
  7.5 35.3 %collective-permute-start.8 = (bf16[384,1536]{1,0:T(8,128)(2,1)S(1)}, bf16[384,1536]{1,0:T(8,128)(2,1)S(1)}, u32[]{:S(2)}, u32[]{:S(2)}) collective-permute-start(bf16[384,1536]{1,0:T(8,128)(2,1)S(1)} %get-tuple-element.61), channel_id=1, source_target_pairs={{0,16},{1,17},{2,18},{3,19},{4,20},{5,21},{6,22},{7,23},{8,24},{9,... | collective-permute-start | bytes 3538952 | tf_op jit(solution)/shard_map/w_0/ppermute | solution.py:49
  9.5 9.2 %collective-permute-start.2 = (bf16[5,128,128]{2,1,0:T(8,128)(2,1)S(1)}, bf16[5,128,128]{2,1,0:T(8,128)(2,1)S(1)}, u32[]{:S(2)}, u32[]{:S(2)}) collective-permute-start(bf16[5,128,128]{2,1,0:T(8,128)(2,1)S(1)} %get-tuple-element.89), channel_id=1, source_target_pairs={{0,48},{1,49},{2,50},{3,51},{4,52},{5,53},{6,54},{7,55},{8,56},{9,... | collective-permute-start | bytes 491528 | tf_op jit(solution)/shard_map/a_sum_y/ppermute | solution.py:49
  12.3 6.6 %collective-permute-start.3 = (bf16[5,128,128]{2,1,0:T(8,128)(2,1)S(1)}, bf16[5,128,128]{2,1,0:T(8,128)(2,1)S(1)}, u32[]{:S(2)}, u32[]{:S(2)}) collective-permute-start(bf16[5,128,128]{2,1,0:T(8,128)(2,1)S(1)} %get-tuple-element.88), channel_id=1, source_target_pairs={{0,64},{1,65},{2,66},{3,67},{4,68},{5,69},{6,70},{7,71},{8,72},{9,... | collective-permute-start | bytes 491528 | tf_op jit(solution)/shard_map/a_sum_x/ppermute | solution.py:49
  15.1 8.4 %collective-permute-start.4 = (bf16[5,128,128]{2,1,0:T(8,128)(2,1)S(1)}, bf16[5,128,128]{2,1,0:T(8,128)(2,1)S(1)}, u32[]{:S(2)}, u32[]{:S(2)}) collective-permute-start(bf16[5,128,128]{2,1,0:T(8,128)(2,1)S(1)} %get-tuple-element.87), channel_id=1, source_target_pairs={{0,112},{1,113},{2,114},{3,115},{4,116},{5,117},{6,118},{7,119},{8... | collective-permute-start | bytes 491528 | tf_op jit(solution)/shard_map/a_sum_both/ppermute | solution.py:49
  23.5 19.3 %collective-permute-start.5 = (bf16[20,128,128]{2,1,0:T(8,128)(2,1)S(1)}, bf16[20,128,128]{2,1,0:T(8,128)(2,1)S(1)}, u32[]{:S(2)}, u32[]{:S(2)}) collective-permute-start(bf16[20,128,128]{2,1,0:T(8,128)(2,1)S(1)} %get-tuple-element.55), channel_id=1, source_target_pairs={{0,64},{1,65},{2,66},{3,67},{4,68},{5,69},{6,70},{7,71},{8,72},{9,... | collective-permute-start | bytes 1966088 | tf_op jit(solution)/shard_map/sum_1_x/ppermute | solution.py:49
  25.2 17.6 %collective-permute-start.6 = (bf16[20,128,128]{2,1,0:T(8,128)(2,1)S(1)}, bf16[20,128,128]{2,1,0:T(8,128)(2,1)S(1)}, u32[]{:S(2)}, u32[]{:S(2)}) collective-permute-start(bf16[20,128,128]{2,1,0:T(8,128)(2,1)S(1)} %get-tuple-element.56), channel_id=1, source_target_pairs={{0,48},{1,49},{2,50},{3,51},{4,52},{5,53},{6,54},{7,55},{8,56},{9,... | collective-permute-start | bytes 1966088 | tf_op jit(solution)/shard_map/sum_1_y/ppermute | solution.py:49
  27.6 15.1 %collective-permute-start.9 = (bf16[64,1536]{1,0:T(8,128)(2,1)S(1)}, bf16[64,1536]{1,0:T(8,128)(2,1)S(1)}, u32[]{:S(2)}, u32[]{:S(2)}) collective-permute-start(bf16[64,1536]{1,0:T(8,128)(2,1)S(1)} %get-tuple-element.62), channel_id=1, source_target_pairs={{0,24},{1,25},{2,26},{3,27},{4,28},{5,29},{6,30},{7,31},{8,16},{9,... | collective-permute-start | bytes 589832 | tf_op jit(solution)/shard_map/w_1/ppermute | solution.py:49
  28.3 14.4 %collective-permute-start.7 = (bf16[5,128,128]{2,1,0:T(8,128)(2,1)S(1)}, bf16[5,128,128]{2,1,0:T(8,128)(2,1)S(1)}, u32[]{:S(2)}, u32[]{:S(2)}) collective-permute-start(bf16[5,128,128]{2,1,0:T(8,128)(2,1)S(1)} %add_convert_fusion.10), channel_id=1, source_target_pairs={{0,16},{1,17},{2,18},{3,19},{4,20},{5,21},{6,22},{7,23},{8,24},{9,... | collective-permute-start | bytes 491528 | tf_op jit(solution)/shard_map/a_near/ppermute | solution.py:49
  42.9 8.4 %collective-permute-start.11 = (bf16[10,128,128]{2,1,0:T(8,128)(2,1)S(1)}, bf16[10,128,128]{2,1,0:T(8,128)(2,1)S(1)}, u32[]{:S(2)}, u32[]{:S(2)}) collective-permute-start(bf16[10,128,128]{2,1,0:T(8,128)(2,1)S(1)} %add_convert_fusion.6), channel_id=1, source_target_pairs={{0,16},{1,17},{2,18},{3,19},{4,20},{5,21},{6,22},{7,23},{8,24},{9,... | collective-permute-start | bytes 983048 | tf_op jit(solution)/shard_map/sum_2_near/ppermute | solution.py:49
  44.4 9.3 %collective-permute-start.10 = (bf16[10,128,128]{2,1,0:T(8,128)(2,1)S(1)}, bf16[10,128,128]{2,1,0:T(8,128)(2,1)S(1)}, u32[]{:S(2)}, u32[]{:S(2)}) collective-permute-start(bf16[10,128,128]{2,1,0:T(8,128)(2,1)S(1)} %add_convert_fusion.7), channel_id=1, source_target_pairs={{0,48},{1,49},{2,50},{3,51},{4,52},{5,53},{6,54},{7,55},{8,56},{9,... | collective-permute-start | bytes 983048 | tf_op jit(solution)/shard_map/sum_2_y/ppermute | solution.py:49
  46.4 4.5 %collective-permute-start.12 = (bf16[5,128,128]{2,1,0:T(8,128)(2,1)S(1)}, bf16[5,128,128]{2,1,0:T(8,128)(2,1)S(1)}, u32[]{:S(2)}, u32[]{:S(2)}) collective-permute-start(bf16[5,128,128]{2,1,0:T(8,128)(2,1)S(1)} %add_convert_fusion.9), channel_id=1, source_target_pairs={{0,4},{1,5},{2,6},{3,7},{4,0},{5,1},{6,2},{7,3},{8,12},{9,13},{10,... | collective-permute-start | bytes 491528 | tf_op jit(solution)/shard_map/a_pair/ppermute | solution.py:49
  47.7 24.7 %collective-permute-start.17 = (bf16[384,1536]{1,0:T(8,128)(2,1)S(1)}, bf16[384,1536]{1,0:T(8,128)(2,1)S(1)}, u32[]{:S(2)}, u32[]{:S(2)}) collective-permute-start(bf16[384,1536]{1,0:T(8,128)(2,1)S(1)} %get-tuple-element.85), channel_id=1, source_target_pairs={{0,8},{1,9},{2,10},{3,11},{4,12},{5,13},{6,14},{7,15},{8,0},{9,1},... | collective-permute-start | bytes 3538952 | tf_op jit(solution)/shard_map/w_core/ppermute | solution.py:49
  53.9 8.7 %collective-permute-start.14 = (bf16[10,128,128]{2,1,0:T(8,128)(2,1)S(1)}, bf16[10,128,128]{2,1,0:T(8,128)(2,1)S(1)}, u32[]{:S(2)}, u32[]{:S(2)}) collective-permute-start(bf16[10,128,128]{2,1,0:T(8,128)(2,1)S(1)} %add_convert_fusion.3), channel_id=1, source_target_pairs={{0,64},{1,65},{2,66},{3,67},{4,68},{5,69},{6,70},{7,71},{8,72},{9,... | collective-permute-start | bytes 983048 | tf_op jit(solution)/shard_map/sum_3_x/ppermute | solution.py:49
  56.9 6.9 %collective-permute-start.13 = (bf16[10,128,128]{2,1,0:T(8,128)(2,1)S(1)}, bf16[10,128,128]{2,1,0:T(8,128)(2,1)S(1)}, u32[]{:S(2)}, u32[]{:S(2)}) collective-permute-start(bf16[10,128,128]{2,1,0:T(8,128)(2,1)S(1)} %add_convert_fusion.5), channel_id=1, source_target_pairs={{0,16},{1,17},{2,18},{3,19},{4,20},{5,21},{6,22},{7,23},{8,24},{9,... | collective-permute-start | bytes 983048 | tf_op jit(solution)/shard_map/sum_3_near/ppermute | solution.py:49
  57.0 9.5 %collective-permute-start.22 = (bf16[10,128,128]{2,1,0:T(8,128)(2,1)S(1)}, bf16[10,128,128]{2,1,0:T(8,128)(2,1)S(1)}, u32[]{:S(2)}, u32[]{:S(2)}) collective-permute-start(bf16[10,128,128]{2,1,0:T(8,128)(2,1)S(1)} %pad_maximum_fusion.2.refs_0_), channel_id=1, source_target_pairs={{0,1},{1,2},{2,3},{3,0},{4,5},{5,6},{6,7},{7,4},{8,9},{9,10},{10,1... | collective-permute-start | bytes 983048 | tf_op jit(solution)/shard_map/a_up/ppermute | solution.py:49
  58.7 12.1 %collective-permute-start.21 = (bf16[10,128,128]{2,1,0:T(8,128)(2,1)S(1)}, bf16[10,128,128]{2,1,0:T(8,128)(2,1)S(1)}, u32[]{:S(2)}, u32[]{:S(2)}) collective-permute-start(bf16[10,128,128]{2,1,0:T(8,128)(2,1)S(1)} %pad_maximum_fusion.2.refs_0_), channel_id=1, source_target_pairs={{0,3},{1,0},{2,1},{3,2},{4,7},{5,4},{6,5},{7,6},{8,11},{9,8},{10,9... | collective-permute-start | bytes 983048 | tf_op jit(solution)/shard_map/a_down/ppermute | solution.py:49
  63.9 15.2 %collective-permute-start.16 = (bf16[10,128,128]{2,1,0:T(8,128)(2,1)S(1)}, bf16[10,128,128]{2,1,0:T(8,128)(2,1)S(1)}, u32[]{:S(2)}, u32[]{:S(2)}) collective-permute-start(bf16[10,128,128]{2,1,0:T(8,128)(2,1)S(1)} %add_convert_fusion.1), channel_id=1, source_target_pairs={{0,16},{1,17},{2,18},{3,19},{4,20},{5,21},{6,22},{7,23},{8,24},{9,... | collective-permute-start | bytes 983048 | tf_op jit(solution)/shard_map/back_4_near/ppermute | solution.py:49
  64.4 15.1 %collective-permute-start.15 = (bf16[10,128,128]{2,1,0:T(8,128)(2,1)S(1)}, bf16[10,128,128]{2,1,0:T(8,128)(2,1)S(1)}, u32[]{:S(2)}, u32[]{:S(2)}) collective-permute-start(bf16[10,128,128]{2,1,0:T(8,128)(2,1)S(1)} %add_convert_fusion.2), channel_id=1, source_target_pairs={{0,48},{1,49},{2,50},{3,51},{4,52},{5,53},{6,54},{7,55},{8,56},{9,... | collective-permute-start | bytes 983048 | tf_op jit(solution)/shard_map/back_4_y/ppermute | solution.py:49
  66.5 12.5 %collective-permute-start.18 = (bf16[64,1536]{1,0:T(8,128)(2,1)S(1)}, bf16[64,1536]{1,0:T(8,128)(2,1)S(1)}, u32[]{:S(2)}, u32[]{:S(2)}) collective-permute-start(bf16[64,1536]{1,0:T(8,128)(2,1)S(1)} %get-tuple-element.72), channel_id=1, source_target_pairs={{0,24},{1,25},{2,26},{3,27},{4,28},{5,29},{6,30},{7,31},{8,16},{9,... | collective-permute-start | bytes 589832 | tf_op jit(solution)/shard_map/w_2/ppermute | solution.py:49
  70.8 7.6 %collective-permute-start.23 = (bf16[5,128,128]{2,1,0:T(8,128)(2,1)S(1)}, bf16[5,128,128]{2,1,0:T(8,128)(2,1)S(1)}, u32[]{:S(2)}, u32[]{:S(2)}) collective-permute-start(bf16[5,128,128]{2,1,0:T(8,128)(2,1)S(1)} %slice.76), channel_id=1, source_target_pairs={{0,1},{1,2},{2,3},{3,0},{4,5},{5,6},{6,7},{7,4},{8,9},{9,10},{10,1... | collective-permute-start | bytes 491528 | tf_op jit(solution)/shard_map/a_up_2/ppermute | solution.py:49
  72.4 6.2 %collective-permute-start.24 = (bf16[5,128,128]{2,1,0:T(8,128)(2,1)S(1)}, bf16[5,128,128]{2,1,0:T(8,128)(2,1)S(1)}, u32[]{:S(2)}, u32[]{:S(2)}) collective-permute-start(bf16[5,128,128]{2,1,0:T(8,128)(2,1)S(1)} %slice.77), channel_id=1, source_target_pairs={{0,3},{1,0},{2,1},{3,2},{4,7},{5,4},{6,5},{7,6},{8,11},{9,8},{10,9... | collective-permute-start | bytes 491528 | tf_op jit(solution)/shard_map/a_down_2/ppermute | solution.py:49
  78.4 1.6 %collective-permute-start.25 = (bf16[10,128,128]{2,1,0:T(8,128)(2,1)S(1)}, bf16[10,128,128]{2,1,0:T(8,128)(2,1)S(1)}, u32[]{:S(2)}, u32[]{:S(2)}) collective-permute-start(bf16[10,128,128]{2,1,0:T(8,128)(2,1)S(1)} %pad_maximum_fusion.2.refs_0_), channel_id=1, source_target_pairs={{0,8},{1,9},{2,10},{3,11},{4,12},{5,13},{6,14},{7,15},{8,0},{9,1},... | collective-permute-start | bytes 983048 | tf_op jit(solution)/shard_map/a_core_back/ppermute | solution.py:49
  78.6 2.2 %collective-permute-start.26 = (bf16[10,128,128]{2,1,0:T(8,128)(2,1)S(1)}, bf16[10,128,128]{2,1,0:T(8,128)(2,1)S(1)}, u32[]{:S(2)}, u32[]{:S(2)}) collective-permute-start(bf16[10,128,128]{2,1,0:T(8,128)(2,1)S(1)} %collective-permute-done.21.refs_1_), channel_id=1, source_target_pairs={{0,8},{1,9},{2,10},{3,11},{4,12},{5,13},{6,14},{7,15},{8,0},{9,1},... | collective-permute-start | bytes 983048 | tf_op jit(solution)/shard_map/a_core_back/ppermute | solution.py:49
  79.0 3.1 %collective-permute-start.29 = (bf16[10,128,128]{2,1,0:T(8,128)(2,1)S(1)}, bf16[10,128,128]{2,1,0:T(8,128)(2,1)S(1)}, u32[]{:S(2)}, u32[]{:S(2)}) collective-permute-start(bf16[10,128,128]{2,1,0:T(8,128)(2,1)S(1)} %collective-permute-done.22.refs_4_), channel_id=1, source_target_pairs={{0,8},{1,9},{2,10},{3,11},{4,12},{5,13},{6,14},{7,15},{8,0},{9,1},... | collective-permute-start | bytes 983048 | tf_op jit(solution)/shard_map/a_core_back/ppermute | solution.py:49
  79.2 4.3 %collective-permute-start.27 = (bf16[5,128,128]{2,1,0:T(8,128)(2,1)S(1)}, bf16[5,128,128]{2,1,0:T(8,128)(2,1)S(1)}, u32[]{:S(2)}, u32[]{:S(2)}) collective-permute-start(bf16[5,128,128]{2,1,0:T(8,128)(2,1)S(1)} %collective-permute-done.23.refs_2_), channel_id=1, source_target_pairs={{0,8},{1,9},{2,10},{3,11},{4,12},{5,13},{6,14},{7,15},{8,0},{9,1},... | collective-permute-start | bytes 491528 | tf_op jit(solution)/shard_map/a_core_back/ppermute | solution.py:49
  79.5 4.0 %collective-permute-start.28 = (bf16[5,128,128]{2,1,0:T(8,128)(2,1)S(1)}, bf16[5,128,128]{2,1,0:T(8,128)(2,1)S(1)}, u32[]{:S(2)}, u32[]{:S(2)}) collective-permute-start(bf16[5,128,128]{2,1,0:T(8,128)(2,1)S(1)} %collective-permute-done.24.refs_3_), channel_id=1, source_target_pairs={{0,8},{1,9},{2,10},{3,11},{4,12},{5,13},{6,14},{7,15},{8,0},{9,1},... | collective-permute-start | bytes 491528 | tf_op jit(solution)/shard_map/a_core_back/ppermute | solution.py:49
  80.1 17.4 %collective-permute-start.20 = (bf16[20,128,128]{2,1,0:T(8,128)(2,1)S(1)}, bf16[20,128,128]{2,1,0:T(8,128)(2,1)S(1)}, u32[]{:S(2)}, u32[]{:S(2)}) collective-permute-start(bf16[20,128,128]{2,1,0:T(8,128)(2,1)S(1)} %pad_maximum_fusion.1.second_own), channel_id=1, source_target_pairs={{0,48},{1,49},{2,50},{3,51},{4,52},{5,53},{6,54},{7,55},{8,56},{9,... | collective-permute-start | bytes 1966088 | tf_op jit(solution)/shard_map/back_5_y/ppermute | solution.py:49
  80.9 17.3 %collective-permute-start.19 = (bf16[20,128,128]{2,1,0:T(8,128)(2,1)S(1)}, bf16[20,128,128]{2,1,0:T(8,128)(2,1)S(1)}, u32[]{:S(2)}, u32[]{:S(2)}) collective-permute-start(bf16[20,128,128]{2,1,0:T(8,128)(2,1)S(1)} %pad_maximum_fusion.first_own), channel_id=1, source_target_pairs={{0,64},{1,65},{2,66},{3,67},{4,68},{5,69},{6,70},{7,71},{8,72},{9,... | collective-permute-start | bytes 1966088 | tf_op jit(solution)/shard_map/back_5_x/ppermute | solution.py:49
  82.1 19.9 %collective-permute-start.30 = (bf16[256,1536]{1,0:T(8,128)(2,1)S(1)}, bf16[256,1536]{1,0:T(8,128)(2,1)S(1)}, u32[]{:S(2)}, u32[]{:S(2)}) collective-permute-start(bf16[256,1536]{1,0:T(8,128)(2,1)S(1)} %get-tuple-element.82), channel_id=1, source_target_pairs={{0,24},{1,25},{2,26},{3,27},{4,28},{5,29},{6,30},{7,31},{8,16},{9,... | collective-permute-start | bytes 2359304 | tf_op jit(solution)/shard_map/w_3/ppermute | solution.py:49
  115.7 3.1 %collective-permute-start.31 = (bf16[384,1536]{1,0:T(8,128)(2,1)S(1)}, bf16[384,1536]{1,0:T(8,128)(2,1)S(1)}, u32[]{:S(2)}, u32[]{:S(2)}) collective-permute-start(bf16[384,1536]{1,0:T(8,128)(2,1)S(1)} %get-tuple-element.84), channel_id=1, source_target_pairs={{0,8},{1,9},{2,10},{3,11},{4,12},{5,13},{6,14},{7,15},{8,0},{9,1},... | collective-permute-start | bytes 3538952 | tf_op jit(solution)/shard_map/out_core/ppermute | solution.py:49
  (3 other events, 16.5 us)

commit v3 on v2

--- a/solution.py
+++ b/solution.py
@@ -230,11 +230,8 @@
     newton_chain(full, ratio, scale, start_of, second, third, finish)
 
 
-LATE = BLK // 4 - CHUNKS[-1][2]
-
-
 def last_start(low, core):
-    return pl.multiple_of(((1 - low) * 2 + 1 - core) * (BLK // 4), TILE)
+    return pl.multiple_of(((1 - low) * 2 + 1 - core) * (BLK // 4) + CHUNKS[-1][1], TILE)
 
 
 def left_kernel(inverse, w_own, w_core, *refs):
@@ -246,7 +243,7 @@
     for chunk, (other, start, _) in zip(chunks, CHUNKS):
         lane = 1 - core if other else core
         pieces.append((chunk, ((1 - low) * 2 + lane) * rows + start))
-    weights[pl.ds(last_start(low, core) + LATE, CHUNKS[-1][2])] = jnp.zeros((CHUNKS[-1][2], BLK), jnp.bfloat16)
+    weights[pl.ds(last_start(low, core), CHUNKS[-1][2])] = jnp.zeros((CHUNKS[-1][2], BLK), jnp.bfloat16)
     for piece, there in pieces:
         weights[pl.ds(pl.multiple_of(there, 64), piece.shape[0])] = piece[...]
     for cols in steps():
@@ -254,7 +251,7 @@
 
 
 def right_kernel(
-    first_own, first_got, second_own, second_got, part_left, inverse, chunk, theirs, mine, full, left, second, third, late
+    first_own, first_got, second_own, second_got, part_left, inverse, chunk, theirs, mine, full, left, second, third
 ):
     x_hi, y, core, _, _ = place()
     code = x_hi * 4 + y
@@ -266,11 +263,9 @@
         put(full, i, j, jnp.where(piece >= 4, gots[part][index], owns[part][index]))
     ratio, scale = scales(diagonal_sum(full))
 
-    late[:LATE] = jnp.zeros((LATE, BLK), jnp.bfloat16)
-    late[LATE:] = chunk[...]
-    last = pl.ds(last_start(y % 2, core), BLK // 4)
+    last = pl.ds(last_start(y % 2, core), CHUNKS[-1][2])
     for cols in steps():
-        left[:, cols] = (part_left[:, cols] + dot(inverse[:, last], late[:, cols])).astype(jnp.bfloat16)
+        left[:, cols] = (part_left[:, cols] + dot(inverse[:, last], chunk[:, cols])).astype(jnp.bfloat16)
 
     def start_of(cols):
         turned = dot(left[...], full[:, cols])
@@ -430,13 +425,15 @@
         [pltpu.VMEM] * 7,
         [shaped(rows, BLK)] * 2,
         [pltpu.VMEM] * 2,
-        [matrix(BLK, BLK)] + [matrix(2 * rows, BLK)] * 3 + [matrix(rows, BLK)],
+        [matrix(BLK, BLK)] + [matrix(2 * rows, BLK)] * 3,
         6 * 2 * rows * BLK * BLK,
         8 << 20,
         24,
     )
     theirs = send(theirs, CORE, "out_core")
-    return jnp.where(core == 0, jnp.concatenate([mine, theirs], 1), jnp.concatenate([theirs, mine], 1))
+    out = jnp.zeros((rows, 2 * BLK), jnp.bfloat16)
+    out = lax.dynamic_update_slice(out, mine, (0, core * BLK))
+    return lax.dynamic_update_slice(out, theirs, (0, other))
 
 
 def solution(mesh):

time: 121 us -> 119 us (0.983)
  other arithmetic: 2.77 us -> 1.09 us
  local copies, waits for them, and re-layouts: 3.41 us -> 4.91 us
    select_n x1 -> x0, other arithmetic: 1.68 us -> none  [on_device(): jnp.where(core == 0, jnp.concatenate([mine, theirs], 1), jnp.concatenate(...]
    dynamic_update_slice x0 -> x2, local copies, waits for them, and re-layouts: none -> 1.23 us  [the longest x1 1.09 us: on_device(): return lax.dynamic_update_slice(out, theirs, (0, other))]
where the time goes in v3:
time: 119 us
  starting transfers between devices  45.7 us (38%)
  waiting for transfers between devices  35.3 us (30%)
  Pallas kernels  31.9 us (27%)
  local copies, waits for them, and re-layouts  4.91 us (4%)
    ppermute x32, starting transfers between devices, send(): return lax.ppermute(array, AXES, pairs)  45.7 us
    ppermute x32, waiting for transfers between devices, send(): return lax.ppermute(array, AXES, pairs)  35.3 us
    pallas_call x5, Pallas kernels, kernel(): pl.pallas_call(body, out_shape=out_shape, in_specs=[whole(space) for spac...  31.9 us
  transfers between devices with their start and end apart: 32, of which 16 were waited for; matrix products, arithmetic and copies ran while one was open for 1% of the time, Pallas kernels for 16%

profile of v3, /device:TPU:1, one launch (start us, length us, event | category | flops | bytes accessed | tf_op | source)
XLA Modules:
  0.0 119.2 jit_solution(6700926833306649979)
XLA Ops:
  1.4 1.9 %constant_dynamic-slice_fusion = (bf16[384,1536]{1,0:T(8,128)(2,1)S(1)}, bf16[384,1536]{1,0:T(8,128)(2,1)S(1)}) fusion(bf16[384,3072]{1,0:T(8,128)(2,1)} %w_own.1, s32[]{:T(128)S(6)} %select_n.17, s32[]{:T(128)S(6)} %select_n.18), kind=kLoop, calls=%fused_computation.16 | loop fusion | bytes 4718600 | tf_op jit(solution)/shard_map/dynamic_slice | solution.py:386
  3.3 1.5 %collective-permute-start.1 = (bf16[256,1536]{1,0:T(8,128)(2,1)S(1)}, bf16[256,1536]{1,0:T(8,128)(2,1)S(1)}, u32[]{:S(2)}, u32[]{:S(2)}) collective-permute-start(bf16[256,1536]{1,0:T(8,128)(2,1)S(1)} %constant_dynamic-slice_fusion.2), channel_id=1, source_target_pairs={{0,8},{1,9},{2,10},{3,11},{4,12},{5,13},{6,14},{7,15},{8,0},{9,1},... | collective-permute-start | bytes 2359304 | tf_op jit(solution)/shard_map/g_tokens/ppermute | solution.py:49
  4.8 2.1 %cov_a.1 = (bf16[20,128,128]{2,1,0:T(8,128)(2,1)S(1)}, bf16[20,128,128]{2,1,0:T(8,128)(2,1)S(1)}, bf16[64,1536]{1,0:T(8,128)(2,1)S(1)}, bf16[64,1536]{1,0:T(8,128)(2,1)S(1)}, bf16[256,1536]{1,0:T(8,128)(2,1)S(1)}) custom-call(bf16[256,6144]{1,0:T(8,128)(2,1)S(1)} %copy-done.1, bf16[384,3072]{1,0:T(8,128)(2,1)S(1)} %copy-done), custom_call_target="tpu_custom_call" | custom-call | flops 335544320 | bytes 5242880 | tf_op jit(solution)/shard_map/cov_a/pallas_call | solution.py:298
  7.5 1.4 %collective-permute-start.8 = (bf16[384,1536]{1,0:T(8,128)(2,1)S(1)}, bf16[384,1536]{1,0:T(8,128)(2,1)S(1)}, u32[]{:S(2)}, u32[]{:S(2)}) collective-permute-start(bf16[384,1536]{1,0:T(8,128)(2,1)S(1)} %get-tuple-element.61), channel_id=1, source_target_pairs={{0,16},{1,17},{2,18},{3,19},{4,20},{5,21},{6,22},{7,23},{8,24},{9,... | collective-permute-start | bytes 3538952 | tf_op jit(solution)/shard_map/w_0/ppermute | solution.py:49
  9.4 2.9 %collective-permute-start.2 = (bf16[5,128,128]{2,1,0:T(8,128)(2,1)S(1)}, bf16[5,128,128]{2,1,0:T(8,128)(2,1)S(1)}, u32[]{:S(2)}, u32[]{:S(2)}) collective-permute-start(bf16[5,128,128]{2,1,0:T(8,128)(2,1)S(1)} %get-tuple-element.89), channel_id=1, source_target_pairs={{0,48},{1,49},{2,50},{3,51},{4,52},{5,53},{6,54},{7,55},{8,56},{9,... | collective-permute-start | bytes 491528 | tf_op jit(solution)/shard_map/a_sum_y/ppermute | solution.py:49
  12.3 2.7 %collective-permute-start.3 = (bf16[5,128,128]{2,1,0:T(8,128)(2,1)S(1)}, bf16[5,128,128]{2,1,0:T(8,128)(2,1)S(1)}, u32[]{:S(2)}, u32[]{:S(2)}) collective-permute-start(bf16[5,128,128]{2,1,0:T(8,128)(2,1)S(1)} %get-tuple-element.88), channel_id=1, source_target_pairs={{0,64},{1,65},{2,66},{3,67},{4,68},{5,69},{6,70},{7,71},{8,72},{9,... | collective-permute-start | bytes 491528 | tf_op jit(solution)/shard_map/a_sum_x/ppermute | solution.py:49
  15.1 3.5 %cov_g.1 = (bf16[20,128,128]{2,1,0:T(8,128)(2,1)S(1)}, bf16[20,128,128]{2,1,0:T(8,128)(2,1)S(1)}, bf16[20,128,128]{2,1,0:T(8,128)(2,1)S(1)}, bf16[20,128,128]{2,1,0:T(8,128)(2,1)S(1)}) custom-call(bf16[256,3072]{1,0:T(8,128)(2,1)S(1)} %copy-done.2, bf16[256,1536]{1,0:T(8,128)(2,1)S(1)} %collective-permute-done.1.got), custom_call_target="tpu_custom_call" | custom-call | flops 1409286144 | bytes 4194304 | tf_op jit(solution)/shard_map/cov_g/pallas_call | solution.py:298
  18.9 4.5 %collective-permute-done.4 = bf16[5,128,128]{2,1,0:T(8,128)(2,1)S(1)} collective-permute-done((bf16[5,128,128]{2,1,0:T(8,128)(2,1)S(1)}, bf16[5,128,128]{2,1,0:T(8,128)(2,1)S(1)}, u32[]{:S(2)}, u32[]{:S(2)}) %collective-permute-start.4) | collective-permute-done | bytes 163872 | tf_op jit(solution)/shard_map/a_sum_both/ppermute | solution.py:49
  23.5 1.7 %collective-permute-start.5 = (bf16[20,128,128]{2,1,0:T(8,128)(2,1)S(1)}, bf16[20,128,128]{2,1,0:T(8,128)(2,1)S(1)}, u32[]{:S(2)}, u32[]{:S(2)}) collective-permute-start(bf16[20,128,128]{2,1,0:T(8,128)(2,1)S(1)} %get-tuple-element.55), channel_id=1, source_target_pairs={{0,64},{1,65},{2,66},{3,67},{4,68},{5,69},{6,70},{7,71},{8,72},{9,... | collective-permute-start | bytes 1966088 | tf_op jit(solution)/shard_map/sum_1_x/ppermute | solution.py:49
  25.2 2.4 %collective-permute-start.6 = (bf16[20,128,128]{2,1,0:T(8,128)(2,1)S(1)}, bf16[20,128,128]{2,1,0:T(8,128)(2,1)S(1)}, u32[]{:S(2)}, u32[]{:S(2)}) collective-permute-start(bf16[20,128,128]{2,1,0:T(8,128)(2,1)S(1)} %get-tuple-element.56), channel_id=1, source_target_pairs={{0,48},{1,49},{2,50},{3,51},{4,52},{5,53},{6,54},{7,55},{8,56},{9,... | collective-permute-start | bytes 1966088 | tf_op jit(solution)/shard_map/sum_1_y/ppermute | solution.py:49
  28.3 2.9 %collective-permute-start.7 = (bf16[5,128,128]{2,1,0:T(8,128)(2,1)S(1)}, bf16[5,128,128]{2,1,0:T(8,128)(2,1)S(1)}, u32[]{:S(2)}, u32[]{:S(2)}) collective-permute-start(bf16[5,128,128]{2,1,0:T(8,128)(2,1)S(1)} %add_convert_fusion.10), channel_id=1, source_target_pairs={{0,16},{1,17},{2,18},{3,19},{4,20},{5,21},{6,22},{7,23},{8,24},{9,... | collective-permute-start | bytes 491528 | tf_op jit(solution)/shard_map/a_near/ppermute | solution.py:49
  31.2 11.5 %collective-permute-done.7 = bf16[5,128,128]{2,1,0:T(8,128)(2,1)S(1)} collective-permute-done((bf16[5,128,128]{2,1,0:T(8,128)(2,1)S(1)}, bf16[5,128,128]{2,1,0:T(8,128)(2,1)S(1)}, u32[]{:S(2)}, u32[]{:S(2)}) %collective-permute-start.7) | collective-permute-done | bytes 163872 | tf_op jit(solution)/shard_map/a_near/ppermute | solution.py:49
  42.8 1.5 %collective-permute-start.11 = (bf16[10,128,128]{2,1,0:T(8,128)(2,1)S(1)}, bf16[10,128,128]{2,1,0:T(8,128)(2,1)S(1)}, u32[]{:S(2)}, u32[]{:S(2)}) collective-permute-start(bf16[10,128,128]{2,1,0:T(8,128)(2,1)S(1)} %add_convert_fusion.6), channel_id=1, source_target_pairs={{0,16},{1,17},{2,18},{3,19},{4,20},{5,21},{6,22},{7,23},{8,24},{9,... | collective-permute-start | bytes 983048 | tf_op jit(solution)/shard_map/sum_2_near/ppermute | solution.py:49
  44.4 2.0 %collective-permute-start.10 = (bf16[10,128,128]{2,1,0:T(8,128)(2,1)S(1)}, bf16[10,128,128]{2,1,0:T(8,128)(2,1)S(1)}, u32[]{:S(2)}, u32[]{:S(2)}) collective-permute-start(bf16[10,128,128]{2,1,0:T(8,128)(2,1)S(1)} %add_convert_fusion.7), channel_id=1, source_target_pairs={{0,48},{1,49},{2,50},{3,51},{4,52},{5,53},{6,54},{7,55},{8,56},{9,... | collective-permute-start | bytes 983048 | tf_op jit(solution)/shard_map/sum_2_y/ppermute | solution.py:49
  47.7 1.7 %collective-permute-start.17 = (bf16[384,1536]{1,0:T(8,128)(2,1)S(1)}, bf16[384,1536]{1,0:T(8,128)(2,1)S(1)}, u32[]{:S(2)}, u32[]{:S(2)}) collective-permute-start(bf16[384,1536]{1,0:T(8,128)(2,1)S(1)} %get-tuple-element.85), channel_id=1, source_target_pairs={{0,8},{1,9},{2,10},{3,11},{4,12},{5,13},{6,14},{7,15},{8,0},{9,1},... | collective-permute-start | bytes 3538952 | tf_op jit(solution)/shard_map/w_core/ppermute | solution.py:49
  49.4 1.5 %collective-permute-done.12 = bf16[5,128,128]{2,1,0:T(8,128)(2,1)S(1)} collective-permute-done((bf16[5,128,128]{2,1,0:T(8,128)(2,1)S(1)}, bf16[5,128,128]{2,1,0:T(8,128)(2,1)S(1)}, u32[]{:S(2)}, u32[]{:S(2)}) %collective-permute-start.12) | collective-permute-done | bytes 163872 | tf_op jit(solution)/shard_map/a_pair/ppermute | solution.py:49
  51.3 2.5 %collective-permute-done.10 = bf16[10,128,128]{2,1,0:T(8,128)(2,1)S(1)} collective-permute-done((bf16[10,128,128]{2,1,0:T(8,128)(2,1)S(1)}, bf16[10,128,128]{2,1,0:T(8,128)(2,1)S(1)}, u32[]{:S(2)}, u32[]{:S(2)}) %collective-permute-start.10) | collective-permute-done | bytes 327712 | tf_op jit(solution)/shard_map/sum_2_y/ppermute | solution.py:49
  53.9 2.8 %collective-permute-start.14 = (bf16[10,128,128]{2,1,0:T(8,128)(2,1)S(1)}, bf16[10,128,128]{2,1,0:T(8,128)(2,1)S(1)}, u32[]{:S(2)}, u32[]{:S(2)}) collective-permute-start(bf16[10,128,128]{2,1,0:T(8,128)(2,1)S(1)} %add_convert_fusion.3), channel_id=1, source_target_pairs={{0,64},{1,65},{2,66},{3,67},{4,68},{5,69},{6,70},{7,71},{8,72},{9,... | collective-permute-start | bytes 983048 | tf_op jit(solution)/shard_map/sum_3_x/ppermute | solution.py:49
  57.0 1.7 %collective-permute-start.22 = (bf16[10,128,128]{2,1,0:T(8,128)(2,1)S(1)}, bf16[10,128,128]{2,1,0:T(8,128)(2,1)S(1)}, u32[]{:S(2)}, u32[]{:S(2)}) collective-permute-start(bf16[10,128,128]{2,1,0:T(8,128)(2,1)S(1)} %pad_maximum_fusion.2.refs_0_), channel_id=1, source_target_pairs={{0,1},{1,2},{2,3},{3,0},{4,5},{5,6},{6,7},{7,4},{8,9},{9,10},{10,1... | collective-permute-start | bytes 983048 | tf_op jit(solution)/shard_map/a_up/ppermute | solution.py:49
  58.7 2.2 %collective-permute-start.21 = (bf16[10,128,128]{2,1,0:T(8,128)(2,1)S(1)}, bf16[10,128,128]{2,1,0:T(8,128)(2,1)S(1)}, u32[]{:S(2)}, u32[]{:S(2)}) collective-permute-start(bf16[10,128,128]{2,1,0:T(8,128)(2,1)S(1)} %pad_maximum_fusion.2.refs_0_), channel_id=1, source_target_pairs={{0,3},{1,0},{2,1},{3,2},{4,7},{5,4},{6,5},{7,6},{8,11},{9,8},{10,9... | collective-permute-start | bytes 983048 | tf_op jit(solution)/shard_map/a_down/ppermute | solution.py:49
  60.9 1.7 %collective-permute-done.14 = bf16[10,128,128]{2,1,0:T(8,128)(2,1)S(1)} collective-permute-done((bf16[10,128,128]{2,1,0:T(8,128)(2,1)S(1)}, bf16[10,128,128]{2,1,0:T(8,128)(2,1)S(1)}, u32[]{:S(2)}, u32[]{:S(2)}) %collective-permute-start.14) | collective-permute-done | bytes 327712 | tf_op jit(solution)/shard_map/sum_3_x/ppermute | solution.py:49
  64.4 1.9 %collective-permute-start.15 = (bf16[10,128,128]{2,1,0:T(8,128)(2,1)S(1)}, bf16[10,128,128]{2,1,0:T(8,128)(2,1)S(1)}, u32[]{:S(2)}, u32[]{:S(2)}) collective-permute-start(bf16[10,128,128]{2,1,0:T(8,128)(2,1)S(1)} %add_convert_fusion.2), channel_id=1, source_target_pairs={{0,48},{1,49},{2,50},{3,51},{4,52},{5,53},{6,54},{7,55},{8,56},{9,... | collective-permute-start | bytes 983048 | tf_op jit(solution)/shard_map/back_4_y/ppermute | solution.py:49
  66.5 4.3 %collective-permute-start.18 = (bf16[64,1536]{1,0:T(8,128)(2,1)S(1)}, bf16[64,1536]{1,0:T(8,128)(2,1)S(1)}, u32[]{:S(2)}, u32[]{:S(2)}) collective-permute-start(bf16[64,1536]{1,0:T(8,128)(2,1)S(1)} %get-tuple-element.72), channel_id=1, source_target_pairs={{0,24},{1,25},{2,26},{3,27},{4,28},{5,29},{6,30},{7,31},{8,16},{9,... | collective-permute-start | bytes 589832 | tf_op jit(solution)/shard_map/w_2/ppermute | solution.py:49
  70.8 1.6 %collective-permute-start.23 = (bf16[5,128,128]{2,1,0:T(8,128)(2,1)S(1)}, bf16[5,128,128]{2,1,0:T(8,128)(2,1)S(1)}, u32[]{:S(2)}, u32[]{:S(2)}) collective-permute-start(bf16[5,128,128]{2,1,0:T(8,128)(2,1)S(1)} %slice.76), channel_id=1, source_target_pairs={{0,1},{1,2},{2,3},{3,0},{4,5},{5,6},{6,7},{7,4},{8,9},{9,10},{10,1... | collective-permute-start | bytes 491528 | tf_op jit(solution)/shard_map/a_up_2/ppermute | solution.py:49
  72.4 2.2 %collective-permute-start.24 = (bf16[5,128,128]{2,1,0:T(8,128)(2,1)S(1)}, bf16[5,128,128]{2,1,0:T(8,128)(2,1)S(1)}, u32[]{:S(2)}, u32[]{:S(2)}) collective-permute-start(bf16[5,128,128]{2,1,0:T(8,128)(2,1)S(1)} %slice.77), channel_id=1, source_target_pairs={{0,3},{1,0},{2,1},{3,2},{4,7},{5,4},{6,5},{7,6},{8,11},{9,8},{10,9... | collective-permute-start | bytes 491528 | tf_op jit(solution)/shard_map/a_down_2/ppermute | solution.py:49
  74.6 3.8 %collective-permute-done.23.refs_2_ = bf16[5,128,128]{2,1,0:T(8,128)(2,1)S(1)} collective-permute-done((bf16[5,128,128]{2,1,0:T(8,128)(2,1)S(1)}, bf16[5,128,128]{2,1,0:T(8,128)(2,1)S(1)}, u32[]{:S(2)}, u32[]{:S(2)}) %collective-permute-start.23) | collective-permute-done | bytes 163872 | tf_op jit(solution)/shard_map/a_up_2/ppermute | solution.py:49
  82.1 1.4 %collective-permute-start.30 = (bf16[256,1536]{1,0:T(8,128)(2,1)S(1)}, bf16[256,1536]{1,0:T(8,128)(2,1)S(1)}, u32[]{:S(2)}, u32[]{:S(2)}) collective-permute-start(bf16[256,1536]{1,0:T(8,128)(2,1)S(1)} %get-tuple-element.82), channel_id=1, source_target_pairs={{0,24},{1,25},{2,26},{3,27},{4,28},{5,29},{6,30},{7,31},{8,16},{9,... | collective-permute-start | bytes 2359304 | tf_op jit(solution)/shard_map/w_3/ppermute | solution.py:49
  83.4 9.2 %inverse.1 = bf16[768,1536]{1,0:T(8,128)(2,1)S(1)} custom-call(bf16[10,128,128]{2,1,0:T(8,128)(2,1)S(1)} %pad_maximum_fusion.2.refs_0_, bf16[10,128,128]{2,1,0:T(8,128)(2,1)S(1)} %collective-permute-done.21.refs_1_, bf16[5,128,128]{2,1,0:T(8,128)(2,1)S(1)} %collective-permute-done.23.refs_2_, bf16[5,128,128]{2,1,0:T(8,128)(2,1)S(1)} %collective-permute-done.24.refs_3_, ...), custom_call_target="tpu_custom_call" | custom-call | flops 7247757312 | bytes 5242880 | tf_op jit(solution)/shard_map/inverse/pallas_call | solution.py:298
  92.7 4.2 %left.1.part_left = f32[768,1536]{1,0:T(8,128)S(1)} custom-call(bf16[768,1536]{1,0:T(8,128)(2,1)S(1)} %inverse.1, bf16[384,3072]{1,0:T(8,128)(2,1)S(1)} %copy-done, bf16[384,1536]{1,0:T(8,128)(2,1)S(1)} %collective-permute-done.17.w_core, bf16[384,1536]{1,0:T(8,128)(2,1)S(1)} %collective-permute-done.8.refs_0_, ...), custom_call_target="tpu_custom_call" | custom-call | flops 3623878656 | bytes 9437184 | tf_op jit(solution)/shard_map/left/pallas_call | solution.py:298
  98.2 3.8 %collective-permute-done.30.chunk = bf16[256,1536]{1,0:T(8,128)(2,1)S(1)} collective-permute-done((bf16[256,1536]{1,0:T(8,128)(2,1)S(1)}, bf16[256,1536]{1,0:T(8,128)(2,1)S(1)}, u32[]{:S(2)}, u32[]{:S(2)}) %collective-permute-start.30) | collective-permute-done | bytes 786464 | tf_op jit(solution)/shard_map/w_3/ppermute | solution.py:49
  102.0 13.0 %right.1 = (bf16[384,1536]{1,0:T(8,128)(2,1)S(1)}, bf16[384,1536]{1,0:T(8,128)(2,1)S(1)}) custom-call(bf16[20,128,128]{2,1,0:T(8,128)(2,1)S(1)} %pad_maximum_fusion.first_own, bf16[20,128,128]{2,1,0:T(8,128)(2,1)S(1)} %collective-permute-done.19.first_got, bf16[20,128,128]{2,1,0:T(8,128)(2,1)S(1)} %pad_maximum_fusion.1.second_own, ...), custom_call_target="tpu_custom_call" | custom-call | flops 10871635968 | bytes 8388608 | tf_op jit(solution)/shard_map/right/pallas_call | solution.py:298
  116.1 2.0 %collective-permute-done.31 = bf16[384,1536]{1,0:T(8,128)(2,1)S(1)} collective-permute-done((bf16[384,1536]{1,0:T(8,128)(2,1)S(1)}, bf16[384,1536]{1,0:T(8,128)(2,1)S(1)}, u32[]{:S(2)}, u32[]{:S(2)}) %collective-permute-start.31) | collective-permute-done | bytes 1179680 | tf_op jit(solution)/shard_map/out_core/ppermute | solution.py:49
  (66 shorter events, 14.9 us)
Async XLA Ops:
  3.3 5.9 %collective-permute-start.1 = (bf16[256,1536]{1,0:T(8,128)(2,1)S(1)}, bf16[256,1536]{1,0:T(8,128)(2,1)S(1)}, u32[]{:S(2)}, u32[]{:S(2)}) collective-permute-start(bf16[256,1536]{1,0:T(8,128)(2,1)S(1)} %constant_dynamic-slice_fusion.2), channel_id=1, source_target_pairs={{0,8},{1,9},{2,10},{3,11},{4,12},{5,13},{6,14},{7,15},{8,0},{9,1},... | collective-permute-start | bytes 2359304 | tf_op jit(solution)/shard_map/g_tokens/ppermute | solution.py:49
  6.9 2.3 %collective-permute-start = (bf16[20,128,128]{2,1,0:T(8,128)(2,1)S(1)}, bf16[20,128,128]{2,1,0:T(8,128)(2,1)S(1)}, u32[]{:S(2)}, u32[]{:S(2)}) collective-permute-start(bf16[20,128,128]{2,1,0:T(8,128)(2,1)S(1)} %get-tuple-element.46), channel_id=1, source_target_pairs={{0,8},{1,9},{2,10},{3,11},{4,12},{5,13},{6,14},{7,15},{8,0},{9,1},... | collective-permute-start | bytes 1966088 | tf_op jit(solution)/shard_map/a_core/ppermute | solution.py:49
  7.5 35.3 %collective-permute-start.8 = (bf16[384,1536]{1,0:T(8,128)(2,1)S(1)}, bf16[384,1536]{1,0:T(8,128)(2,1)S(1)}, u32[]{:S(2)}, u32[]{:S(2)}) collective-permute-start(bf16[384,1536]{1,0:T(8,128)(2,1)S(1)} %get-tuple-element.61), channel_id=1, source_target_pairs={{0,16},{1,17},{2,18},{3,19},{4,20},{5,21},{6,22},{7,23},{8,24},{9,... | collective-permute-start | bytes 3538952 | tf_op jit(solution)/shard_map/w_0/ppermute | solution.py:49
  9.4 9.2 %collective-permute-start.2 = (bf16[5,128,128]{2,1,0:T(8,128)(2,1)S(1)}, bf16[5,128,128]{2,1,0:T(8,128)(2,1)S(1)}, u32[]{:S(2)}, u32[]{:S(2)}) collective-permute-start(bf16[5,128,128]{2,1,0:T(8,128)(2,1)S(1)} %get-tuple-element.89), channel_id=1, source_target_pairs={{0,48},{1,49},{2,50},{3,51},{4,52},{5,53},{6,54},{7,55},{8,56},{9,... | collective-permute-start | bytes 491528 | tf_op jit(solution)/shard_map/a_sum_y/ppermute | solution.py:49
  12.3 6.6 %collective-permute-start.3 = (bf16[5,128,128]{2,1,0:T(8,128)(2,1)S(1)}, bf16[5,128,128]{2,1,0:T(8,128)(2,1)S(1)}, u32[]{:S(2)}, u32[]{:S(2)}) collective-permute-start(bf16[5,128,128]{2,1,0:T(8,128)(2,1)S(1)} %get-tuple-element.88), channel_id=1, source_target_pairs={{0,64},{1,65},{2,66},{3,67},{4,68},{5,69},{6,70},{7,71},{8,72},{9,... | collective-permute-start | bytes 491528 | tf_op jit(solution)/shard_map/a_sum_x/ppermute | solution.py:49
  15.1 8.4 %collective-permute-start.4 = (bf16[5,128,128]{2,1,0:T(8,128)(2,1)S(1)}, bf16[5,128,128]{2,1,0:T(8,128)(2,1)S(1)}, u32[]{:S(2)}, u32[]{:S(2)}) collective-permute-start(bf16[5,128,128]{2,1,0:T(8,128)(2,1)S(1)} %get-tuple-element.87), channel_id=1, source_target_pairs={{0,112},{1,113},{2,114},{3,115},{4,116},{5,117},{6,118},{7,119},{8... | collective-permute-start | bytes 491528 | tf_op jit(solution)/shard_map/a_sum_both/ppermute | solution.py:49
  23.5 19.3 %collective-permute-start.5 = (bf16[20,128,128]{2,1,0:T(8,128)(2,1)S(1)}, bf16[20,128,128]{2,1,0:T(8,128)(2,1)S(1)}, u32[]{:S(2)}, u32[]{:S(2)}) collective-permute-start(bf16[20,128,128]{2,1,0:T(8,128)(2,1)S(1)} %get-tuple-element.55), channel_id=1, source_target_pairs={{0,64},{1,65},{2,66},{3,67},{4,68},{5,69},{6,70},{7,71},{8,72},{9,... | collective-permute-start | bytes 1966088 | tf_op jit(solution)/shard_map/sum_1_x/ppermute | solution.py:49
  25.2 17.6 %collective-permute-start.6 = (bf16[20,128,128]{2,1,0:T(8,128)(2,1)S(1)}, bf16[20,128,128]{2,1,0:T(8,128)(2,1)S(1)}, u32[]{:S(2)}, u32[]{:S(2)}) collective-permute-start(bf16[20,128,128]{2,1,0:T(8,128)(2,1)S(1)} %get-tuple-element.56), channel_id=1, source_target_pairs={{0,48},{1,49},{2,50},{3,51},{4,52},{5,53},{6,54},{7,55},{8,56},{9,... | collective-permute-start | bytes 1966088 | tf_op jit(solution)/shard_map/sum_1_y/ppermute | solution.py:49
  27.6 15.1 %collective-permute-start.9 = (bf16[64,1536]{1,0:T(8,128)(2,1)S(1)}, bf16[64,1536]{1,0:T(8,128)(2,1)S(1)}, u32[]{:S(2)}, u32[]{:S(2)}) collective-permute-start(bf16[64,1536]{1,0:T(8,128)(2,1)S(1)} %get-tuple-element.62), channel_id=1, source_target_pairs={{0,24},{1,25},{2,26},{3,27},{4,28},{5,29},{6,30},{7,31},{8,16},{9,... | collective-permute-start | bytes 589832 | tf_op jit(solution)/shard_map/w_1/ppermute | solution.py:49
  28.3 14.4 %collective-permute-start.7 = (bf16[5,128,128]{2,1,0:T(8,128)(2,1)S(1)}, bf16[5,128,128]{2,1,0:T(8,128)(2,1)S(1)}, u32[]{:S(2)}, u32[]{:S(2)}) collective-permute-start(bf16[5,128,128]{2,1,0:T(8,128)(2,1)S(1)} %add_convert_fusion.10), channel_id=1, source_target_pairs={{0,16},{1,17},{2,18},{3,19},{4,20},{5,21},{6,22},{7,23},{8,24},{9,... | collective-permute-start | bytes 491528 | tf_op jit(solution)/shard_map/a_near/ppermute | solution.py:49
  42.8 8.4 %collective-permute-start.11 = (bf16[10,128,128]{2,1,0:T(8,128)(2,1)S(1)}, bf16[10,128,128]{2,1,0:T(8,128)(2,1)S(1)}, u32[]{:S(2)}, u32[]{:S(2)}) collective-permute-start(bf16[10,128,128]{2,1,0:T(8,128)(2,1)S(1)} %add_convert_fusion.6), channel_id=1, source_target_pairs={{0,16},{1,17},{2,18},{3,19},{4,20},{5,21},{6,22},{7,23},{8,24},{9,... | collective-permute-start | bytes 983048 | tf_op jit(solution)/shard_map/sum_2_near/ppermute | solution.py:49
  44.4 9.3 %collective-permute-start.10 = (bf16[10,128,128]{2,1,0:T(8,128)(2,1)S(1)}, bf16[10,128,128]{2,1,0:T(8,128)(2,1)S(1)}, u32[]{:S(2)}, u32[]{:S(2)}) collective-permute-start(bf16[10,128,128]{2,1,0:T(8,128)(2,1)S(1)} %add_convert_fusion.7), channel_id=1, source_target_pairs={{0,48},{1,49},{2,50},{3,51},{4,52},{5,53},{6,54},{7,55},{8,56},{9,... | collective-permute-start | bytes 983048 | tf_op jit(solution)/shard_map/sum_2_y/ppermute | solution.py:49
  46.4 4.5 %collective-permute-start.12 = (bf16[5,128,128]{2,1,0:T(8,128)(2,1)S(1)}, bf16[5,128,128]{2,1,0:T(8,128)(2,1)S(1)}, u32[]{:S(2)}, u32[]{:S(2)}) collective-permute-start(bf16[5,128,128]{2,1,0:T(8,128)(2,1)S(1)} %add_convert_fusion.9), channel_id=1, source_target_pairs={{0,4},{1,5},{2,6},{3,7},{4,0},{5,1},{6,2},{7,3},{8,12},{9,13},{10,... | collective-permute-start | bytes 491528 | tf_op jit(solution)/shard_map/a_pair/ppermute | solution.py:49
  47.7 24.7 %collective-permute-start.17 = (bf16[384,1536]{1,0:T(8,128)(2,1)S(1)}, bf16[384,1536]{1,0:T(8,128)(2,1)S(1)}, u32[]{:S(2)}, u32[]{:S(2)}) collective-permute-start(bf16[384,1536]{1,0:T(8,128)(2,1)S(1)} %get-tuple-element.85), channel_id=1, source_target_pairs={{0,8},{1,9},{2,10},{3,11},{4,12},{5,13},{6,14},{7,15},{8,0},{9,1},... | collective-permute-start | bytes 3538952 | tf_op jit(solution)/shard_map/w_core/ppermute | solution.py:49
  53.9 8.7 %collective-permute-start.14 = (bf16[10,128,128]{2,1,0:T(8,128)(2,1)S(1)}, bf16[10,128,128]{2,1,0:T(8,128)(2,1)S(1)}, u32[]{:S(2)}, u32[]{:S(2)}) collective-permute-start(bf16[10,128,128]{2,1,0:T(8,128)(2,1)S(1)} %add_convert_fusion.3), channel_id=1, source_target_pairs={{0,64},{1,65},{2,66},{3,67},{4,68},{5,69},{6,70},{7,71},{8,72},{9,... | collective-permute-start | bytes 983048 | tf_op jit(solution)/shard_map/sum_3_x/ppermute | solution.py:49
  56.8 6.9 %collective-permute-start.13 = (bf16[10,128,128]{2,1,0:T(8,128)(2,1)S(1)}, bf16[10,128,128]{2,1,0:T(8,128)(2,1)S(1)}, u32[]{:S(2)}, u32[]{:S(2)}) collective-permute-start(bf16[10,128,128]{2,1,0:T(8,128)(2,1)S(1)} %add_convert_fusion.5), channel_id=1, source_target_pairs={{0,16},{1,17},{2,18},{3,19},{4,20},{5,21},{6,22},{7,23},{8,24},{9,... | collective-permute-start | bytes 983048 | tf_op jit(solution)/shard_map/sum_3_near/ppermute | solution.py:49
  57.0 9.5 %collective-permute-start.22 = (bf16[10,128,128]{2,1,0:T(8,128)(2,1)S(1)}, bf16[10,128,128]{2,1,0:T(8,128)(2,1)S(1)}, u32[]{:S(2)}, u32[]{:S(2)}) collective-permute-start(bf16[10,128,128]{2,1,0:T(8,128)(2,1)S(1)} %pad_maximum_fusion.2.refs_0_), channel_id=1, source_target_pairs={{0,1},{1,2},{2,3},{3,0},{4,5},{5,6},{6,7},{7,4},{8,9},{9,10},{10,1... | collective-permute-start | bytes 983048 | tf_op jit(solution)/shard_map/a_up/ppermute | solution.py:49
  58.7 12.1 %collective-permute-start.21 = (bf16[10,128,128]{2,1,0:T(8,128)(2,1)S(1)}, bf16[10,128,128]{2,1,0:T(8,128)(2,1)S(1)}, u32[]{:S(2)}, u32[]{:S(2)}) collective-permute-start(bf16[10,128,128]{2,1,0:T(8,128)(2,1)S(1)} %pad_maximum_fusion.2.refs_0_), channel_id=1, source_target_pairs={{0,3},{1,0},{2,1},{3,2},{4,7},{5,4},{6,5},{7,6},{8,11},{9,8},{10,9... | collective-permute-start | bytes 983048 | tf_op jit(solution)/shard_map/a_down/ppermute | solution.py:49
  63.9 15.2 %collective-permute-start.16 = (bf16[10,128,128]{2,1,0:T(8,128)(2,1)S(1)}, bf16[10,128,128]{2,1,0:T(8,128)(2,1)S(1)}, u32[]{:S(2)}, u32[]{:S(2)}) collective-permute-start(bf16[10,128,128]{2,1,0:T(8,128)(2,1)S(1)} %add_convert_fusion.1), channel_id=1, source_target_pairs={{0,16},{1,17},{2,18},{3,19},{4,20},{5,21},{6,22},{7,23},{8,24},{9,... | collective-permute-start | bytes 983048 | tf_op jit(solution)/shard_map/back_4_near/ppermute | solution.py:49
  64.4 15.1 %collective-permute-start.15 = (bf16[10,128,128]{2,1,0:T(8,128)(2,1)S(1)}, bf16[10,128,128]{2,1,0:T(8,128)(2,1)S(1)}, u32[]{:S(2)}, u32[]{:S(2)}) collective-permute-start(bf16[10,128,128]{2,1,0:T(8,128)(2,1)S(1)} %add_convert_fusion.2), channel_id=1, source_target_pairs={{0,48},{1,49},{2,50},{3,51},{4,52},{5,53},{6,54},{7,55},{8,56},{9,... | collective-permute-start | bytes 983048 | tf_op jit(solution)/shard_map/back_4_y/ppermute | solution.py:49
  66.5 12.5 %collective-permute-start.18 = (bf16[64,1536]{1,0:T(8,128)(2,1)S(1)}, bf16[64,1536]{1,0:T(8,128)(2,1)S(1)}, u32[]{:S(2)}, u32[]{:S(2)}) collective-permute-start(bf16[64,1536]{1,0:T(8,128)(2,1)S(1)} %get-tuple-element.72), channel_id=1, source_target_pairs={{0,24},{1,25},{2,26},{3,27},{4,28},{5,29},{6,30},{7,31},{8,16},{9,... | collective-permute-start | bytes 589832 | tf_op jit(solution)/shard_map/w_2/ppermute | solution.py:49
  70.8 7.6 %collective-permute-start.23 = (bf16[5,128,128]{2,1,0:T(8,128)(2,1)S(1)}, bf16[5,128,128]{2,1,0:T(8,128)(2,1)S(1)}, u32[]{:S(2)}, u32[]{:S(2)}) collective-permute-start(bf16[5,128,128]{2,1,0:T(8,128)(2,1)S(1)} %slice.76), channel_id=1, source_target_pairs={{0,1},{1,2},{2,3},{3,0},{4,5},{5,6},{6,7},{7,4},{8,9},{9,10},{10,1... | collective-permute-start | bytes 491528 | tf_op jit(solution)/shard_map/a_up_2/ppermute | solution.py:49
  72.4 6.2 %collective-permute-start.24 = (bf16[5,128,128]{2,1,0:T(8,128)(2,1)S(1)}, bf16[5,128,128]{2,1,0:T(8,128)(2,1)S(1)}, u32[]{:S(2)}, u32[]{:S(2)}) collective-permute-start(bf16[5,128,128]{2,1,0:T(8,128)(2,1)S(1)} %slice.77), channel_id=1, source_target_pairs={{0,3},{1,0},{2,1},{3,2},{4,7},{5,4},{6,5},{7,6},{8,11},{9,8},{10,9... | collective-permute-start | bytes 491528 | tf_op jit(solution)/shard_map/a_down_2/ppermute | solution.py:49
  78.4 1.6 %collective-permute-start.25 = (bf16[10,128,128]{2,1,0:T(8,128)(2,1)S(1)}, bf16[10,128,128]{2,1,0:T(8,128)(2,1)S(1)}, u32[]{:S(2)}, u32[]{:S(2)}) collective-permute-start(bf16[10,128,128]{2,1,0:T(8,128)(2,1)S(1)} %pad_maximum_fusion.2.refs_0_), channel_id=1, source_target_pairs={{0,8},{1,9},{2,10},{3,11},{4,12},{5,13},{6,14},{7,15},{8,0},{9,1},... | collective-permute-start | bytes 983048 | tf_op jit(solution)/shard_map/a_core_back/ppermute | solution.py:49
  78.6 2.2 %collective-permute-start.26 = (bf16[10,128,128]{2,1,0:T(8,128)(2,1)S(1)}, bf16[10,128,128]{2,1,0:T(8,128)(2,1)S(1)}, u32[]{:S(2)}, u32[]{:S(2)}) collective-permute-start(bf16[10,128,128]{2,1,0:T(8,128)(2,1)S(1)} %collective-permute-done.21.refs_1_), channel_id=1, source_target_pairs={{0,8},{1,9},{2,10},{3,11},{4,12},{5,13},{6,14},{7,15},{8,0},{9,1},... | collective-permute-start | bytes 983048 | tf_op jit(solution)/shard_map/a_core_back/ppermute | solution.py:49
  79.0 3.1 %collective-permute-start.29 = (bf16[10,128,128]{2,1,0:T(8,128)(2,1)S(1)}, bf16[10,128,128]{2,1,0:T(8,128)(2,1)S(1)}, u32[]{:S(2)}, u32[]{:S(2)}) collective-permute-start(bf16[10,128,128]{2,1,0:T(8,128)(2,1)S(1)} %collective-permute-done.22.refs_4_), channel_id=1, source_target_pairs={{0,8},{1,9},{2,10},{3,11},{4,12},{5,13},{6,14},{7,15},{8,0},{9,1},... | collective-permute-start | bytes 983048 | tf_op jit(solution)/shard_map/a_core_back/ppermute | solution.py:49
  79.2 4.3 %collective-permute-start.27 = (bf16[5,128,128]{2,1,0:T(8,128)(2,1)S(1)}, bf16[5,128,128]{2,1,0:T(8,128)(2,1)S(1)}, u32[]{:S(2)}, u32[]{:S(2)}) collective-permute-start(bf16[5,128,128]{2,1,0:T(8,128)(2,1)S(1)} %collective-permute-done.23.refs_2_), channel_id=1, source_target_pairs={{0,8},{1,9},{2,10},{3,11},{4,12},{5,13},{6,14},{7,15},{8,0},{9,1},... | collective-permute-start | bytes 491528 | tf_op jit(solution)/shard_map/a_core_back/ppermute | solution.py:49
  79.5 4.0 %collective-permute-start.28 = (bf16[5,128,128]{2,1,0:T(8,128)(2,1)S(1)}, bf16[5,128,128]{2,1,0:T(8,128)(2,1)S(1)}, u32[]{:S(2)}, u32[]{:S(2)}) collective-permute-start(bf16[5,128,128]{2,1,0:T(8,128)(2,1)S(1)} %collective-permute-done.24.refs_3_), channel_id=1, source_target_pairs={{0,8},{1,9},{2,10},{3,11},{4,12},{5,13},{6,14},{7,15},{8,0},{9,1},... | collective-permute-start | bytes 491528 | tf_op jit(solution)/shard_map/a_core_back/ppermute | solution.py:49
  80.1 17.4 %collective-permute-start.20 = (bf16[20,128,128]{2,1,0:T(8,128)(2,1)S(1)}, bf16[20,128,128]{2,1,0:T(8,128)(2,1)S(1)}, u32[]{:S(2)}, u32[]{:S(2)}) collective-permute-start(bf16[20,128,128]{2,1,0:T(8,128)(2,1)S(1)} %pad_maximum_fusion.1.second_own), channel_id=1, source_target_pairs={{0,48},{1,49},{2,50},{3,51},{4,52},{5,53},{6,54},{7,55},{8,56},{9,... | collective-permute-start | bytes 1966088 | tf_op jit(solution)/shard_map/back_5_y/ppermute | solution.py:49
  80.8 17.3 %collective-permute-start.19 = (bf16[20,128,128]{2,1,0:T(8,128)(2,1)S(1)}, bf16[20,128,128]{2,1,0:T(8,128)(2,1)S(1)}, u32[]{:S(2)}, u32[]{:S(2)}) collective-permute-start(bf16[20,128,128]{2,1,0:T(8,128)(2,1)S(1)} %pad_maximum_fusion.first_own), channel_id=1, source_target_pairs={{0,64},{1,65},{2,66},{3,67},{4,68},{5,69},{6,70},{7,71},{8,72},{9,... | collective-permute-start | bytes 1966088 | tf_op jit(solution)/shard_map/back_5_x/ppermute | solution.py:49
  82.1 19.9 %collective-permute-start.30 = (bf16[256,1536]{1,0:T(8,128)(2,1)S(1)}, bf16[256,1536]{1,0:T(8,128)(2,1)S(1)}, u32[]{:S(2)}, u32[]{:S(2)}) collective-permute-start(bf16[256,1536]{1,0:T(8,128)(2,1)S(1)} %get-tuple-element.82), channel_id=1, source_target_pairs={{0,24},{1,25},{2,26},{3,27},{4,28},{5,29},{6,30},{7,31},{8,16},{9,... | collective-permute-start | bytes 2359304 | tf_op jit(solution)/shard_map/w_3/ppermute | solution.py:49
  115.0 3.2 %collective-permute-start.31 = (bf16[384,1536]{1,0:T(8,128)(2,1)S(1)}, bf16[384,1536]{1,0:T(8,128)(2,1)S(1)}, u32[]{:S(2)}, u32[]{:S(2)}) collective-permute-start(bf16[384,1536]{1,0:T(8,128)(2,1)S(1)} %get-tuple-element.84), channel_id=1, source_target_pairs={{0,8},{1,9},{2,10},{3,11},{4,12},{5,13},{6,14},{7,15},{8,0},{9,1},... | collective-permute-start | bytes 3538952 | tf_op jit(solution)/shard_map/out_core/ppermute | solution.py:49
  (4 other events, 16.2 us)

commit v4 on v3

--- a/solution.py
+++ b/solution.py
@@ -382,17 +382,16 @@
     second_got = send(second_own, Y_NEAR, "back_4_near")
     a_far = [send(a_below[:a], Z_UP, "a_up_2"), send(a_above[a:], Z_DOWN, "a_down_2")]
     a_parts = (a_own, a_above, *a_far, a_below)
-    a_swapped = [send(part, CORE, "a_core_back") for part in a_parts]
     w_core = send(lax.dynamic_slice_in_dim(weight_grad, other, BLK, 1), CORE, "w_core")
     w_2 = send(w_2, Y_NEAR_CORE, "w_2")
 
-    first_got, second_got, w_core, w_2, w_3, a_own = together(first_got, second_got, w_core, w_2, w_3, a_own)
+    first_got, second_got, w_core, w_2, w_3, *a_parts = together(first_got, second_got, w_core, w_2, w_3, *a_parts)
     first_own = jnp.concatenate([first_own, first_got])
     second_own = jnp.concatenate([second_own, second_got])
     first_got = send(first_own, X_HALF, "back_5_x")
     second_got = send(second_own, Y_FAR, "back_5_y")
     w_3 = send(w_3, Y_NEAR_CORE, "w_3")
-    a_parts = (a_own, *a_parts[1:], *a_swapped)
+    a_parts = (*a_parts, *(send(part, CORE, "a_core_back") for part in a_parts))
 
     inverse = kernel(
         inverse_kernel,

time: 119 us -> 123 us (1.034)
  waiting for transfers between devices: 35.3 us -> 41.3 us
  starting transfers between devices: 45.7 us -> 43.7 us
    ppermute x32, waiting for transfers between devices: 35.3 us -> 41.3 us  [send(): return lax.ppermute(array, AXES, pairs)]
    ppermute x32, starting transfers between devices: 45.7 us -> 43.7 us  [send(): return lax.ppermute(array, AXES, pairs)]
  transfers between devices with their start and end apart: 32 -> 32, of which waited for: 16 -> 15; matrix products, arithmetic and copies ran while one was open for 1% -> 1% of each run, Pallas kernels for 16% -> 15%
where the time goes in v4:
time: 123 us
  starting transfers between devices  43.7 us (36%)
  waiting for transfers between devices  41.3 us (34%)
  Pallas kernels  31.9 us (26%)
  local copies, waits for them, and re-layouts  4.91 us (4%)
    ppermute x32, starting transfers between devices, send(): return lax.ppermute(array, AXES, pairs)  43.7 us
    ppermute x32, waiting for transfers between devices, send(): return lax.ppermute(array, AXES, pairs)  41.3 us
    pallas_call x5, Pallas kernels, kernel(): pl.pallas_call(body, out_shape=out_shape, in_specs=[whole(space) for spac...  31.9 us
  transfers between devices with their start and end apart: 32, of which 15 were waited for; matrix products, arithmetic and copies ran while one was open for 1% of the time, Pallas kernels for 15%

profile of v4, /device:TPU:1, one launch (start us, length us, event | category | flops | bytes accessed | tf_op | source)
XLA Modules:
  0.0 123.2 jit_solution(12926210810043775758)
XLA Ops:
  1.4 1.9 %constant_dynamic-slice_fusion = (bf16[384,1536]{1,0:T(8,128)(2,1)S(1)}, bf16[384,1536]{1,0:T(8,128)(2,1)S(1)}) fusion(bf16[384,3072]{1,0:T(8,128)(2,1)} %w_own.1, s32[]{:T(128)S(6)} %select_n.17, s32[]{:T(128)S(6)} %select_n.18), kind=kLoop, calls=%fused_computation.16 | loop fusion | bytes 4718600 | tf_op jit(solution)/shard_map/dynamic_slice | solution.py:385
  3.3 1.5 %collective-permute-start.1 = (bf16[256,1536]{1,0:T(8,128)(2,1)S(1)}, bf16[256,1536]{1,0:T(8,128)(2,1)S(1)}, u32[]{:S(2)}, u32[]{:S(2)}) collective-permute-start(bf16[256,1536]{1,0:T(8,128)(2,1)S(1)} %constant_dynamic-slice_fusion.2), channel_id=1, source_target_pairs={{0,8},{1,9},{2,10},{3,11},{4,12},{5,13},{6,14},{7,15},{8,0},{9,1},... | collective-permute-start | bytes 2359304 | tf_op jit(solution)/shard_map/g_tokens/ppermute | solution.py:49
  4.8 2.1 %cov_a.1 = (bf16[20,128,128]{2,1,0:T(8,128)(2,1)S(1)}, bf16[20,128,128]{2,1,0:T(8,128)(2,1)S(1)}, bf16[64,1536]{1,0:T(8,128)(2,1)S(1)}, bf16[64,1536]{1,0:T(8,128)(2,1)S(1)}, bf16[256,1536]{1,0:T(8,128)(2,1)S(1)}) custom-call(bf16[256,6144]{1,0:T(8,128)(2,1)S(1)} %copy-done.1, bf16[384,3072]{1,0:T(8,128)(2,1)S(1)} %copy-done), custom_call_target="tpu_custom_call" | custom-call | flops 335544320 | bytes 5242880 | tf_op jit(solution)/shard_map/cov_a/pallas_call | solution.py:298
  9.4 2.9 %collective-permute-start.2 = (bf16[5,128,128]{2,1,0:T(8,128)(2,1)S(1)}, bf16[5,128,128]{2,1,0:T(8,128)(2,1)S(1)}, u32[]{:S(2)}, u32[]{:S(2)}) collective-permute-start(bf16[5,128,128]{2,1,0:T(8,128)(2,1)S(1)} %get-tuple-element.97), channel_id=1, source_target_pairs={{0,48},{1,49},{2,50},{3,51},{4,52},{5,53},{6,54},{7,55},{8,56},{9,... | collective-permute-start | bytes 491528 | tf_op jit(solution)/shard_map/a_sum_y/ppermute | solution.py:49
  12.3 2.7 %collective-permute-start.3 = (bf16[5,128,128]{2,1,0:T(8,128)(2,1)S(1)}, bf16[5,128,128]{2,1,0:T(8,128)(2,1)S(1)}, u32[]{:S(2)}, u32[]{:S(2)}) collective-permute-start(bf16[5,128,128]{2,1,0:T(8,128)(2,1)S(1)} %get-tuple-element.96), channel_id=1, source_target_pairs={{0,64},{1,65},{2,66},{3,67},{4,68},{5,69},{6,70},{7,71},{8,72},{9,... | collective-permute-start | bytes 491528 | tf_op jit(solution)/shard_map/a_sum_x/ppermute | solution.py:49
  15.1 3.5 %cov_g.1 = (bf16[20,128,128]{2,1,0:T(8,128)(2,1)S(1)}, bf16[20,128,128]{2,1,0:T(8,128)(2,1)S(1)}, bf16[20,128,128]{2,1,0:T(8,128)(2,1)S(1)}, bf16[20,128,128]{2,1,0:T(8,128)(2,1)S(1)}) custom-call(bf16[256,3072]{1,0:T(8,128)(2,1)S(1)} %copy-done.2, bf16[256,1536]{1,0:T(8,128)(2,1)S(1)} %collective-permute-done.1.got), custom_call_target="tpu_custom_call" | custom-call | flops 1409286144 | bytes 4194304 | tf_op jit(solution)/shard_map/cov_g/pallas_call | solution.py:298
  18.9 4.5 %collective-permute-done.4 = bf16[5,128,128]{2,1,0:T(8,128)(2,1)S(1)} collective-permute-done((bf16[5,128,128]{2,1,0:T(8,128)(2,1)S(1)}, bf16[5,128,128]{2,1,0:T(8,128)(2,1)S(1)}, u32[]{:S(2)}, u32[]{:S(2)}) %collective-permute-start.4) | collective-permute-done | bytes 163872 | tf_op jit(solution)/shard_map/a_sum_both/ppermute | solution.py:49
  23.5 1.7 %collective-permute-start.5 = (bf16[20,128,128]{2,1,0:T(8,128)(2,1)S(1)}, bf16[20,128,128]{2,1,0:T(8,128)(2,1)S(1)}, u32[]{:S(2)}, u32[]{:S(2)}) collective-permute-start(bf16[20,128,128]{2,1,0:T(8,128)(2,1)S(1)} %get-tuple-element.59), channel_id=1, source_target_pairs={{0,64},{1,65},{2,66},{3,67},{4,68},{5,69},{6,70},{7,71},{8,72},{9,... | collective-permute-start | bytes 1966088 | tf_op jit(solution)/shard_map/sum_1_x/ppermute | solution.py:49
  25.2 2.4 %collective-permute-start.6 = (bf16[20,128,128]{2,1,0:T(8,128)(2,1)S(1)}, bf16[20,128,128]{2,1,0:T(8,128)(2,1)S(1)}, u32[]{:S(2)}, u32[]{:S(2)}) collective-permute-start(bf16[20,128,128]{2,1,0:T(8,128)(2,1)S(1)} %get-tuple-element.60), channel_id=1, source_target_pairs={{0,48},{1,49},{2,50},{3,51},{4,52},{5,53},{6,54},{7,55},{8,56},{9,... | collective-permute-start | bytes 1966088 | tf_op jit(solution)/shard_map/sum_1_y/ppermute | solution.py:49
  28.3 2.9 %collective-permute-start.7 = (bf16[5,128,128]{2,1,0:T(8,128)(2,1)S(1)}, bf16[5,128,128]{2,1,0:T(8,128)(2,1)S(1)}, u32[]{:S(2)}, u32[]{:S(2)}) collective-permute-start(bf16[5,128,128]{2,1,0:T(8,128)(2,1)S(1)} %add_convert_fusion.10), channel_id=1, source_target_pairs={{0,16},{1,17},{2,18},{3,19},{4,20},{5,21},{6,22},{7,23},{8,24},{9,... | collective-permute-start | bytes 491528 | tf_op jit(solution)/shard_map/a_near/ppermute | solution.py:49
  31.2 11.5 %collective-permute-done.7 = bf16[5,128,128]{2,1,0:T(8,128)(2,1)S(1)} collective-permute-done((bf16[5,128,128]{2,1,0:T(8,128)(2,1)S(1)}, bf16[5,128,128]{2,1,0:T(8,128)(2,1)S(1)}, u32[]{:S(2)}, u32[]{:S(2)}) %collective-permute-start.7) | collective-permute-done | bytes 163872 | tf_op jit(solution)/shard_map/a_near/ppermute | solution.py:49
  42.8 1.5 %collective-permute-start.11 = (bf16[10,128,128]{2,1,0:T(8,128)(2,1)S(1)}, bf16[10,128,128]{2,1,0:T(8,128)(2,1)S(1)}, u32[]{:S(2)}, u32[]{:S(2)}) collective-permute-start(bf16[10,128,128]{2,1,0:T(8,128)(2,1)S(1)} %add_convert_fusion.6), channel_id=1, source_target_pairs={{0,16},{1,17},{2,18},{3,19},{4,20},{5,21},{6,22},{7,23},{8,24},{9,... | collective-permute-start | bytes 983048 | tf_op jit(solution)/shard_map/sum_2_near/ppermute | solution.py:49
  44.4 2.0 %collective-permute-start.10 = (bf16[10,128,128]{2,1,0:T(8,128)(2,1)S(1)}, bf16[10,128,128]{2,1,0:T(8,128)(2,1)S(1)}, u32[]{:S(2)}, u32[]{:S(2)}) collective-permute-start(bf16[10,128,128]{2,1,0:T(8,128)(2,1)S(1)} %add_convert_fusion.7), channel_id=1, source_target_pairs={{0,48},{1,49},{2,50},{3,51},{4,52},{5,53},{6,54},{7,55},{8,56},{9,... | collective-permute-start | bytes 983048 | tf_op jit(solution)/shard_map/sum_2_y/ppermute | solution.py:49
  47.7 3.2 %collective-permute-done.12 = bf16[5,128,128]{2,1,0:T(8,128)(2,1)S(1)} collective-permute-done((bf16[5,128,128]{2,1,0:T(8,128)(2,1)S(1)}, bf16[5,128,128]{2,1,0:T(8,128)(2,1)S(1)}, u32[]{:S(2)}, u32[]{:S(2)}) %collective-permute-start.12) | collective-permute-done | bytes 163872 | tf_op jit(solution)/shard_map/a_pair/ppermute | solution.py:49
  51.3 2.5 %collective-permute-done.10 = bf16[10,128,128]{2,1,0:T(8,128)(2,1)S(1)} collective-permute-done((bf16[10,128,128]{2,1,0:T(8,128)(2,1)S(1)}, bf16[10,128,128]{2,1,0:T(8,128)(2,1)S(1)}, u32[]{:S(2)}, u32[]{:S(2)}) %collective-permute-start.10) | collective-permute-done | bytes 327712 | tf_op jit(solution)/shard_map/sum_2_y/ppermute | solution.py:49
  53.9 2.8 %collective-permute-start.14 = (bf16[10,128,128]{2,1,0:T(8,128)(2,1)S(1)}, bf16[10,128,128]{2,1,0:T(8,128)(2,1)S(1)}, u32[]{:S(2)}, u32[]{:S(2)}) collective-permute-start(bf16[10,128,128]{2,1,0:T(8,128)(2,1)S(1)} %add_convert_fusion.3), channel_id=1, source_target_pairs={{0,64},{1,65},{2,66},{3,67},{4,68},{5,69},{6,70},{7,71},{8,72},{9,... | collective-permute-start | bytes 983048 | tf_op jit(solution)/shard_map/sum_3_x/ppermute | solution.py:49
  56.9 2.4 %collective-permute-start.17 = (bf16[384,1536]{1,0:T(8,128)(2,1)S(1)}, bf16[384,1536]{1,0:T(8,128)(2,1)S(1)}, u32[]{:S(2)}, u32[]{:S(2)}) collective-permute-start(bf16[384,1536]{1,0:T(8,128)(2,1)S(1)} %get-tuple-element.93), channel_id=1, source_target_pairs={{0,8},{1,9},{2,10},{3,11},{4,12},{5,13},{6,14},{7,15},{8,0},{9,1},... | collective-permute-start | bytes 3538952 | tf_op jit(solution)/shard_map/w_core/ppermute | solution.py:49
  59.4 1.7 %collective-permute-start.20 = (bf16[10,128,128]{2,1,0:T(8,128)(2,1)S(1)}, bf16[10,128,128]{2,1,0:T(8,128)(2,1)S(1)}, u32[]{:S(2)}, u32[]{:S(2)}) collective-permute-start(bf16[10,128,128]{2,1,0:T(8,128)(2,1)S(1)} %pad_maximum_fusion.2.refs_0_), channel_id=1, source_target_pairs={{0,1},{1,2},{2,3},{3,0},{4,5},{5,6},{6,7},{7,4},{8,9},{9,10},{10,1... | collective-permute-start | bytes 983048 | tf_op jit(solution)/shard_map/a_up/ppermute | solution.py:49
  61.1 2.2 %collective-permute-start.19 = (bf16[10,128,128]{2,1,0:T(8,128)(2,1)S(1)}, bf16[10,128,128]{2,1,0:T(8,128)(2,1)S(1)}, u32[]{:S(2)}, u32[]{:S(2)}) collective-permute-start(bf16[10,128,128]{2,1,0:T(8,128)(2,1)S(1)} %pad_maximum_fusion.2.refs_0_), channel_id=1, source_target_pairs={{0,3},{1,0},{2,1},{3,2},{4,7},{5,4},{6,5},{7,6},{8,11},{9,8},{10,9... | collective-permute-start | bytes 983048 | tf_op jit(solution)/shard_map/a_down/ppermute | solution.py:49
  65.3 2.0 %collective-permute-start.15 = (bf16[10,128,128]{2,1,0:T(8,128)(2,1)S(1)}, bf16[10,128,128]{2,1,0:T(8,128)(2,1)S(1)}, u32[]{:S(2)}, u32[]{:S(2)}) collective-permute-start(bf16[10,128,128]{2,1,0:T(8,128)(2,1)S(1)} %add_convert_fusion.2), channel_id=1, source_target_pairs={{0,48},{1,49},{2,50},{3,51},{4,52},{5,53},{6,54},{7,55},{8,56},{9,... | collective-permute-start | bytes 983048 | tf_op jit(solution)/shard_map/back_4_y/ppermute | solution.py:49
  67.3 4.0 %collective-permute-done.20.refs_4_ = bf16[10,128,128]{2,1,0:T(8,128)(2,1)S(1)} collective-permute-done((bf16[10,128,128]{2,1,0:T(8,128)(2,1)S(1)}, bf16[10,128,128]{2,1,0:T(8,128)(2,1)S(1)}, u32[]{:S(2)}, u32[]{:S(2)}) %collective-permute-start.20) | collective-permute-done | bytes 327712 | tf_op jit(solution)/shard_map/a_up/ppermute | solution.py:49
  71.3 2.1 %collective-permute-start.18 = (bf16[64,1536]{1,0:T(8,128)(2,1)S(1)}, bf16[64,1536]{1,0:T(8,128)(2,1)S(1)}, u32[]{:S(2)}, u32[]{:S(2)}) collective-permute-start(bf16[64,1536]{1,0:T(8,128)(2,1)S(1)} %get-tuple-element.76), channel_id=1, source_target_pairs={{0,24},{1,25},{2,26},{3,27},{4,28},{5,29},{6,30},{7,31},{8,16},{9,... | collective-permute-start | bytes 589832 | tf_op jit(solution)/shard_map/w_2/ppermute | solution.py:49
  73.6 2.7 %collective-permute-start.22 = (bf16[5,128,128]{2,1,0:T(8,128)(2,1)S(1)}, bf16[5,128,128]{2,1,0:T(8,128)(2,1)S(1)}, u32[]{:S(2)}, u32[]{:S(2)}) collective-permute-start(bf16[5,128,128]{2,1,0:T(8,128)(2,1)S(1)} %slice.77), channel_id=1, source_target_pairs={{0,3},{1,0},{2,1},{3,2},{4,7},{5,4},{6,5},{7,6},{8,11},{9,8},{10,9... | collective-permute-start | bytes 491528 | tf_op jit(solution)/shard_map/a_down_2/ppermute | solution.py:49
  76.3 4.4 %collective-permute-done.21.refs_2_ = bf16[5,128,128]{2,1,0:T(8,128)(2,1)S(1)} collective-permute-done((bf16[5,128,128]{2,1,0:T(8,128)(2,1)S(1)}, bf16[5,128,128]{2,1,0:T(8,128)(2,1)S(1)}, u32[]{:S(2)}, u32[]{:S(2)}) %collective-permute-start.21) | collective-permute-done | bytes 163872 | tf_op jit(solution)/shard_map/a_up_2/ppermute | solution.py:49
  83.9 1.9 %collective-permute-start.24 = (bf16[20,128,128]{2,1,0:T(8,128)(2,1)S(1)}, bf16[20,128,128]{2,1,0:T(8,128)(2,1)S(1)}, u32[]{:S(2)}, u32[]{:S(2)}) collective-permute-start(bf16[20,128,128]{2,1,0:T(8,128)(2,1)S(1)} %pad_maximum_fusion.1.second_own), channel_id=1, source_target_pairs={{0,48},{1,49},{2,50},{3,51},{4,52},{5,53},{6,54},{7,55},{8,56},{9,... | collective-permute-start | bytes 1966088 | tf_op jit(solution)/shard_map/back_5_y/ppermute | solution.py:49
  86.1 9.2 %inverse.1 = bf16[768,1536]{1,0:T(8,128)(2,1)S(1)} custom-call(bf16[10,128,128]{2,1,0:T(8,128)(2,1)S(1)} %pad_maximum_fusion.2.refs_0_, bf16[10,128,128]{2,1,0:T(8,128)(2,1)S(1)} %collective-permute-done.19.refs_1_, bf16[5,128,128]{2,1,0:T(8,128)(2,1)S(1)} %collective-permute-done.21.refs_2_, bf16[5,128,128]{2,1,0:T(8,128)(2,1)S(1)} %collective-permute-done.22.refs_3_, ...), custom_call_target="tpu_custom_call" | custom-call | flops 7247757312 | bytes 5242880 | tf_op jit(solution)/shard_map/inverse/pallas_call | solution.py:298
  95.3 4.2 %left.1.part_left = f32[768,1536]{1,0:T(8,128)S(1)} custom-call(bf16[768,1536]{1,0:T(8,128)(2,1)S(1)} %inverse.1, bf16[384,3072]{1,0:T(8,128)(2,1)S(1)} %copy-done, bf16[384,1536]{1,0:T(8,128)(2,1)S(1)} %collective-permute-done.17.w_core, bf16[384,1536]{1,0:T(8,128)(2,1)S(1)} %collective-permute-done.8.refs_0_, ...), custom_call_target="tpu_custom_call" | custom-call | flops 3623878656 | bytes 9437184 | tf_op jit(solution)/shard_map/left/pallas_call | solution.py:298
  99.4 1.6 %collective-permute-done.24.second_got = bf16[20,128,128]{2,1,0:T(8,128)(2,1)S(1)} collective-permute-done((bf16[20,128,128]{2,1,0:T(8,128)(2,1)S(1)}, bf16[20,128,128]{2,1,0:T(8,128)(2,1)S(1)}, u32[]{:S(2)}, u32[]{:S(2)}) %collective-permute-start.24) | collective-permute-done | bytes 655392 | tf_op jit(solution)/shard_map/back_5_y/ppermute | solution.py:49
  101.0 1.9 %collective-permute-done.23.first_got = bf16[20,128,128]{2,1,0:T(8,128)(2,1)S(1)} collective-permute-done((bf16[20,128,128]{2,1,0:T(8,128)(2,1)S(1)}, bf16[20,128,128]{2,1,0:T(8,128)(2,1)S(1)}, u32[]{:S(2)}, u32[]{:S(2)}) %collective-permute-start.23) | collective-permute-done | bytes 655392 | tf_op jit(solution)/shard_map/back_5_x/ppermute | solution.py:49
  102.9 3.0 %collective-permute-done.30.chunk = bf16[256,1536]{1,0:T(8,128)(2,1)S(1)} collective-permute-done((bf16[256,1536]{1,0:T(8,128)(2,1)S(1)}, bf16[256,1536]{1,0:T(8,128)(2,1)S(1)}, u32[]{:S(2)}, u32[]{:S(2)}) %collective-permute-start.30) | collective-permute-done | bytes 786464 | tf_op jit(solution)/shard_map/w_3/ppermute | solution.py:49
  105.9 13.0 %right.1 = (bf16[384,1536]{1,0:T(8,128)(2,1)S(1)}, bf16[384,1536]{1,0:T(8,128)(2,1)S(1)}) custom-call(bf16[20,128,128]{2,1,0:T(8,128)(2,1)S(1)} %pad_maximum_fusion.first_own, bf16[20,128,128]{2,1,0:T(8,128)(2,1)S(1)} %collective-permute-done.23.first_got, bf16[20,128,128]{2,1,0:T(8,128)(2,1)S(1)} %pad_maximum_fusion.1.second_own, ...), custom_call_target="tpu_custom_call" | custom-call | flops 10871635968 | bytes 8388608 | tf_op jit(solution)/shard_map/right/pallas_call | solution.py:298
  120.0 2.0 %collective-permute-done.31 = bf16[384,1536]{1,0:T(8,128)(2,1)S(1)} collective-permute-done((bf16[384,1536]{1,0:T(8,128)(2,1)S(1)}, bf16[384,1536]{1,0:T(8,128)(2,1)S(1)}, u32[]{:S(2)}, u32[]{:S(2)}) %collective-permute-start.31) | collective-permute-done | bytes 1179680 | tf_op jit(solution)/shard_map/out_core/ppermute | solution.py:49
  (66 shorter events, 14.9 us)
Async XLA Ops:
  3.3 5.9 %collective-permute-start.1 = (bf16[256,1536]{1,0:T(8,128)(2,1)S(1)}, bf16[256,1536]{1,0:T(8,128)(2,1)S(1)}, u32[]{:S(2)}, u32[]{:S(2)}) collective-permute-start(bf16[256,1536]{1,0:T(8,128)(2,1)S(1)} %constant_dynamic-slice_fusion.2), channel_id=1, source_target_pairs={{0,8},{1,9},{2,10},{3,11},{4,12},{5,13},{6,14},{7,15},{8,0},{9,1},... | collective-permute-start | bytes 2359304 | tf_op jit(solution)/shard_map/g_tokens/ppermute | solution.py:49
  6.9 2.3 %collective-permute-start = (bf16[20,128,128]{2,1,0:T(8,128)(2,1)S(1)}, bf16[20,128,128]{2,1,0:T(8,128)(2,1)S(1)}, u32[]{:S(2)}, u32[]{:S(2)}) collective-permute-start(bf16[20,128,128]{2,1,0:T(8,128)(2,1)S(1)} %get-tuple-element.50), channel_id=1, source_target_pairs={{0,8},{1,9},{2,10},{3,11},{4,12},{5,13},{6,14},{7,15},{8,0},{9,1},... | collective-permute-start | bytes 1966088 | tf_op jit(solution)/shard_map/a_core/ppermute | solution.py:49
  7.5 35.3 %collective-permute-start.8 = (bf16[384,1536]{1,0:T(8,128)(2,1)S(1)}, bf16[384,1536]{1,0:T(8,128)(2,1)S(1)}, u32[]{:S(2)}, u32[]{:S(2)}) collective-permute-start(bf16[384,1536]{1,0:T(8,128)(2,1)S(1)} %get-tuple-element.65), channel_id=1, source_target_pairs={{0,16},{1,17},{2,18},{3,19},{4,20},{5,21},{6,22},{7,23},{8,24},{9,... | collective-permute-start | bytes 3538952 | tf_op jit(solution)/shard_map/w_0/ppermute | solution.py:49
  9.4 9.2 %collective-permute-start.2 = (bf16[5,128,128]{2,1,0:T(8,128)(2,1)S(1)}, bf16[5,128,128]{2,1,0:T(8,128)(2,1)S(1)}, u32[]{:S(2)}, u32[]{:S(2)}) collective-permute-start(bf16[5,128,128]{2,1,0:T(8,128)(2,1)S(1)} %get-tuple-element.97), channel_id=1, source_target_pairs={{0,48},{1,49},{2,50},{3,51},{4,52},{5,53},{6,54},{7,55},{8,56},{9,... | collective-permute-start | bytes 491528 | tf_op jit(solution)/shard_map/a_sum_y/ppermute | solution.py:49
  12.3 6.6 %collective-permute-start.3 = (bf16[5,128,128]{2,1,0:T(8,128)(2,1)S(1)}, bf16[5,128,128]{2,1,0:T(8,128)(2,1)S(1)}, u32[]{:S(2)}, u32[]{:S(2)}) collective-permute-start(bf16[5,128,128]{2,1,0:T(8,128)(2,1)S(1)} %get-tuple-element.96), channel_id=1, source_target_pairs={{0,64},{1,65},{2,66},{3,67},{4,68},{5,69},{6,70},{7,71},{8,72},{9,... | collective-permute-start | bytes 491528 | tf_op jit(solution)/shard_map/a_sum_x/ppermute | solution.py:49
  15.1 8.4 %collective-permute-start.4 = (bf16[5,128,128]{2,1,0:T(8,128)(2,1)S(1)}, bf16[5,128,128]{2,1,0:T(8,128)(2,1)S(1)}, u32[]{:S(2)}, u32[]{:S(2)}) collective-permute-start(bf16[5,128,128]{2,1,0:T(8,128)(2,1)S(1)} %get-tuple-element.95), channel_id=1, source_target_pairs={{0,112},{1,113},{2,114},{3,115},{4,116},{5,117},{6,118},{7,119},{8... | collective-permute-start | bytes 491528 | tf_op jit(solution)/shard_map/a_sum_both/ppermute | solution.py:49
  23.5 19.3 %collective-permute-start.5 = (bf16[20,128,128]{2,1,0:T(8,128)(2,1)S(1)}, bf16[20,128,128]{2,1,0:T(8,128)(2,1)S(1)}, u32[]{:S(2)}, u32[]{:S(2)}) collective-permute-start(bf16[20,128,128]{2,1,0:T(8,128)(2,1)S(1)} %get-tuple-element.59), channel_id=1, source_target_pairs={{0,64},{1,65},{2,66},{3,67},{4,68},{5,69},{6,70},{7,71},{8,72},{9,... | collective-permute-start | bytes 1966088 | tf_op jit(solution)/shard_map/sum_1_x/ppermute | solution.py:49
  25.2 17.6 %collective-permute-start.6 = (bf16[20,128,128]{2,1,0:T(8,128)(2,1)S(1)}, bf16[20,128,128]{2,1,0:T(8,128)(2,1)S(1)}, u32[]{:S(2)}, u32[]{:S(2)}) collective-permute-start(bf16[20,128,128]{2,1,0:T(8,128)(2,1)S(1)} %get-tuple-element.60), channel_id=1, source_target_pairs={{0,48},{1,49},{2,50},{3,51},{4,52},{5,53},{6,54},{7,55},{8,56},{9,... | collective-permute-start | bytes 1966088 | tf_op jit(solution)/shard_map/sum_1_y/ppermute | solution.py:49
  27.6 15.1 %collective-permute-start.9 = (bf16[64,1536]{1,0:T(8,128)(2,1)S(1)}, bf16[64,1536]{1,0:T(8,128)(2,1)S(1)}, u32[]{:S(2)}, u32[]{:S(2)}) collective-permute-start(bf16[64,1536]{1,0:T(8,128)(2,1)S(1)} %get-tuple-element.66), channel_id=1, source_target_pairs={{0,24},{1,25},{2,26},{3,27},{4,28},{5,29},{6,30},{7,31},{8,16},{9,... | collective-permute-start | bytes 589832 | tf_op jit(solution)/shard_map/w_1/ppermute | solution.py:49
  28.3 14.4 %collective-permute-start.7 = (bf16[5,128,128]{2,1,0:T(8,128)(2,1)S(1)}, bf16[5,128,128]{2,1,0:T(8,128)(2,1)S(1)}, u32[]{:S(2)}, u32[]{:S(2)}) collective-permute-start(bf16[5,128,128]{2,1,0:T(8,128)(2,1)S(1)} %add_convert_fusion.10), channel_id=1, source_target_pairs={{0,16},{1,17},{2,18},{3,19},{4,20},{5,21},{6,22},{7,23},{8,24},{9,... | collective-permute-start | bytes 491528 | tf_op jit(solution)/shard_map/a_near/ppermute | solution.py:49
  42.8 8.4 %collective-permute-start.11 = (bf16[10,128,128]{2,1,0:T(8,128)(2,1)S(1)}, bf16[10,128,128]{2,1,0:T(8,128)(2,1)S(1)}, u32[]{:S(2)}, u32[]{:S(2)}) collective-permute-start(bf16[10,128,128]{2,1,0:T(8,128)(2,1)S(1)} %add_convert_fusion.6), channel_id=1, source_target_pairs={{0,16},{1,17},{2,18},{3,19},{4,20},{5,21},{6,22},{7,23},{8,24},{9,... | collective-permute-start | bytes 983048 | tf_op jit(solution)/shard_map/sum_2_near/ppermute | solution.py:49
  44.4 9.3 %collective-permute-start.10 = (bf16[10,128,128]{2,1,0:T(8,128)(2,1)S(1)}, bf16[10,128,128]{2,1,0:T(8,128)(2,1)S(1)}, u32[]{:S(2)}, u32[]{:S(2)}) collective-permute-start(bf16[10,128,128]{2,1,0:T(8,128)(2,1)S(1)} %add_convert_fusion.7), channel_id=1, source_target_pairs={{0,48},{1,49},{2,50},{3,51},{4,52},{5,53},{6,54},{7,55},{8,56},{9,... | collective-permute-start | bytes 983048 | tf_op jit(solution)/shard_map/sum_2_y/ppermute | solution.py:49
  46.4 4.5 %collective-permute-start.12 = (bf16[5,128,128]{2,1,0:T(8,128)(2,1)S(1)}, bf16[5,128,128]{2,1,0:T(8,128)(2,1)S(1)}, u32[]{:S(2)}, u32[]{:S(2)}) collective-permute-start(bf16[5,128,128]{2,1,0:T(8,128)(2,1)S(1)} %add_convert_fusion.9), channel_id=1, source_target_pairs={{0,4},{1,5},{2,6},{3,7},{4,0},{5,1},{6,2},{7,3},{8,12},{9,13},{10,... | collective-permute-start | bytes 491528 | tf_op jit(solution)/shard_map/a_pair/ppermute | solution.py:49
  53.9 9.4 %collective-permute-start.14 = (bf16[10,128,128]{2,1,0:T(8,128)(2,1)S(1)}, bf16[10,128,128]{2,1,0:T(8,128)(2,1)S(1)}, u32[]{:S(2)}, u32[]{:S(2)}) collective-permute-start(bf16[10,128,128]{2,1,0:T(8,128)(2,1)S(1)} %add_convert_fusion.3), channel_id=1, source_target_pairs={{0,64},{1,65},{2,66},{3,67},{4,68},{5,69},{6,70},{7,71},{8,72},{9,... | collective-permute-start | bytes 983048 | tf_op jit(solution)/shard_map/sum_3_x/ppermute | solution.py:49
  56.8 6.9 %collective-permute-start.13 = (bf16[10,128,128]{2,1,0:T(8,128)(2,1)S(1)}, bf16[10,128,128]{2,1,0:T(8,128)(2,1)S(1)}, u32[]{:S(2)}, u32[]{:S(2)}) collective-permute-start(bf16[10,128,128]{2,1,0:T(8,128)(2,1)S(1)} %add_convert_fusion.5), channel_id=1, source_target_pairs={{0,16},{1,17},{2,18},{3,19},{4,20},{5,21},{6,22},{7,23},{8,24},{9,... | collective-permute-start | bytes 983048 | tf_op jit(solution)/shard_map/sum_3_near/ppermute | solution.py:49
  56.9 16.6 %collective-permute-start.17 = (bf16[384,1536]{1,0:T(8,128)(2,1)S(1)}, bf16[384,1536]{1,0:T(8,128)(2,1)S(1)}, u32[]{:S(2)}, u32[]{:S(2)}) collective-permute-start(bf16[384,1536]{1,0:T(8,128)(2,1)S(1)} %get-tuple-element.93), channel_id=1, source_target_pairs={{0,8},{1,9},{2,10},{3,11},{4,12},{5,13},{6,14},{7,15},{8,0},{9,1},... | collective-permute-start | bytes 3538952 | tf_op jit(solution)/shard_map/w_core/ppermute | solution.py:49
  59.4 11.9 %collective-permute-start.20 = (bf16[10,128,128]{2,1,0:T(8,128)(2,1)S(1)}, bf16[10,128,128]{2,1,0:T(8,128)(2,1)S(1)}, u32[]{:S(2)}, u32[]{:S(2)}) collective-permute-start(bf16[10,128,128]{2,1,0:T(8,128)(2,1)S(1)} %pad_maximum_fusion.2.refs_0_), channel_id=1, source_target_pairs={{0,1},{1,2},{2,3},{3,0},{4,5},{5,6},{6,7},{7,4},{8,9},{9,10},{10,1... | collective-permute-start | bytes 983048 | tf_op jit(solution)/shard_map/a_up/ppermute | solution.py:49
  61.1 12.3 %collective-permute-start.19 = (bf16[10,128,128]{2,1,0:T(8,128)(2,1)S(1)}, bf16[10,128,128]{2,1,0:T(8,128)(2,1)S(1)}, u32[]{:S(2)}, u32[]{:S(2)}) collective-permute-start(bf16[10,128,128]{2,1,0:T(8,128)(2,1)S(1)} %pad_maximum_fusion.2.refs_0_), channel_id=1, source_target_pairs={{0,3},{1,0},{2,1},{3,2},{4,7},{5,4},{6,5},{7,6},{8,11},{9,8},{10,9... | collective-permute-start | bytes 983048 | tf_op jit(solution)/shard_map/a_down/ppermute | solution.py:49
  63.9 16.7 %collective-permute-start.16 = (bf16[10,128,128]{2,1,0:T(8,128)(2,1)S(1)}, bf16[10,128,128]{2,1,0:T(8,128)(2,1)S(1)}, u32[]{:S(2)}, u32[]{:S(2)}) collective-permute-start(bf16[10,128,128]{2,1,0:T(8,128)(2,1)S(1)} %add_convert_fusion.1), channel_id=1, source_target_pairs={{0,16},{1,17},{2,18},{3,19},{4,20},{5,21},{6,22},{7,23},{8,24},{9,... | collective-permute-start | bytes 983048 | tf_op jit(solution)/shard_map/back_4_near/ppermute | solution.py:49
  65.3 15.4 %collective-permute-start.15 = (bf16[10,128,128]{2,1,0:T(8,128)(2,1)S(1)}, bf16[10,128,128]{2,1,0:T(8,128)(2,1)S(1)}, u32[]{:S(2)}, u32[]{:S(2)}) collective-permute-start(bf16[10,128,128]{2,1,0:T(8,128)(2,1)S(1)} %add_convert_fusion.2), channel_id=1, source_target_pairs={{0,48},{1,49},{2,50},{3,51},{4,52},{5,53},{6,54},{7,55},{8,56},{9,... | collective-permute-start | bytes 983048 | tf_op jit(solution)/shard_map/back_4_y/ppermute | solution.py:49
  71.3 9.4 %collective-permute-start.18 = (bf16[64,1536]{1,0:T(8,128)(2,1)S(1)}, bf16[64,1536]{1,0:T(8,128)(2,1)S(1)}, u32[]{:S(2)}, u32[]{:S(2)}) collective-permute-start(bf16[64,1536]{1,0:T(8,128)(2,1)S(1)} %get-tuple-element.76), channel_id=1, source_target_pairs={{0,24},{1,25},{2,26},{3,27},{4,28},{5,29},{6,30},{7,31},{8,16},{9,... | collective-permute-start | bytes 589832 | tf_op jit(solution)/shard_map/w_2/ppermute | solution.py:49
  73.5 7.2 %collective-permute-start.21 = (bf16[5,128,128]{2,1,0:T(8,128)(2,1)S(1)}, bf16[5,128,128]{2,1,0:T(8,128)(2,1)S(1)}, u32[]{:S(2)}, u32[]{:S(2)}) collective-permute-start(bf16[5,128,128]{2,1,0:T(8,128)(2,1)S(1)} %slice.76), channel_id=1, source_target_pairs={{0,1},{1,2},{2,3},{3,0},{4,5},{5,6},{6,7},{7,4},{8,9},{9,10},{10,1... | collective-permute-start | bytes 491528 | tf_op jit(solution)/shard_map/a_up_2/ppermute | solution.py:49
  73.6 7.1 %collective-permute-start.22 = (bf16[5,128,128]{2,1,0:T(8,128)(2,1)S(1)}, bf16[5,128,128]{2,1,0:T(8,128)(2,1)S(1)}, u32[]{:S(2)}, u32[]{:S(2)}) collective-permute-start(bf16[5,128,128]{2,1,0:T(8,128)(2,1)S(1)} %slice.77), channel_id=1, source_target_pairs={{0,3},{1,0},{2,1},{3,2},{4,7},{5,4},{6,5},{7,6},{8,11},{9,8},{10,9... | collective-permute-start | bytes 491528 | tf_op jit(solution)/shard_map/a_down_2/ppermute | solution.py:49
  80.7 5.3 %collective-permute-start.25 = (bf16[10,128,128]{2,1,0:T(8,128)(2,1)S(1)}, bf16[10,128,128]{2,1,0:T(8,128)(2,1)S(1)}, u32[]{:S(2)}, u32[]{:S(2)}) collective-permute-start(bf16[10,128,128]{2,1,0:T(8,128)(2,1)S(1)} %pad_maximum_fusion.2.refs_0_), channel_id=1, source_target_pairs={{0,8},{1,9},{2,10},{3,11},{4,12},{5,13},{6,14},{7,15},{8,0},{9,1},... | collective-permute-start | bytes 983048 | tf_op jit(solution)/shard_map/a_core_back/ppermute | solution.py:49
  81.5 4.6 %collective-permute-start.26 = (bf16[10,128,128]{2,1,0:T(8,128)(2,1)S(1)}, bf16[10,128,128]{2,1,0:T(8,128)(2,1)S(1)}, u32[]{:S(2)}, u32[]{:S(2)}) collective-permute-start(bf16[10,128,128]{2,1,0:T(8,128)(2,1)S(1)} %collective-permute-done.19.refs_1_), channel_id=1, source_target_pairs={{0,8},{1,9},{2,10},{3,11},{4,12},{5,13},{6,14},{7,15},{8,0},{9,1},... | collective-permute-start | bytes 983048 | tf_op jit(solution)/shard_map/a_core_back/ppermute | solution.py:49
  81.5 4.5 %collective-permute-start.29 = (bf16[10,128,128]{2,1,0:T(8,128)(2,1)S(1)}, bf16[10,128,128]{2,1,0:T(8,128)(2,1)S(1)}, u32[]{:S(2)}, u32[]{:S(2)}) collective-permute-start(bf16[10,128,128]{2,1,0:T(8,128)(2,1)S(1)} %collective-permute-done.20.refs_4_), channel_id=1, source_target_pairs={{0,8},{1,9},{2,10},{3,11},{4,12},{5,13},{6,14},{7,15},{8,0},{9,1},... | collective-permute-start | bytes 983048 | tf_op jit(solution)/shard_map/a_core_back/ppermute | solution.py:49
  82.0 1.9 %collective-permute-start.27 = (bf16[5,128,128]{2,1,0:T(8,128)(2,1)S(1)}, bf16[5,128,128]{2,1,0:T(8,128)(2,1)S(1)}, u32[]{:S(2)}, u32[]{:S(2)}) collective-permute-start(bf16[5,128,128]{2,1,0:T(8,128)(2,1)S(1)} %collective-permute-done.21.refs_2_), channel_id=1, source_target_pairs={{0,8},{1,9},{2,10},{3,11},{4,12},{5,13},{6,14},{7,15},{8,0},{9,1},... | collective-permute-start | bytes 491528 | tf_op jit(solution)/shard_map/a_core_back/ppermute | solution.py:49
  82.1 3.7 %collective-permute-start.28 = (bf16[5,128,128]{2,1,0:T(8,128)(2,1)S(1)}, bf16[5,128,128]{2,1,0:T(8,128)(2,1)S(1)}, u32[]{:S(2)}, u32[]{:S(2)}) collective-permute-start(bf16[5,128,128]{2,1,0:T(8,128)(2,1)S(1)} %collective-permute-done.22.refs_3_), channel_id=1, source_target_pairs={{0,8},{1,9},{2,10},{3,11},{4,12},{5,13},{6,14},{7,15},{8,0},{9,1},... | collective-permute-start | bytes 491528 | tf_op jit(solution)/shard_map/a_core_back/ppermute | solution.py:49
  83.9 17.2 %collective-permute-start.24 = (bf16[20,128,128]{2,1,0:T(8,128)(2,1)S(1)}, bf16[20,128,128]{2,1,0:T(8,128)(2,1)S(1)}, u32[]{:S(2)}, u32[]{:S(2)}) collective-permute-start(bf16[20,128,128]{2,1,0:T(8,128)(2,1)S(1)} %pad_maximum_fusion.1.second_own), channel_id=1, source_target_pairs={{0,48},{1,49},{2,50},{3,51},{4,52},{5,53},{6,54},{7,55},{8,56},{9,... | collective-permute-start | bytes 1966088 | tf_op jit(solution)/shard_map/back_5_y/ppermute | solution.py:49
  85.8 17.1 %collective-permute-start.23 = (bf16[20,128,128]{2,1,0:T(8,128)(2,1)S(1)}, bf16[20,128,128]{2,1,0:T(8,128)(2,1)S(1)}, u32[]{:S(2)}, u32[]{:S(2)}) collective-permute-start(bf16[20,128,128]{2,1,0:T(8,128)(2,1)S(1)} %pad_maximum_fusion.first_own), channel_id=1, source_target_pairs={{0,64},{1,65},{2,66},{3,67},{4,68},{5,69},{6,70},{7,71},{8,72},{9,... | collective-permute-start | bytes 1966088 | tf_op jit(solution)/shard_map/back_5_x/ppermute | solution.py:49
  86.0 19.9 %collective-permute-start.30 = (bf16[256,1536]{1,0:T(8,128)(2,1)S(1)}, bf16[256,1536]{1,0:T(8,128)(2,1)S(1)}, u32[]{:S(2)}, u32[]{:S(2)}) collective-permute-start(bf16[256,1536]{1,0:T(8,128)(2,1)S(1)} %get-tuple-element.90), channel_id=1, source_target_pairs={{0,24},{1,25},{2,26},{3,27},{4,28},{5,29},{6,30},{7,31},{8,16},{9,... | collective-permute-start | bytes 2359304 | tf_op jit(solution)/shard_map/w_3/ppermute | solution.py:49
  118.9 3.2 %collective-permute-start.31 = (bf16[384,1536]{1,0:T(8,128)(2,1)S(1)}, bf16[384,1536]{1,0:T(8,128)(2,1)S(1)}, u32[]{:S(2)}, u32[]{:S(2)}) collective-permute-start(bf16[384,1536]{1,0:T(8,128)(2,1)S(1)} %get-tuple-element.92), channel_id=1, source_target_pairs={{0,8},{1,9},{2,10},{3,11},{4,12},{5,13},{6,14},{7,15},{8,0},{9,1},... | collective-permute-start | bytes 3538952 | tf_op jit(solution)/shard_map/out_core/ppermute | solution.py:49
  (4 other events, 16.2 us)

commit v5 on v3

--- a/solution.py
+++ b/solution.py
@@ -250,19 +250,20 @@
         out[:, cols] = dot(inverse[...], weights[:, cols])
 
 
-def right_kernel(
-    first_own, first_got, second_own, second_got, part_left, inverse, chunk, theirs, mine, full, left, second, third
-):
-    x_hi, y, core, _, _ = place()
+def spread_kernel(first_own, first_got, second_own, second_got, full):
+    x_hi, y, _, _, _ = place()
     code = x_hi * 4 + y
-    rows = mine.shape[0]
     owns, gots = (first_own, second_own), (first_got, second_got)
     for tile, (i, j) in enumerate(UPPER):
         part, piece, at = slot_of(tile, code, WIDTH)
         index = (piece & 3) * (WIDTH, PIECE - WIDTH)[part] + at
         put(full, i, j, jnp.where(piece >= 4, gots[part][index], owns[part][index]))
+
+
+def right_kernel(full, part_left, inverse, chunk, theirs, mine, left, second, third):
+    _, y, core, _, _ = place()
+    rows = mine.shape[0]
     ratio, scale = scales(diagonal_sum(full))
-
     last = pl.ds(last_start(y % 2, core), CHUNKS[-1][2])
     for cols in steps():
         left[:, cols] = (part_left[:, cols] + dot(inverse[:, last], chunk[:, cols])).astype(jnp.bfloat16)
@@ -418,14 +419,26 @@
         9 << 20,
         20,
     )
+    full = kernel(
+        spread_kernel,
+        "spread",
+        (first_own, first_got, second_own, second_got),
+        [pltpu.VMEM] * 4,
+        shaped(BLK, BLK),
+        pltpu.VMEM,
+        [],
+        0,
+        8 << 20,
+        8,
+    )
     theirs, mine = kernel(
         right_kernel,
         "right",
-        (first_own, first_got, second_own, second_got, left, inverse, w_3),
-        [pltpu.VMEM] * 7,
+        (full, left, inverse, w_3),
+        [pltpu.VMEM] * 4,
         [shaped(rows, BLK)] * 2,
         [pltpu.VMEM] * 2,
-        [matrix(BLK, BLK)] + [matrix(2 * rows, BLK)] * 3,
+        [matrix(2 * rows, BLK)] * 3,
         6 * 2 * rows * BLK * BLK,
         8 << 20,
         24,

time: 119 us -> 119 us (level)
    pallas_call x5 -> x6, Pallas kernels: 31.9 us -> 32.7 us  [kernel(): pl.pallas_call(body, out_shape=out_shape, in_specs=[whole(space) for spac...]
  transfers between devices with their start and end apart: 32 -> 32, of which waited for: 16 -> 16; matrix products, arithmetic and copies ran while one was open for 1% -> 1% of each run, Pallas kernels for 16% -> 17%
where the time goes in v5:
time: 119 us
  starting transfers between devices  45.7 us (38%)
  waiting for transfers between devices  34.3 us (29%)
  Pallas kernels  32.7 us (27%)
  local copies, waits for them, and re-layouts  4.91 us (4%)
    ppermute x32, starting transfers between devices, send(): return lax.ppermute(array, AXES, pairs)  45.7 us
    ppermute x32, waiting for transfers between devices, send(): return lax.ppermute(array, AXES, pairs)  34.3 us
    pallas_call x6, Pallas kernels, kernel(): pl.pallas_call(body, out_shape=out_shape, in_specs=[whole(space) for spac...  32.7 us
  transfers between devices with their start and end apart: 32, of which 16 were waited for; matrix products, arithmetic and copies ran while one was open for 1% of the time, Pallas kernels for 17%

profile of v5, /device:TPU:1, one launch (start us, length us, event | category | flops | bytes accessed | tf_op | source)
XLA Modules:
  0.0 119.0 jit_solution(14319600581880566629)
XLA Ops:
  1.4 1.9 %constant_dynamic-slice_fusion = (bf16[384,1536]{1,0:T(8,128)(2,1)S(1)}, bf16[384,1536]{1,0:T(8,128)(2,1)S(1)}) fusion(bf16[384,3072]{1,0:T(8,128)(2,1)} %w_own.1, s32[]{:T(128)S(6)} %select_n.17, s32[]{:T(128)S(6)} %select_n.18), kind=kLoop, calls=%fused_computation.16 | loop fusion | bytes 4718600 | tf_op jit(solution)/shard_map/dynamic_slice | solution.py:387
  3.3 1.5 %collective-permute-start.1 = (bf16[256,1536]{1,0:T(8,128)(2,1)S(1)}, bf16[256,1536]{1,0:T(8,128)(2,1)S(1)}, u32[]{:S(2)}, u32[]{:S(2)}) collective-permute-start(bf16[256,1536]{1,0:T(8,128)(2,1)S(1)} %constant_dynamic-slice_fusion.2), channel_id=1, source_target_pairs={{0,8},{1,9},{2,10},{3,11},{4,12},{5,13},{6,14},{7,15},{8,0},{9,1},... | collective-permute-start | bytes 2359304 | tf_op jit(solution)/shard_map/g_tokens/ppermute | solution.py:49
  4.8 2.1 %cov_a.1 = (bf16[20,128,128]{2,1,0:T(8,128)(2,1)S(1)}, bf16[20,128,128]{2,1,0:T(8,128)(2,1)S(1)}, bf16[64,1536]{1,0:T(8,128)(2,1)S(1)}, bf16[64,1536]{1,0:T(8,128)(2,1)S(1)}, bf16[256,1536]{1,0:T(8,128)(2,1)S(1)}) custom-call(bf16[256,6144]{1,0:T(8,128)(2,1)S(1)} %copy-done.1, bf16[384,3072]{1,0:T(8,128)(2,1)S(1)} %copy-done), custom_call_target="tpu_custom_call" | custom-call | flops 335544320 | bytes 5242880 | tf_op jit(solution)/shard_map/cov_a/pallas_call | solution.py:299
  7.5 1.4 %collective-permute-start.8 = (bf16[384,1536]{1,0:T(8,128)(2,1)S(1)}, bf16[384,1536]{1,0:T(8,128)(2,1)S(1)}, u32[]{:S(2)}, u32[]{:S(2)}) collective-permute-start(bf16[384,1536]{1,0:T(8,128)(2,1)S(1)} %get-tuple-element.61), channel_id=1, source_target_pairs={{0,16},{1,17},{2,18},{3,19},{4,20},{5,21},{6,22},{7,23},{8,24},{9,... | collective-permute-start | bytes 3538952 | tf_op jit(solution)/shard_map/w_0/ppermute | solution.py:49
  9.4 2.9 %collective-permute-start.2 = (bf16[5,128,128]{2,1,0:T(8,128)(2,1)S(1)}, bf16[5,128,128]{2,1,0:T(8,128)(2,1)S(1)}, u32[]{:S(2)}, u32[]{:S(2)}) collective-permute-start(bf16[5,128,128]{2,1,0:T(8,128)(2,1)S(1)} %get-tuple-element.89), channel_id=1, source_target_pairs={{0,48},{1,49},{2,50},{3,51},{4,52},{5,53},{6,54},{7,55},{8,56},{9,... | collective-permute-start | bytes 491528 | tf_op jit(solution)/shard_map/a_sum_y/ppermute | solution.py:49
  12.3 2.7 %collective-permute-start.3 = (bf16[5,128,128]{2,1,0:T(8,128)(2,1)S(1)}, bf16[5,128,128]{2,1,0:T(8,128)(2,1)S(1)}, u32[]{:S(2)}, u32[]{:S(2)}) collective-permute-start(bf16[5,128,128]{2,1,0:T(8,128)(2,1)S(1)} %get-tuple-element.88), channel_id=1, source_target_pairs={{0,64},{1,65},{2,66},{3,67},{4,68},{5,69},{6,70},{7,71},{8,72},{9,... | collective-permute-start | bytes 491528 | tf_op jit(solution)/shard_map/a_sum_x/ppermute | solution.py:49
  15.1 3.5 %cov_g.1 = (bf16[20,128,128]{2,1,0:T(8,128)(2,1)S(1)}, bf16[20,128,128]{2,1,0:T(8,128)(2,1)S(1)}, bf16[20,128,128]{2,1,0:T(8,128)(2,1)S(1)}, bf16[20,128,128]{2,1,0:T(8,128)(2,1)S(1)}) custom-call(bf16[256,3072]{1,0:T(8,128)(2,1)S(1)} %copy-done.2, bf16[256,1536]{1,0:T(8,128)(2,1)S(1)} %collective-permute-done.1.got), custom_call_target="tpu_custom_call" | custom-call | flops 1409286144 | bytes 4194304 | tf_op jit(solution)/shard_map/cov_g/pallas_call | solution.py:299
  18.9 4.5 %collective-permute-done.4 = bf16[5,128,128]{2,1,0:T(8,128)(2,1)S(1)} collective-permute-done((bf16[5,128,128]{2,1,0:T(8,128)(2,1)S(1)}, bf16[5,128,128]{2,1,0:T(8,128)(2,1)S(1)}, u32[]{:S(2)}, u32[]{:S(2)}) %collective-permute-start.4) | collective-permute-done | bytes 163872 | tf_op jit(solution)/shard_map/a_sum_both/ppermute | solution.py:49
  23.5 1.7 %collective-permute-start.5 = (bf16[20,128,128]{2,1,0:T(8,128)(2,1)S(1)}, bf16[20,128,128]{2,1,0:T(8,128)(2,1)S(1)}, u32[]{:S(2)}, u32[]{:S(2)}) collective-permute-start(bf16[20,128,128]{2,1,0:T(8,128)(2,1)S(1)} %get-tuple-element.55), channel_id=1, source_target_pairs={{0,64},{1,65},{2,66},{3,67},{4,68},{5,69},{6,70},{7,71},{8,72},{9,... | collective-permute-start | bytes 1966088 | tf_op jit(solution)/shard_map/sum_1_x/ppermute | solution.py:49
  25.2 2.4 %collective-permute-start.6 = (bf16[20,128,128]{2,1,0:T(8,128)(2,1)S(1)}, bf16[20,128,128]{2,1,0:T(8,128)(2,1)S(1)}, u32[]{:S(2)}, u32[]{:S(2)}) collective-permute-start(bf16[20,128,128]{2,1,0:T(8,128)(2,1)S(1)} %get-tuple-element.56), channel_id=1, source_target_pairs={{0,48},{1,49},{2,50},{3,51},{4,52},{5,53},{6,54},{7,55},{8,56},{9,... | collective-permute-start | bytes 1966088 | tf_op jit(solution)/shard_map/sum_1_y/ppermute | solution.py:49
  28.3 2.9 %collective-permute-start.7 = (bf16[5,128,128]{2,1,0:T(8,128)(2,1)S(1)}, bf16[5,128,128]{2,1,0:T(8,128)(2,1)S(1)}, u32[]{:S(2)}, u32[]{:S(2)}) collective-permute-start(bf16[5,128,128]{2,1,0:T(8,128)(2,1)S(1)} %add_convert_fusion.10), channel_id=1, source_target_pairs={{0,16},{1,17},{2,18},{3,19},{4,20},{5,21},{6,22},{7,23},{8,24},{9,... | collective-permute-start | bytes 491528 | tf_op jit(solution)/shard_map/a_near/ppermute | solution.py:49
  31.2 11.5 %collective-permute-done.7 = bf16[5,128,128]{2,1,0:T(8,128)(2,1)S(1)} collective-permute-done((bf16[5,128,128]{2,1,0:T(8,128)(2,1)S(1)}, bf16[5,128,128]{2,1,0:T(8,128)(2,1)S(1)}, u32[]{:S(2)}, u32[]{:S(2)}) %collective-permute-start.7) | collective-permute-done | bytes 163872 | tf_op jit(solution)/shard_map/a_near/ppermute | solution.py:49
  42.8 1.5 %collective-permute-start.11 = (bf16[10,128,128]{2,1,0:T(8,128)(2,1)S(1)}, bf16[10,128,128]{2,1,0:T(8,128)(2,1)S(1)}, u32[]{:S(2)}, u32[]{:S(2)}) collective-permute-start(bf16[10,128,128]{2,1,0:T(8,128)(2,1)S(1)} %add_convert_fusion.6), channel_id=1, source_target_pairs={{0,16},{1,17},{2,18},{3,19},{4,20},{5,21},{6,22},{7,23},{8,24},{9,... | collective-permute-start | bytes 983048 | tf_op jit(solution)/shard_map/sum_2_near/ppermute | solution.py:49
  44.4 2.0 %collective-permute-start.10 = (bf16[10,128,128]{2,1,0:T(8,128)(2,1)S(1)}, bf16[10,128,128]{2,1,0:T(8,128)(2,1)S(1)}, u32[]{:S(2)}, u32[]{:S(2)}) collective-permute-start(bf16[10,128,128]{2,1,0:T(8,128)(2,1)S(1)} %add_convert_fusion.7), channel_id=1, source_target_pairs={{0,48},{1,49},{2,50},{3,51},{4,52},{5,53},{6,54},{7,55},{8,56},{9,... | collective-permute-start | bytes 983048 | tf_op jit(solution)/shard_map/sum_2_y/ppermute | solution.py:49
  47.7 1.7 %collective-permute-start.17 = (bf16[384,1536]{1,0:T(8,128)(2,1)S(1)}, bf16[384,1536]{1,0:T(8,128)(2,1)S(1)}, u32[]{:S(2)}, u32[]{:S(2)}) collective-permute-start(bf16[384,1536]{1,0:T(8,128)(2,1)S(1)} %get-tuple-element.85), channel_id=1, source_target_pairs={{0,8},{1,9},{2,10},{3,11},{4,12},{5,13},{6,14},{7,15},{8,0},{9,1},... | collective-permute-start | bytes 3538952 | tf_op jit(solution)/shard_map/w_core/ppermute | solution.py:49
  49.4 1.5 %collective-permute-done.12 = bf16[5,128,128]{2,1,0:T(8,128)(2,1)S(1)} collective-permute-done((bf16[5,128,128]{2,1,0:T(8,128)(2,1)S(1)}, bf16[5,128,128]{2,1,0:T(8,128)(2,1)S(1)}, u32[]{:S(2)}, u32[]{:S(2)}) %collective-permute-start.12) | collective-permute-done | bytes 163872 | tf_op jit(solution)/shard_map/a_pair/ppermute | solution.py:49
  51.3 2.5 %collective-permute-done.10 = bf16[10,128,128]{2,1,0:T(8,128)(2,1)S(1)} collective-permute-done((bf16[10,128,128]{2,1,0:T(8,128)(2,1)S(1)}, bf16[10,128,128]{2,1,0:T(8,128)(2,1)S(1)}, u32[]{:S(2)}, u32[]{:S(2)}) %collective-permute-start.10) | collective-permute-done | bytes 327712 | tf_op jit(solution)/shard_map/sum_2_y/ppermute | solution.py:49
  53.9 2.8 %collective-permute-start.14 = (bf16[10,128,128]{2,1,0:T(8,128)(2,1)S(1)}, bf16[10,128,128]{2,1,0:T(8,128)(2,1)S(1)}, u32[]{:S(2)}, u32[]{:S(2)}) collective-permute-start(bf16[10,128,128]{2,1,0:T(8,128)(2,1)S(1)} %add_convert_fusion.3), channel_id=1, source_target_pairs={{0,64},{1,65},{2,66},{3,67},{4,68},{5,69},{6,70},{7,71},{8,72},{9,... | collective-permute-start | bytes 983048 | tf_op jit(solution)/shard_map/sum_3_x/ppermute | solution.py:49
  57.0 1.7 %collective-permute-start.22 = (bf16[10,128,128]{2,1,0:T(8,128)(2,1)S(1)}, bf16[10,128,128]{2,1,0:T(8,128)(2,1)S(1)}, u32[]{:S(2)}, u32[]{:S(2)}) collective-permute-start(bf16[10,128,128]{2,1,0:T(8,128)(2,1)S(1)} %pad_maximum_fusion.2.refs_0_), channel_id=1, source_target_pairs={{0,1},{1,2},{2,3},{3,0},{4,5},{5,6},{6,7},{7,4},{8,9},{9,10},{10,1... | collective-permute-start | bytes 983048 | tf_op jit(solution)/shard_map/a_up/ppermute | solution.py:49
  58.7 2.2 %collective-permute-start.21 = (bf16[10,128,128]{2,1,0:T(8,128)(2,1)S(1)}, bf16[10,128,128]{2,1,0:T(8,128)(2,1)S(1)}, u32[]{:S(2)}, u32[]{:S(2)}) collective-permute-start(bf16[10,128,128]{2,1,0:T(8,128)(2,1)S(1)} %pad_maximum_fusion.2.refs_0_), channel_id=1, source_target_pairs={{0,3},{1,0},{2,1},{3,2},{4,7},{5,4},{6,5},{7,6},{8,11},{9,8},{10,9... | collective-permute-start | bytes 983048 | tf_op jit(solution)/shard_map/a_down/ppermute | solution.py:49
  60.9 1.7 %collective-permute-done.14 = bf16[10,128,128]{2,1,0:T(8,128)(2,1)S(1)} collective-permute-done((bf16[10,128,128]{2,1,0:T(8,128)(2,1)S(1)}, bf16[10,128,128]{2,1,0:T(8,128)(2,1)S(1)}, u32[]{:S(2)}, u32[]{:S(2)}) %collective-permute-start.14) | collective-permute-done | bytes 327712 | tf_op jit(solution)/shard_map/sum_3_x/ppermute | solution.py:49
  64.4 1.9 %collective-permute-start.15 = (bf16[10,128,128]{2,1,0:T(8,128)(2,1)S(1)}, bf16[10,128,128]{2,1,0:T(8,128)(2,1)S(1)}, u32[]{:S(2)}, u32[]{:S(2)}) collective-permute-start(bf16[10,128,128]{2,1,0:T(8,128)(2,1)S(1)} %add_convert_fusion.2), channel_id=1, source_target_pairs={{0,48},{1,49},{2,50},{3,51},{4,52},{5,53},{6,54},{7,55},{8,56},{9,... | collective-permute-start | bytes 983048 | tf_op jit(solution)/shard_map/back_4_y/ppermute | solution.py:49
  66.5 4.3 %collective-permute-start.18 = (bf16[64,1536]{1,0:T(8,128)(2,1)S(1)}, bf16[64,1536]{1,0:T(8,128)(2,1)S(1)}, u32[]{:S(2)}, u32[]{:S(2)}) collective-permute-start(bf16[64,1536]{1,0:T(8,128)(2,1)S(1)} %get-tuple-element.72), channel_id=1, source_target_pairs={{0,24},{1,25},{2,26},{3,27},{4,28},{5,29},{6,30},{7,31},{8,16},{9,... | collective-permute-start | bytes 589832 | tf_op jit(solution)/shard_map/w_2/ppermute | solution.py:49
  70.8 1.6 %collective-permute-start.23 = (bf16[5,128,128]{2,1,0:T(8,128)(2,1)S(1)}, bf16[5,128,128]{2,1,0:T(8,128)(2,1)S(1)}, u32[]{:S(2)}, u32[]{:S(2)}) collective-permute-start(bf16[5,128,128]{2,1,0:T(8,128)(2,1)S(1)} %slice.76), channel_id=1, source_target_pairs={{0,1},{1,2},{2,3},{3,0},{4,5},{5,6},{6,7},{7,4},{8,9},{9,10},{10,1... | collective-permute-start | bytes 491528 | tf_op jit(solution)/shard_map/a_up_2/ppermute | solution.py:49
  72.4 2.2 %collective-permute-start.24 = (bf16[5,128,128]{2,1,0:T(8,128)(2,1)S(1)}, bf16[5,128,128]{2,1,0:T(8,128)(2,1)S(1)}, u32[]{:S(2)}, u32[]{:S(2)}) collective-permute-start(bf16[5,128,128]{2,1,0:T(8,128)(2,1)S(1)} %slice.77), channel_id=1, source_target_pairs={{0,3},{1,0},{2,1},{3,2},{4,7},{5,4},{6,5},{7,6},{8,11},{9,8},{10,9... | collective-permute-start | bytes 491528 | tf_op jit(solution)/shard_map/a_down_2/ppermute | solution.py:49
  74.6 3.8 %collective-permute-done.23.refs_2_ = bf16[5,128,128]{2,1,0:T(8,128)(2,1)S(1)} collective-permute-done((bf16[5,128,128]{2,1,0:T(8,128)(2,1)S(1)}, bf16[5,128,128]{2,1,0:T(8,128)(2,1)S(1)}, u32[]{:S(2)}, u32[]{:S(2)}) %collective-permute-start.23) | collective-permute-done | bytes 163872 | tf_op jit(solution)/shard_map/a_up_2/ppermute | solution.py:49
  82.1 1.4 %collective-permute-start.30 = (bf16[256,1536]{1,0:T(8,128)(2,1)S(1)}, bf16[256,1536]{1,0:T(8,128)(2,1)S(1)}, u32[]{:S(2)}, u32[]{:S(2)}) collective-permute-start(bf16[256,1536]{1,0:T(8,128)(2,1)S(1)} %get-tuple-element.82), channel_id=1, source_target_pairs={{0,24},{1,25},{2,26},{3,27},{4,28},{5,29},{6,30},{7,31},{8,16},{9,... | collective-permute-start | bytes 2359304 | tf_op jit(solution)/shard_map/w_3/ppermute | solution.py:49
  83.4 9.2 %inverse.1 = bf16[768,1536]{1,0:T(8,128)(2,1)S(1)} custom-call(bf16[10,128,128]{2,1,0:T(8,128)(2,1)S(1)} %pad_maximum_fusion.2.refs_0_, bf16[10,128,128]{2,1,0:T(8,128)(2,1)S(1)} %collective-permute-done.21.refs_1_, bf16[5,128,128]{2,1,0:T(8,128)(2,1)S(1)} %collective-permute-done.23.refs_2_, bf16[5,128,128]{2,1,0:T(8,128)(2,1)S(1)} %collective-permute-done.24.refs_3_, ...), custom_call_target="tpu_custom_call" | custom-call | flops 7247757312 | bytes 5242880 | tf_op jit(solution)/shard_map/inverse/pallas_call | solution.py:299
  92.7 4.2 %left.1.part_left = f32[768,1536]{1,0:T(8,128)S(1)} custom-call(bf16[768,1536]{1,0:T(8,128)(2,1)S(1)} %inverse.1, bf16[384,3072]{1,0:T(8,128)(2,1)S(1)} %copy-done, bf16[384,1536]{1,0:T(8,128)(2,1)S(1)} %collective-permute-done.17.w_core, bf16[384,1536]{1,0:T(8,128)(2,1)S(1)} %collective-permute-done.8.refs_0_, ...), custom_call_target="tpu_custom_call" | custom-call | flops 3623878656 | bytes 9437184 | tf_op jit(solution)/shard_map/left/pallas_call | solution.py:299
  99.2 2.8 %collective-permute-done.30.chunk = bf16[256,1536]{1,0:T(8,128)(2,1)S(1)} collective-permute-done((bf16[256,1536]{1,0:T(8,128)(2,1)S(1)}, bf16[256,1536]{1,0:T(8,128)(2,1)S(1)}, u32[]{:S(2)}, u32[]{:S(2)}) %collective-permute-start.30) | collective-permute-done | bytes 786464 | tf_op jit(solution)/shard_map/w_3/ppermute | solution.py:49
  102.0 12.7 %right.1 = (bf16[384,1536]{1,0:T(8,128)(2,1)S(1)}, bf16[384,1536]{1,0:T(8,128)(2,1)S(1)}) custom-call(bf16[1536,1536]{1,0:T(8,128)(2,1)S(1)} %spread.1.full, f32[768,1536]{1,0:T(8,128)S(1)} %left.1.part_left, bf16[768,1536]{1,0:T(8,128)(2,1)S(1)} %inverse.1, bf16[256,1536]{1,0:T(8,128)(2,1)S(1)} %collective-permute-done.30.chunk), custom_call_target="tpu_custom_call" | custom-call | flops 10871635968 | bytes 8388608 | tf_op jit(solution)/shard_map/right/pallas_call | solution.py:299
  115.8 2.0 %collective-permute-done.31 = bf16[384,1536]{1,0:T(8,128)(2,1)S(1)} collective-permute-done((bf16[384,1536]{1,0:T(8,128)(2,1)S(1)}, bf16[384,1536]{1,0:T(8,128)(2,1)S(1)}, u32[]{:S(2)}, u32[]{:S(2)}) %collective-permute-start.31) | collective-permute-done | bytes 1179680 | tf_op jit(solution)/shard_map/out_core/ppermute | solution.py:49
  (67 shorter events, 15.9 us)
Async XLA Ops:
  3.3 5.9 %collective-permute-start.1 = (bf16[256,1536]{1,0:T(8,128)(2,1)S(1)}, bf16[256,1536]{1,0:T(8,128)(2,1)S(1)}, u32[]{:S(2)}, u32[]{:S(2)}) collective-permute-start(bf16[256,1536]{1,0:T(8,128)(2,1)S(1)} %constant_dynamic-slice_fusion.2), channel_id=1, source_target_pairs={{0,8},{1,9},{2,10},{3,11},{4,12},{5,13},{6,14},{7,15},{8,0},{9,1},... | collective-permute-start | bytes 2359304 | tf_op jit(solution)/shard_map/g_tokens/ppermute | solution.py:49
  6.9 2.3 %collective-permute-start = (bf16[20,128,128]{2,1,0:T(8,128)(2,1)S(1)}, bf16[20,128,128]{2,1,0:T(8,128)(2,1)S(1)}, u32[]{:S(2)}, u32[]{:S(2)}) collective-permute-start(bf16[20,128,128]{2,1,0:T(8,128)(2,1)S(1)} %get-tuple-element.46), channel_id=1, source_target_pairs={{0,8},{1,9},{2,10},{3,11},{4,12},{5,13},{6,14},{7,15},{8,0},{9,1},... | collective-permute-start | bytes 1966088 | tf_op jit(solution)/shard_map/a_core/ppermute | solution.py:49
  7.5 35.3 %collective-permute-start.8 = (bf16[384,1536]{1,0:T(8,128)(2,1)S(1)}, bf16[384,1536]{1,0:T(8,128)(2,1)S(1)}, u32[]{:S(2)}, u32[]{:S(2)}) collective-permute-start(bf16[384,1536]{1,0:T(8,128)(2,1)S(1)} %get-tuple-element.61), channel_id=1, source_target_pairs={{0,16},{1,17},{2,18},{3,19},{4,20},{5,21},{6,22},{7,23},{8,24},{9,... | collective-permute-start | bytes 3538952 | tf_op jit(solution)/shard_map/w_0/ppermute | solution.py:49
  9.4 9.2 %collective-permute-start.2 = (bf16[5,128,128]{2,1,0:T(8,128)(2,1)S(1)}, bf16[5,128,128]{2,1,0:T(8,128)(2,1)S(1)}, u32[]{:S(2)}, u32[]{:S(2)}) collective-permute-start(bf16[5,128,128]{2,1,0:T(8,128)(2,1)S(1)} %get-tuple-element.89), channel_id=1, source_target_pairs={{0,48},{1,49},{2,50},{3,51},{4,52},{5,53},{6,54},{7,55},{8,56},{9,... | collective-permute-start | bytes 491528 | tf_op jit(solution)/shard_map/a_sum_y/ppermute | solution.py:49
  12.3 6.6 %collective-permute-start.3 = (bf16[5,128,128]{2,1,0:T(8,128)(2,1)S(1)}, bf16[5,128,128]{2,1,0:T(8,128)(2,1)S(1)}, u32[]{:S(2)}, u32[]{:S(2)}) collective-permute-start(bf16[5,128,128]{2,1,0:T(8,128)(2,1)S(1)} %get-tuple-element.88), channel_id=1, source_target_pairs={{0,64},{1,65},{2,66},{3,67},{4,68},{5,69},{6,70},{7,71},{8,72},{9,... | collective-permute-start | bytes 491528 | tf_op jit(solution)/shard_map/a_sum_x/ppermute | solution.py:49
  15.1 8.4 %collective-permute-start.4 = (bf16[5,128,128]{2,1,0:T(8,128)(2,1)S(1)}, bf16[5,128,128]{2,1,0:T(8,128)(2,1)S(1)}, u32[]{:S(2)}, u32[]{:S(2)}) collective-permute-start(bf16[5,128,128]{2,1,0:T(8,128)(2,1)S(1)} %get-tuple-element.87), channel_id=1, source_target_pairs={{0,112},{1,113},{2,114},{3,115},{4,116},{5,117},{6,118},{7,119},{8... | collective-permute-start | bytes 491528 | tf_op jit(solution)/shard_map/a_sum_both/ppermute | solution.py:49
  23.5 19.3 %collective-permute-start.5 = (bf16[20,128,128]{2,1,0:T(8,128)(2,1)S(1)}, bf16[20,128,128]{2,1,0:T(8,128)(2,1)S(1)}, u32[]{:S(2)}, u32[]{:S(2)}) collective-permute-start(bf16[20,128,128]{2,1,0:T(8,128)(2,1)S(1)} %get-tuple-element.55), channel_id=1, source_target_pairs={{0,64},{1,65},{2,66},{3,67},{4,68},{5,69},{6,70},{7,71},{8,72},{9,... | collective-permute-start | bytes 1966088 | tf_op jit(solution)/shard_map/sum_1_x/ppermute | solution.py:49
  25.2 17.6 %collective-permute-start.6 = (bf16[20,128,128]{2,1,0:T(8,128)(2,1)S(1)}, bf16[20,128,128]{2,1,0:T(8,128)(2,1)S(1)}, u32[]{:S(2)}, u32[]{:S(2)}) collective-permute-start(bf16[20,128,128]{2,1,0:T(8,128)(2,1)S(1)} %get-tuple-element.56), channel_id=1, source_target_pairs={{0,48},{1,49},{2,50},{3,51},{4,52},{5,53},{6,54},{7,55},{8,56},{9,... | collective-permute-start | bytes 1966088 | tf_op jit(solution)/shard_map/sum_1_y/ppermute | solution.py:49
  27.6 15.1 %collective-permute-start.9 = (bf16[64,1536]{1,0:T(8,128)(2,1)S(1)}, bf16[64,1536]{1,0:T(8,128)(2,1)S(1)}, u32[]{:S(2)}, u32[]{:S(2)}) collective-permute-start(bf16[64,1536]{1,0:T(8,128)(2,1)S(1)} %get-tuple-element.62), channel_id=1, source_target_pairs={{0,24},{1,25},{2,26},{3,27},{4,28},{5,29},{6,30},{7,31},{8,16},{9,... | collective-permute-start | bytes 589832 | tf_op jit(solution)/shard_map/w_1/ppermute | solution.py:49
  28.3 14.4 %collective-permute-start.7 = (bf16[5,128,128]{2,1,0:T(8,128)(2,1)S(1)}, bf16[5,128,128]{2,1,0:T(8,128)(2,1)S(1)}, u32[]{:S(2)}, u32[]{:S(2)}) collective-permute-start(bf16[5,128,128]{2,1,0:T(8,128)(2,1)S(1)} %add_convert_fusion.10), channel_id=1, source_target_pairs={{0,16},{1,17},{2,18},{3,19},{4,20},{5,21},{6,22},{7,23},{8,24},{9,... | collective-permute-start | bytes 491528 | tf_op jit(solution)/shard_map/a_near/ppermute | solution.py:49
  42.8 8.4 %collective-permute-start.11 = (bf16[10,128,128]{2,1,0:T(8,128)(2,1)S(1)}, bf16[10,128,128]{2,1,0:T(8,128)(2,1)S(1)}, u32[]{:S(2)}, u32[]{:S(2)}) collective-permute-start(bf16[10,128,128]{2,1,0:T(8,128)(2,1)S(1)} %add_convert_fusion.6), channel_id=1, source_target_pairs={{0,16},{1,17},{2,18},{3,19},{4,20},{5,21},{6,22},{7,23},{8,24},{9,... | collective-permute-start | bytes 983048 | tf_op jit(solution)/shard_map/sum_2_near/ppermute | solution.py:49
  44.4 9.3 %collective-permute-start.10 = (bf16[10,128,128]{2,1,0:T(8,128)(2,1)S(1)}, bf16[10,128,128]{2,1,0:T(8,128)(2,1)S(1)}, u32[]{:S(2)}, u32[]{:S(2)}) collective-permute-start(bf16[10,128,128]{2,1,0:T(8,128)(2,1)S(1)} %add_convert_fusion.7), channel_id=1, source_target_pairs={{0,48},{1,49},{2,50},{3,51},{4,52},{5,53},{6,54},{7,55},{8,56},{9,... | collective-permute-start | bytes 983048 | tf_op jit(solution)/shard_map/sum_2_y/ppermute | solution.py:49
  46.4 4.5 %collective-permute-start.12 = (bf16[5,128,128]{2,1,0:T(8,128)(2,1)S(1)}, bf16[5,128,128]{2,1,0:T(8,128)(2,1)S(1)}, u32[]{:S(2)}, u32[]{:S(2)}) collective-permute-start(bf16[5,128,128]{2,1,0:T(8,128)(2,1)S(1)} %add_convert_fusion.9), channel_id=1, source_target_pairs={{0,4},{1,5},{2,6},{3,7},{4,0},{5,1},{6,2},{7,3},{8,12},{9,13},{10,... | collective-permute-start | bytes 491528 | tf_op jit(solution)/shard_map/a_pair/ppermute | solution.py:49
  47.7 24.7 %collective-permute-start.17 = (bf16[384,1536]{1,0:T(8,128)(2,1)S(1)}, bf16[384,1536]{1,0:T(8,128)(2,1)S(1)}, u32[]{:S(2)}, u32[]{:S(2)}) collective-permute-start(bf16[384,1536]{1,0:T(8,128)(2,1)S(1)} %get-tuple-element.85), channel_id=1, source_target_pairs={{0,8},{1,9},{2,10},{3,11},{4,12},{5,13},{6,14},{7,15},{8,0},{9,1},... | collective-permute-start | bytes 3538952 | tf_op jit(solution)/shard_map/w_core/ppermute | solution.py:49
  53.9 8.7 %collective-permute-start.14 = (bf16[10,128,128]{2,1,0:T(8,128)(2,1)S(1)}, bf16[10,128,128]{2,1,0:T(8,128)(2,1)S(1)}, u32[]{:S(2)}, u32[]{:S(2)}) collective-permute-start(bf16[10,128,128]{2,1,0:T(8,128)(2,1)S(1)} %add_convert_fusion.3), channel_id=1, source_target_pairs={{0,64},{1,65},{2,66},{3,67},{4,68},{5,69},{6,70},{7,71},{8,72},{9,... | collective-permute-start | bytes 983048 | tf_op jit(solution)/shard_map/sum_3_x/ppermute | solution.py:49
  56.8 6.9 %collective-permute-start.13 = (bf16[10,128,128]{2,1,0:T(8,128)(2,1)S(1)}, bf16[10,128,128]{2,1,0:T(8,128)(2,1)S(1)}, u32[]{:S(2)}, u32[]{:S(2)}) collective-permute-start(bf16[10,128,128]{2,1,0:T(8,128)(2,1)S(1)} %add_convert_fusion.5), channel_id=1, source_target_pairs={{0,16},{1,17},{2,18},{3,19},{4,20},{5,21},{6,22},{7,23},{8,24},{9,... | collective-permute-start | bytes 983048 | tf_op jit(solution)/shard_map/sum_3_near/ppermute | solution.py:49
  57.0 9.5 %collective-permute-start.22 = (bf16[10,128,128]{2,1,0:T(8,128)(2,1)S(1)}, bf16[10,128,128]{2,1,0:T(8,128)(2,1)S(1)}, u32[]{:S(2)}, u32[]{:S(2)}) collective-permute-start(bf16[10,128,128]{2,1,0:T(8,128)(2,1)S(1)} %pad_maximum_fusion.2.refs_0_), channel_id=1, source_target_pairs={{0,1},{1,2},{2,3},{3,0},{4,5},{5,6},{6,7},{7,4},{8,9},{9,10},{10,1... | collective-permute-start | bytes 983048 | tf_op jit(solution)/shard_map/a_up/ppermute | solution.py:49
  58.7 12.1 %collective-permute-start.21 = (bf16[10,128,128]{2,1,0:T(8,128)(2,1)S(1)}, bf16[10,128,128]{2,1,0:T(8,128)(2,1)S(1)}, u32[]{:S(2)}, u32[]{:S(2)}) collective-permute-start(bf16[10,128,128]{2,1,0:T(8,128)(2,1)S(1)} %pad_maximum_fusion.2.refs_0_), channel_id=1, source_target_pairs={{0,3},{1,0},{2,1},{3,2},{4,7},{5,4},{6,5},{7,6},{8,11},{9,8},{10,9... | collective-permute-start | bytes 983048 | tf_op jit(solution)/shard_map/a_down/ppermute | solution.py:49
  63.9 15.2 %collective-permute-start.16 = (bf16[10,128,128]{2,1,0:T(8,128)(2,1)S(1)}, bf16[10,128,128]{2,1,0:T(8,128)(2,1)S(1)}, u32[]{:S(2)}, u32[]{:S(2)}) collective-permute-start(bf16[10,128,128]{2,1,0:T(8,128)(2,1)S(1)} %add_convert_fusion.1), channel_id=1, source_target_pairs={{0,16},{1,17},{2,18},{3,19},{4,20},{5,21},{6,22},{7,23},{8,24},{9,... | collective-permute-start | bytes 983048 | tf_op jit(solution)/shard_map/back_4_near/ppermute | solution.py:49
  64.4 15.1 %collective-permute-start.15 = (bf16[10,128,128]{2,1,0:T(8,128)(2,1)S(1)}, bf16[10,128,128]{2,1,0:T(8,128)(2,1)S(1)}, u32[]{:S(2)}, u32[]{:S(2)}) collective-permute-start(bf16[10,128,128]{2,1,0:T(8,128)(2,1)S(1)} %add_convert_fusion.2), channel_id=1, source_target_pairs={{0,48},{1,49},{2,50},{3,51},{4,52},{5,53},{6,54},{7,55},{8,56},{9,... | collective-permute-start | bytes 983048 | tf_op jit(solution)/shard_map/back_4_y/ppermute | solution.py:49
  66.5 12.5 %collective-permute-start.18 = (bf16[64,1536]{1,0:T(8,128)(2,1)S(1)}, bf16[64,1536]{1,0:T(8,128)(2,1)S(1)}, u32[]{:S(2)}, u32[]{:S(2)}) collective-permute-start(bf16[64,1536]{1,0:T(8,128)(2,1)S(1)} %get-tuple-element.72), channel_id=1, source_target_pairs={{0,24},{1,25},{2,26},{3,27},{4,28},{5,29},{6,30},{7,31},{8,16},{9,... | collective-permute-start | bytes 589832 | tf_op jit(solution)/shard_map/w_2/ppermute | solution.py:49
  70.8 7.6 %collective-permute-start.23 = (bf16[5,128,128]{2,1,0:T(8,128)(2,1)S(1)}, bf16[5,128,128]{2,1,0:T(8,128)(2,1)S(1)}, u32[]{:S(2)}, u32[]{:S(2)}) collective-permute-start(bf16[5,128,128]{2,1,0:T(8,128)(2,1)S(1)} %slice.76), channel_id=1, source_target_pairs={{0,1},{1,2},{2,3},{3,0},{4,5},{5,6},{6,7},{7,4},{8,9},{9,10},{10,1... | collective-permute-start | bytes 491528 | tf_op jit(solution)/shard_map/a_up_2/ppermute | solution.py:49
  72.4 6.2 %collective-permute-start.24 = (bf16[5,128,128]{2,1,0:T(8,128)(2,1)S(1)}, bf16[5,128,128]{2,1,0:T(8,128)(2,1)S(1)}, u32[]{:S(2)}, u32[]{:S(2)}) collective-permute-start(bf16[5,128,128]{2,1,0:T(8,128)(2,1)S(1)} %slice.77), channel_id=1, source_target_pairs={{0,3},{1,0},{2,1},{3,2},{4,7},{5,4},{6,5},{7,6},{8,11},{9,8},{10,9... | collective-permute-start | bytes 491528 | tf_op jit(solution)/shard_map/a_down_2/ppermute | solution.py:49
  78.4 1.6 %collective-permute-start.25 = (bf16[10,128,128]{2,1,0:T(8,128)(2,1)S(1)}, bf16[10,128,128]{2,1,0:T(8,128)(2,1)S(1)}, u32[]{:S(2)}, u32[]{:S(2)}) collective-permute-start(bf16[10,128,128]{2,1,0:T(8,128)(2,1)S(1)} %pad_maximum_fusion.2.refs_0_), channel_id=1, source_target_pairs={{0,8},{1,9},{2,10},{3,11},{4,12},{5,13},{6,14},{7,15},{8,0},{9,1},... | collective-permute-start | bytes 983048 | tf_op jit(solution)/shard_map/a_core_back/ppermute | solution.py:49
  78.6 2.2 %collective-permute-start.26 = (bf16[10,128,128]{2,1,0:T(8,128)(2,1)S(1)}, bf16[10,128,128]{2,1,0:T(8,128)(2,1)S(1)}, u32[]{:S(2)}, u32[]{:S(2)}) collective-permute-start(bf16[10,128,128]{2,1,0:T(8,128)(2,1)S(1)} %collective-permute-done.21.refs_1_), channel_id=1, source_target_pairs={{0,8},{1,9},{2,10},{3,11},{4,12},{5,13},{6,14},{7,15},{8,0},{9,1},... | collective-permute-start | bytes 983048 | tf_op jit(solution)/shard_map/a_core_back/ppermute | solution.py:49
  79.0 3.1 %collective-permute-start.29 = (bf16[10,128,128]{2,1,0:T(8,128)(2,1)S(1)}, bf16[10,128,128]{2,1,0:T(8,128)(2,1)S(1)}, u32[]{:S(2)}, u32[]{:S(2)}) collective-permute-start(bf16[10,128,128]{2,1,0:T(8,128)(2,1)S(1)} %collective-permute-done.22.refs_4_), channel_id=1, source_target_pairs={{0,8},{1,9},{2,10},{3,11},{4,12},{5,13},{6,14},{7,15},{8,0},{9,1},... | collective-permute-start | bytes 983048 | tf_op jit(solution)/shard_map/a_core_back/ppermute | solution.py:49
  79.2 4.3 %collective-permute-start.27 = (bf16[5,128,128]{2,1,0:T(8,128)(2,1)S(1)}, bf16[5,128,128]{2,1,0:T(8,128)(2,1)S(1)}, u32[]{:S(2)}, u32[]{:S(2)}) collective-permute-start(bf16[5,128,128]{2,1,0:T(8,128)(2,1)S(1)} %collective-permute-done.23.refs_2_), channel_id=1, source_target_pairs={{0,8},{1,9},{2,10},{3,11},{4,12},{5,13},{6,14},{7,15},{8,0},{9,1},... | collective-permute-start | bytes 491528 | tf_op jit(solution)/shard_map/a_core_back/ppermute | solution.py:49
  79.5 4.0 %collective-permute-start.28 = (bf16[5,128,128]{2,1,0:T(8,128)(2,1)S(1)}, bf16[5,128,128]{2,1,0:T(8,128)(2,1)S(1)}, u32[]{:S(2)}, u32[]{:S(2)}) collective-permute-start(bf16[5,128,128]{2,1,0:T(8,128)(2,1)S(1)} %collective-permute-done.24.refs_3_), channel_id=1, source_target_pairs={{0,8},{1,9},{2,10},{3,11},{4,12},{5,13},{6,14},{7,15},{8,0},{9,1},... | collective-permute-start | bytes 491528 | tf_op jit(solution)/shard_map/a_core_back/ppermute | solution.py:49
  80.1 17.4 %collective-permute-start.20 = (bf16[20,128,128]{2,1,0:T(8,128)(2,1)S(1)}, bf16[20,128,128]{2,1,0:T(8,128)(2,1)S(1)}, u32[]{:S(2)}, u32[]{:S(2)}) collective-permute-start(bf16[20,128,128]{2,1,0:T(8,128)(2,1)S(1)} %pad_maximum_fusion.1.second_own), channel_id=1, source_target_pairs={{0,48},{1,49},{2,50},{3,51},{4,52},{5,53},{6,54},{7,55},{8,56},{9,... | collective-permute-start | bytes 1966088 | tf_op jit(solution)/shard_map/back_5_y/ppermute | solution.py:49
  80.8 17.3 %collective-permute-start.19 = (bf16[20,128,128]{2,1,0:T(8,128)(2,1)S(1)}, bf16[20,128,128]{2,1,0:T(8,128)(2,1)S(1)}, u32[]{:S(2)}, u32[]{:S(2)}) collective-permute-start(bf16[20,128,128]{2,1,0:T(8,128)(2,1)S(1)} %pad_maximum_fusion.first_own), channel_id=1, source_target_pairs={{0,64},{1,65},{2,66},{3,67},{4,68},{5,69},{6,70},{7,71},{8,72},{9,... | collective-permute-start | bytes 1966088 | tf_op jit(solution)/shard_map/back_5_x/ppermute | solution.py:49
  82.1 19.9 %collective-permute-start.30 = (bf16[256,1536]{1,0:T(8,128)(2,1)S(1)}, bf16[256,1536]{1,0:T(8,128)(2,1)S(1)}, u32[]{:S(2)}, u32[]{:S(2)}) collective-permute-start(bf16[256,1536]{1,0:T(8,128)(2,1)S(1)} %get-tuple-element.82), channel_id=1, source_target_pairs={{0,24},{1,25},{2,26},{3,27},{4,28},{5,29},{6,30},{7,31},{8,16},{9,... | collective-permute-start | bytes 2359304 | tf_op jit(solution)/shard_map/w_3/ppermute | solution.py:49
  114.7 3.2 %collective-permute-start.31 = (bf16[384,1536]{1,0:T(8,128)(2,1)S(1)}, bf16[384,1536]{1,0:T(8,128)(2,1)S(1)}, u32[]{:S(2)}, u32[]{:S(2)}) collective-permute-start(bf16[384,1536]{1,0:T(8,128)(2,1)S(1)} %get-tuple-element.84), channel_id=1, source_target_pairs={{0,8},{1,9},{2,10},{3,11},{4,12},{5,13},{6,14},{7,15},{8,0},{9,1},... | collective-permute-start | bytes 3538952 | tf_op jit(solution)/shard_map/out_core/ppermute | solution.py:49
  (4 other events, 16.2 us)
